TPU v7x, 32 devices: a whole 2x2x4 slice. The times are simulated.
32 devices in a mesh: date: 8 (over z, core), book: 4 (over y, x).
Axes of the slice: x: 2, y: 2, z: 4, core: 2. Of those that a mesh axis runs over, the one named last changes fastest.
Arguments:
- shocks: bfloat16 [16, 512, 2048], P('date', None, 'book'), may hold values from -6 to 6
- persistence: float32 [2048], P('book'), may hold values from 0.5 to 1
- volatility: float32 [2048], P('book'), may hold values from 0.05 to 0.4
- base_rate: float32 [2048], P('book'), may hold values from 0 to 1
- cashflows: bfloat16 [16384, 512], P('book'), may hold values from -0.125 to 0.125
- block_owner: int32 [64, 1], P('book'), may hold values from 0 to 3; in each aligned block of 16 rows (0 to 15, 16 to 31, ...) at most 8 rows name the same one
- trade_set: int32 [16384], P('book'), may hold values from 0 to 511
- threshold: float32 [512], P('book'), may hold values from 0.1 to 1
- margin_lag: int32 [512], P('book'), may hold values from 1 to 2
Outputs:
- net_value: float32 [16, 512, 512], P('date', None, 'book')
- expected_exposure: float32 [16, 512], P('date', 'book')
Inputs may be any that keep to these rules, and one draw needn't show every extreme that they name: `block_owner`: among the blocks of one index of book, no value is named by more than 8 blocks.
All inputs are finite; a program needn't handle non-finite values.
Results may differ from a plain program's by a relative error of at most 0.0039.
Values may be sent and summed in bfloat16 or wider, within the bound.
No kernel may reach another device: no remote copies, remote signals or barrier semaphores. Data moves between devices by JAX's collectives and lax.ppermute only.
A program may use at most 128 MiB of HBM per device.

v0:
```python
import jax
import jax.numpy as jnp
from jax import lax
from jax.sharding import PartitionSpec as P

SETS = 512


def prefix(array, axis, combine, identity):
    devices, here = (lax.axis_size(axis), lax.axis_index(axis))
    everything = jax.tree.map(lambda part: lax.all_gather(part, axis), array)
    start = jax.tree.map(
        lambda part, zero: jnp.broadcast_to(jnp.asarray(zero, part.dtype), part.shape),
        array,
        identity,
    )

    def hop(k, before):
        reached = k < here
        new = combine(before, jax.tree.map(lambda part: part[k], everything))
        return jax.tree.map(lambda a, b: jnp.where(reached, a, b), new, before)

    return lax.fori_loop(0, devices, hop, start)


def shifted(block, axis, distance):
    devices = range(lax.axis_size(axis))
    route = [(i - distance, i) for i in devices if i - distance in devices]
    return lax.ppermute(block, axis, route)


def combine(earlier, later):
    return (earlier[0] * later[0], later[0] * earlier[1] + later[1])


def on_device(
    shocks,
    persistence,
    volatility,
    base_rate,
    cashflows,
    block_owner,
    trade_set,
    threshold,
    margin_lag,
):
    dates_here = shocks.shape[0]
    paths = shocks.shape[1]
    width = shocks.shape[2]
    blocks = block_owner.shape[0]
    block_rows = cashflows.shape[0] // blocks
    rows = dates_here * paths
    books = lax.axis_size("book")
    driven = volatility * shocks.astype(jnp.float32)
    carried = jnp.zeros((paths, width), jnp.float32)
    for step in range(dates_here):
        carried = persistence * carried + driven[step]
    factor = persistence**dates_here
    identity = (jnp.ones_like(persistence), jnp.zeros((paths, width), jnp.float32))
    _, state = prefix((factor, carried), "date", combine, identity)
    levels = []
    for step in range(dates_here):
        state = persistence * state + driven[step]
        levels.append(state)
    level = jnp.stack(levels, 0)
    discount = jnp.exp(-(base_rate + level)).astype(jnp.bfloat16).reshape(rows, width)
    owners = block_owner[:, 0]
    labels = jnp.arange(SETS, dtype=jnp.int32)
    most = max(2, 2 * blocks // books)
    order = jnp.arange(blocks, dtype=jnp.int32)
    before = (owners[:, None] == owners[None, :]) & (order[:, None] > order[None, :])
    rank = jnp.sum(before.astype(jnp.int32), axis=1)
    slot = owners * most + rank
    place = slot[:, None] == jnp.arange(books * most, dtype=jnp.int32)[None, :]
    packed = jnp.einsum(
        "bs,bx->sx",
        place.astype(jnp.bfloat16),
        cashflows.reshape(blocks, block_rows * width),
        preferred_element_type=jnp.float32,
    )
    packed = packed.astype(jnp.bfloat16).reshape(books, most, block_rows, width)
    set_rows = trade_set.reshape(blocks, block_rows) + 1
    slot_sets = jnp.sum(jnp.where(place[:, :, None], set_rows[:, None, :], 0), axis=0) - 1
    slot_sets = slot_sets.reshape(books, most, block_rows)
    arrived, arrived_sets = (
        lax.all_to_all(packed, "book", split_axis=0, concat_axis=0, tiled=True),
        lax.all_to_all(slot_sets, "book", split_axis=0, concat_axis=0, tiled=True),
    )
    price = jnp.einsum(
        "rk,tk->rt", discount, arrived.reshape(-1, width), preferred_element_type=jnp.float32
    )
    price = price.astype(jnp.bfloat16)
    onehot = (arrived_sets.reshape(-1)[:, None] == labels[None, :]).astype(jnp.bfloat16)
    partial_sets = jnp.dot(price, onehot, preferred_element_type=jnp.float32).reshape(
        dates_here, paths, SETS
    )
    net_value = lax.psum_scatter(partial_sets, "book", scatter_dimension=2, tiled=True)
    earlier = shifted(net_value, "date", 1)
    joined = jnp.concatenate([earlier, net_value], 0)
    collateral = jnp.zeros_like(net_value)
    for lag in range(1, dates_here + 1):
        collateral = jnp.where(
            margin_lag[None, None, :] == lag,
            joined[dates_here - lag : 2 * dates_here - lag],
            collateral,
        )
    exposure = jnp.maximum(net_value - collateral - threshold[None, None, :], 0.0)
    return (net_value, jnp.mean(exposure, axis=1))


def solution(mesh):
    return jax.shard_map(
        on_device,
        mesh=mesh,
        in_specs=(
            P("date", None, "book"),
            P("book"),
            P("book"),
            P("book"),
            P("book", None),
            P("book", None),
            P("book"),
            P("book"),
            P("book"),
        ),
        out_specs=(P("date", None, "book"), P("date", "book")),
        check_vma=False,
    )
```

profile of v0, /device:TPU:1, one launch (start us, length us, event | category | flops | bytes accessed | tf_op | source)
XLA Modules:
  0.0 223.9 jit_solution(10932426382861168364)
XLA Ops:
  7.9 1.5 convert_multiply_fusion
  9.4 2.0 multiply_add_fusion
  12.5 4.3 %all-to-all-start.1 = ((s32[4,8,256]{2,1,0:T(8,128)}), s32[4,8,256]{2,1,0:T(8,128)S(1)}, u32[]{:S(2)}, u32[]{:S(2)}) async-start(s32[4,8,256]{2,1,0:T(8,128)} %add_bitcast_fusion), calls=%async_computation.1 | async-start | bytes 65536 | tf_op jit(solution)/shard_map/all_to_all | solution.py:87
  16.8 4.8 %reshape.97 = bf16[16,131072]{1,0:T(8,128)(2,1)} reshape(bf16[4096,512]{1,0:T(8,128)(2,1)} %param.15) | data formatting | bytes 8388608 | tf_op jit(solution)/shard_map/reshape | solution.py:78
  21.6 8.4 %convolution_convert_fusion = bf16[32,131072]{1,0:T(8,128)(2,1)} fusion(bf16[16,131072]{1,0:T(8,128)(2,1)} %reshape.97, s32[16]{0:T(128)S(1)} %fusion.16), kind=kOutput, calls=%fused_computation.3 | convolution fusion | flops 138412544 | bytes 12582976 | tf_op jit(solution)/shard_map/bs,bx->sx/dot_general | solution.py:75
  30.0 9.9 %copy.13 = bf16[4,8,256,512]{3,2,1,0:T(8,128)(2,1)} copy(bf16[4,8,256,512]{3,1,2,0:T(8,128)(2,1)} %bitcast.46) | data formatting | bytes 16777216 | tf_op jit(solution)/shard_map/reshape | solution.py:81
  39.9 5.6 %all-to-all-start = ((bf16[4,8,256,512]{3,2,1,0:T(8,128)(2,1)}), bf16[4,8,256,512]{3,2,1,0:T(8,128)(2,1)}, u32[]{:S(2)}, u32[]{:S(2)}) async-start(bf16[4,8,256,512]{3,2,1,0:T(8,128)(2,1)} %copy.13), calls=%async_computation | async-start | bytes 16777216 | tf_op jit(solution)/shard_map/all_to_all | solution.py:86
  45.6 14.2 %all-gather.1 = f32[8,1,512]{2,1,0:T(1,128)S(1)} all-gather(f32[1,1,512]{2,1,0:T(1,128)S(1)} %bitcast.53), channel_id=2, replica_groups=mesh['date'=8,'book'=4] {'date'}, dimensions={0}, use_global_device_ids=true | all-gather | bytes 18432 | tf_op jit(solution)/shard_map/all_gather | solution.py:11
  59.8 36.4 %all-gather.4.cloned.1.call-done = f32[8,512,512]{2,1,0:T(8,128)} async-done(((f32[1,512,512]{2,1,0:T(8,128)}), f32[8,512,512]{2,1,0:T(8,128)}) %all-gather.4.cloned.1.call-update) | async-done | bytes 8388624 | tf_op jit(solution)/shard_map/all_gather | solution.py:11
  96.3 17.4 %while.14 = (s32[]{:T(128)}, f32[512,512]{1,0:T(8,128)S(1)}, s32[]{:T(128)}, f32[8,512]{1,0:T(8,128)S(1)}, f32[8,512,512]{2,1,0:T(8,128)}, /*index=5*/s32[]{:T(128)}, s32[]{:T(128)}) while((s32[]{:T(128)}, f32[512,512]{1,0:T(8,128)S(1)}, s32[]{:T(128)}, f32[8,512]{1,0:T(8,128)S(1)}, f32[8,512,512]{2,1,0:T(8,128)}, ...), condition=%wide.region_1.2_spmd.clone, body=%wide.region_0.1_spmd.clone.sunk | while | flops 1048580 | bytes 3151977 | solution.py:23
  96.3 2.1 fusion.23
  98.5 2.1 fusion.23
  100.6 2.1 fusion.23
  102.8 2.1 fusion.23
  105.0 2.1 fusion.23
  107.2 2.1 fusion.23
  109.3 2.1 fusion.23
  111.5 2.1 fusion.23
  114.7 22.7 %all-to-all-done = bf16[4,8,256,512]{3,2,1,0:T(8,128)(2,1)} async-done(((bf16[4,8,256,512]{3,2,1,0:T(8,128)(2,1)}), bf16[4,8,256,512]{3,2,1,0:T(8,128)(2,1)}, u32[]{:S(2)}, u32[]{:S(2)}) %all-to-all-start) | async-done | bytes 8388640 | tf_op jit(solution)/shard_map/all_to_all | solution.py:86
  137.3 15.1 %fusion.17 = bf16[1024,8192]{1,0:T(8,128)(2,1)} fusion(bf16[1024,512]{1,0:T(8,128)(2,1)S(1)} %bitcast.48, bf16[8192,512]{1,0:T(8,128)(2,1)} %bitcast.10), kind=kOutput, calls=%fused_computation.39 | convolution fusion | flops 8589934592 | bytes 26214400 | tf_op jit(solution)/shard_map/rk,tk->rt/dot_general | solution.py:89
  152.5 16.1 %fusion.1 = f32[1024,512]{1,0:T(8,128)} fusion(bf16[1024,8192]{1,0:T(8,128)(2,1)} %fusion.17, s32[8192]{0:T(1024)S(1)} %bitcast.52), kind=kOutput, calls=%fused_computation.5 | convolution fusion | flops 8594128896 | bytes 18907136 | tf_op jit(solution)/shard_map/dot_general | solution.py:94
  168.6 36.6 %reduce-scatter.2.cloned.1.call-done = f32[2,512,128]{2,1,0:T(8,128)} async-done(((f32[2,512,512]{2,1,0:T(8,128)}), f32[2,512,128]{2,1,0:T(8,128)}) %reduce-scatter.2.cloned.1.call-update) | async-done | bytes 524304 | tf_op jit(solution)/shard_map/reduce_scatter | solution.py:97
  205.2 3.7 %collective-permute-start = (f32[2,512,128]{2,1,0:T(8,128)}, f32[2,512,128]{2,1,0:T(8,128)S(1)}, u32[]{:S(2)}, u32[]{:S(2)}) collective-permute-start(f32[2,512,128]{2,1,0:T(8,128)} %reduce-scatter.2.cloned.1.call-done), channel_id=1, source_target_pairs={{0,4},{4,8},{8,12},{12,16},{16,20},{20,24},{24,28},{1,5},{5,9},{9,... | collective-permute-start | bytes 1572872 | tf_op jit(solution)/shard_map/ppermute | solution.py:29
  208.9 6.4 %collective-permute-done = f32[2,512,128]{2,1,0:T(8,128)S(1)} collective-permute-done((f32[2,512,128]{2,1,0:T(8,128)}, f32[2,512,128]{2,1,0:T(8,128)S(1)}, u32[]{:S(2)}, u32[]{:S(2)}) %collective-permute-start) | collective-permute-done | bytes 524320 | tf_op jit(solution)/shard_map/ppermute | solution.py:29
  (41 shorter events, 4.7 us)
Async XLA Ops:
  7.2 4.3 %copy-start.1 = (s32[4096]{0:T(1024)S(1)}, s32[4096]{0:T(1024)}, u32[]{:S(2)}) copy-start(s32[4096]{0:T(1024)} %param.17) | copy-start | bytes 49156
  7.2 4.3 %copy-start.4 = (s32[16,1]{0,1:T(1,128)S(1)}, s32[16,1]{0,1:T(1,128)}, u32[]{:S(2)}) copy-start(s32[16,1]{0,1:T(1,128)} %param.16) | copy-start | bytes 196
  7.2 89.1 %all-gather.4.cloned.1.call-start = ((), (), s32[]{:S(2)}) async-start(), calls=%async_computation.3 | async-start | bytes 9437184 | tf_op jit(solution)/shard_map/all_gather | solution.py:11
  12.5 27.4 %all-to-all-start.1 = ((s32[4,8,256]{2,1,0:T(8,128)}), s32[4,8,256]{2,1,0:T(8,128)S(1)}, u32[]{:S(2)}, u32[]{:S(2)}) async-start(s32[4,8,256]{2,1,0:T(8,128)} %add_bitcast_fusion), calls=%async_computation.1 | async-start | bytes 65536 | tf_op jit(solution)/shard_map/all_to_all | solution.py:87
  39.9 97.5 %all-to-all-start = ((bf16[4,8,256,512]{3,2,1,0:T(8,128)(2,1)}), bf16[4,8,256,512]{3,2,1,0:T(8,128)(2,1)}, u32[]{:S(2)}, u32[]{:S(2)}) async-start(bf16[4,8,256,512]{3,2,1,0:T(8,128)(2,1)} %copy.13), calls=%async_computation | async-start | bytes 16777216 | tf_op jit(solution)/shard_map/all_to_all | solution.py:86
  45.5 159.7 %reduce-scatter.2.cloned.1.call-start = ((), (), s32[]{:S(2)}) async-start(), calls=%async_computation.4 | async-start | bytes 2621440 | tf_op jit(solution)/shard_map/reduce_scatter | solution.py:97
  96.3 17.4 %copy-start = (f32[512]{0:T(512)S(1)}, f32[512]{0:T(512)}, u32[]{:S(2)}) copy-start(f32[512]{0:T(512)} %param.12) | copy-start | bytes 6148
  113.7 0.7 copy-start.2
  152.5 56.4 %copy-start.5 = (s32[128]{0:T(128)S(1)}, s32[128]{0:T(128)}, u32[]{:S(2)}) copy-start(s32[128]{0:T(128)} %param.19) | copy-start | bytes 1540
  152.5 62.8 %copy-start.3 = (f32[128]{0:T(128)S(1)}, f32[128]{0:T(128)}, u32[]{:S(2)}) copy-start(f32[128]{0:T(128)} %param.18) | copy-start | bytes 1540
  205.2 10.1 %collective-permute-start = (f32[2,512,128]{2,1,0:T(8,128)}, f32[2,512,128]{2,1,0:T(8,128)S(1)}, u32[]{:S(2)}, u32[]{:S(2)}) collective-permute-start(f32[2,512,128]{2,1,0:T(8,128)} %reduce-scatter.2.cloned.1.call-done), channel_id=1, source_target_pairs={{0,4},{4,8},{8,12},{12,16},{16,20},{20,24},{24,28},{1,5},{5,9},{9,... | collective-permute-start | bytes 1572872 | tf_op jit(solution)/shard_map/ppermute | solution.py:29
Sparse Core Ops, SparseCore 0:
  11.6 84.6 all-gather.3
  168.7 36.4 reduce-scatter.1
where the time goes:
time: 225 us; the launch traced here: 224 us
  waiting for transfers between devices  102 us (45%)
  matrix products  39.6 us (18%)
  other arithmetic  24.8 us (11%)
  local copies, waits for them, and re-layouts  15.1 us (7%)
  blocking collectives  14.2 us (6%)
  between operations  14.2 us (6%)
  starting transfers between devices  13.6 us (6%)
    reduce_scatter x1, waiting for transfers between devices, on_device(): lax.psum_scatter(partial_sets, 'book', scatter_dimension=2, tiled=True)  36.6 us
    all_gather x1, waiting for transfers between devices, prefix(): everything = jax.tree.map(lambda part: lax.all_gather(part, axis), array)  36.4 us
    all_to_all x1, waiting for transfers between devices, on_device(): lax.all_to_all(packed, 'book', split_axis=0, concat_axis=0, tiled=True)  22.7 us
    select_n x8, other arithmetic, hop(): return jax.tree.map(lambda a, b: jnp.where(reached, a, b), new, before)  17.1 us
    dot_general x1, matrix products, on_device(): jnp.dot(price, onehot, preferred_element_type=jnp.float32)  16.1 us
    dot_general x1, matrix products, on_device(): jnp.einsum('rk,tk->rt', discount, arrived.reshape(-1, width), preferred_e...  15.1 us
    all_gather x1, blocking collectives, prefix(): everything = jax.tree.map(lambda part: lax.all_gather(part, axis), array)  14.2 us
    reshape x1, local copies, waits for them, and re-layouts, on_device(): packed = packed.astype(jnp.bfloat16).reshape(books, most, block_rows, width)  9.87 us
  transfers between devices with their start and end apart: 5, of which 4 were waited for; matrix products, arithmetic and copies ran while one was open for 19% of the time, Pallas kernels for 0%

commit v1 on v0

v1 whole, which is shorter than its diff:
```python
import functools

import jax
import jax.numpy as jnp
from jax import lax
from jax.experimental import pallas as pl
from jax.experimental.pallas import tpu as pltpu
from jax.sharding import PartitionSpec as P

SETS = 512
CORES = 2
SHOCK = 6.0
TOP = 32760.0
MIB = 1 << 20


def swap(block):
    n = lax.axis_size("date")
    return lax.ppermute(block, "date", [(i, i ^ 1) for i in range(n)])


def later(block, chips):
    n = lax.axis_size("date")
    hop = CORES * chips
    return lax.ppermute(block, "date", [(i, i + hop) for i in range(n - hop)])


def exchange(slots):
    n = len(slots)
    return [
        lax.ppermute(slots[i], "book", [(j, j ^ i) for j in range(n)])
        for i in range(1, n)
    ]


def weights_kernel(books, per, here_ref, owner_ref, sets_ref, flows_ref, *refs):
    outs, total = refs[:books], refs[books]
    step = pl.program_id(0)
    core, me = here_ref[0], here_ref[1]
    half = outs[0].shape[0]
    rows = sets_ref.shape[2] // per
    sets_here = SETS // books

    @pl.when(step == 0)
    def _():
        total[...] = jnp.zeros_like(total)

    row = lax.broadcasted_iota(jnp.int32, (half, rows), 0) + core * half
    for b in range(per):
        owner = owner_ref[step * per + b]
        name = sets_ref[0, :, b * rows : (b + 1) * rows]
        name = ((name // sets_here) ^ owner) * sets_here + name % sets_here
        hot = jnp.where(name == row, 1.0, 0.0).astype(jnp.bfloat16)
        part = jnp.dot(
            hot, flows_ref[b * rows : (b + 1) * rows, :], preferred_element_type=jnp.float32
        )
        slot = owner ^ me
        total[slot] = total[slot] + part

    @pl.when(step == pl.num_programs(0) - 1)
    def _():
        for i in range(books):
            outs[i][...] = total[i].astype(outs[i].dtype)


def weights(here, owners, trade_set, cashflows, books):
    blocks = owners.shape[0]
    trades, width = cashflows.shape
    rows = trades // blocks
    per = 4 if blocks % 4 == 0 else 1
    steps = blocks // per
    half = SETS // CORES
    return pl.pallas_call(
        functools.partial(weights_kernel, books, per),
        grid_spec=pltpu.PrefetchScalarGridSpec(
            num_scalar_prefetch=2,
            grid=(steps,),
            in_specs=[
                pl.BlockSpec((1, 1, per * rows), lambda i, *_: (i, 0, 0)),
                pl.BlockSpec((per * rows, width), lambda i, *_: (i, 0)),
            ],
            out_specs=[pl.BlockSpec((half, width), lambda i, *_: (0, 0))] * books,
            scratch_shapes=[pltpu.VMEM((books, half, width), jnp.float32)],
        ),
        out_shape=[
            jax.ShapeDtypeStruct((half, width), jnp.bfloat16 if i else jnp.float32)
            for i in range(books)
        ],
        compiler_params=pltpu.CompilerParams(vmem_limit_bytes=32 * MIB),
        cost_estimate=pl.CostEstimate(
            flops=2 * trades * half * width, bytes_accessed=2 * trades * width, transcendentals=0
        ),
        name="weights",
    )(here, owners, trade_set.reshape(steps, 1, per * rows), cashflows)


def values_kernel(books, here_ref, par_ref, first_ref, second_ref, start_ref, mine_ref, other_ref, *refs):
    outs, matrix, disc = refs[:books], refs[books], refs[books + 1]
    core = here_ref[0]
    dates, paths, width = first_ref.shape
    half = mine_ref.shape[0]
    matrix[pl.ds(core * half, half), :] = mine_ref[...]
    matrix[pl.ds((1 - core) * half, half), :] = other_ref[...]
    tile = 32

    def walk(i, _):
        at = pl.ds(i * tile, tile)
        pers, vol, base = par_ref[0:1, :], par_ref[1:2, :], par_ref[2:3, :]
        state = start_ref[at, :]
        for t in range(2 * dates):
            source = first_ref if t < dates else second_ref
            state = pers * state + vol * source[t % dates, at, :].astype(jnp.float32)
            disc[pl.ds(t * paths + i * tile, tile), :] = jnp.exp(-(base + state)).astype(jnp.bfloat16)
        return 0

    lax.fori_loop(0, paths // tile, walk, 0)
    sets_here = SETS // books
    rows = 256
    for r in range(2 * dates * paths // rows):
        part = lax.dot_general(
            disc[r * rows : (r + 1) * rows, :],
            matrix[...],
            (((1,), (1,)), ((), ())),
            preferred_element_type=jnp.float32,
        )
        for i in range(books):
            outs[i][r * rows : (r + 1) * rows, :] = part[:, i * sets_here : (i + 1) * sets_here].astype(
                outs[i].dtype
            )


def values(here, par, first, second, start, mine, other, books):
    dates, paths, width = first.shape
    rows = 2 * dates * paths
    whole = pl.BlockSpec(memory_space=pltpu.VMEM)
    return pl.pallas_call(
        functools.partial(values_kernel, books),
        in_specs=[pl.BlockSpec(memory_space=pltpu.SMEM)] + [whole] * 6,
        out_specs=[whole] * books,
        out_shape=[
            jax.ShapeDtypeStruct((rows, SETS // books), jnp.bfloat16 if i else jnp.float32)
            for i in range(books)
        ],
        scratch_shapes=[
            pltpu.VMEM((SETS, width), jnp.bfloat16),
            pltpu.VMEM((rows, width), jnp.bfloat16),
        ],
        compiler_params=pltpu.CompilerParams(vmem_limit_bytes=32 * MIB),
        cost_estimate=pl.CostEstimate(
            flops=2 * rows * SETS * width, bytes_accessed=4 * MIB, transcendentals=rows * width
        ),
        name="values",
    )(here, par, first, second, start, mine, other)


def on_device(
    shocks,
    persistence,
    volatility,
    base_rate,
    cashflows,
    block_owner,
    trade_set,
    threshold,
    margin_lag,
):
    dates, paths, width = shocks.shape
    books = lax.axis_size("book")
    chips = lax.axis_size("date") // CORES
    me = lax.axis_index("book")
    core = lax.axis_index("date") % CORES
    here = jnp.stack([core, me]).astype(jnp.int32)
    half = paths // CORES
    span = CORES * dates

    def side(array, which, axis):
        size = array.shape[axis] // CORES
        return lax.dynamic_slice_in_dim(array, which * size, size, axis)

    kept = side(shocks, core, 1)
    got = swap(side(shocks, 1 - core, 1))
    first = jnp.where(core == 0, kept, got)
    second = jnp.where(core == 0, got, kept)

    power = [jnp.ones_like(persistence)]
    for _ in range(span * chips):
        power.append(power[-1] * persistence)
    decay = power[span]

    gain = jnp.zeros((half, width), jnp.float32)
    for t in range(span):
        source = first if t < dates else second
        gain = persistence * gain + volatility * source[t % dates].astype(jnp.float32)

    mats = weights(here, block_owner[:, 0], trade_set, cashflows, books)

    start = jnp.zeros((half, width), jnp.float32)
    reach, fade = 1, jnp.ones_like(decay)
    while reach < chips:
        bound = SHOCK * volatility * sum(power[: min(reach, chips) * span])
        upto = gain + decay * start
        code = jnp.round(upto * (TOP / bound)).astype(jnp.int16)
        came = later(code, reach).astype(jnp.float32) * (bound / TOP)
        start = start + fade * came
        fade = fade * power[reach * span]
        reach *= 2

    mine = mats[0]
    for part in exchange(mats):
        mine = mine + part.astype(jnp.float32)
    mine = mine.astype(jnp.bfloat16)
    other = swap(mine)

    par = jnp.stack([persistence, volatility, base_rate])
    pieces = values(here, par, first, second, start, mine, other, books)
    net = pieces[0]
    for part in exchange(pieces):
        net = net + part.astype(jnp.float32)
    sets_here = SETS // books
    net = net.reshape(span, half, sets_here)

    before = later(net[span - dates :].astype(jnp.bfloat16), 1).astype(jnp.float32)
    net_got = swap(side(net, 1 - core, 0))
    net_kept = side(net, core, 0)
    net_value = jnp.concatenate(
        [jnp.where(core == 0, net_kept, net_got), jnp.where(core == 0, net_got, net_kept)], 1
    )

    joined = jnp.concatenate([before, net], 0)
    collateral = jnp.zeros_like(net)
    for lag in range(1, dates + 1):
        collateral = jnp.where(
            margin_lag[None, None, :] == lag, joined[dates - lag : dates - lag + span], collateral
        )
    exposure = jnp.sum(jnp.maximum(net - collateral - threshold[None, None, :], 0.0), axis=1)
    exposure = side(exposure, core, 0) + swap(side(exposure, 1 - core, 0))
    return (net_value, exposure / paths)


def solution(mesh):
    return jax.shard_map(
        on_device,
        mesh=mesh,
        in_specs=(
            P("date", None, "book"),
            P("book"),
            P("book"),
            P("book"),
            P("book", None),
            P("book", None),
            P("book"),
            P("book"),
            P("book"),
        ),
        out_specs=(P("date", None, "book"), P("date", "book")),
        check_vma=False,
    )
```

time: 225 us -> 59.3 us (0.26)
  the two profiles are of different devices: /device:TPU:1 before, /device:TPU:0 now
where the time goes in v1:
time: 59.3 us; the launch traced here: 58.5 us
  waiting for transfers between devices  23.3 us (39%)
  starting transfers between devices  20.7 us (35%)
  other arithmetic  5.66 us (10%)
  Pallas kernels  4.58 us (8%)
  local copies, waits for them, and re-layouts  3.36 us (6%)
  between operations  0.93 us (2%)
    ppermute x6, waiting for transfers between devices, exchange(): lax.ppermute(slots[i], 'book', [(j, j ^ i) for j in range(n)])  17.8 us
    ppermute x3, starting transfers between devices, later(): return lax.ppermute(block, 'date', [(i, i + hop) for i in range(n - hop)])  12.8 us
    ppermute x6, starting transfers between devices, exchange(): lax.ppermute(slots[i], 'book', [(j, j ^ i) for j in range(n)])  7.11 us
    ppermute x4, waiting for transfers between devices, swap(): return lax.ppermute(block, 'date', [(i, i ^ 1) for i in range(n)])  3.14 us
    pallas_call x1, Pallas kernels, weights(): pl.pallas_call(functools.partial(weights_kernel, books, per), grid_spec=p...  2.6 us
    ppermute x3, waiting for transfers between devices, later(): return lax.ppermute(block, 'date', [(i, i + hop) for i in range(n - hop)])  2.36 us
    unnamed x16, local copies, waits for them, and re-layouts  2.22 us
    pallas_call x1, Pallas kernels, values(): pl.pallas_call(functools.partial(values_kernel, books), in_specs=[pl.Bloc...  1.98 us
  transfers between devices with their start and end apart: 13, of which 9 were waited for; matrix products, arithmetic and copies ran while one was open for 4% of the time, Pallas kernels for 4%

profile of v1, /device:TPU:0, one launch (start us, length us, event | category | flops | bytes accessed | tf_op | source)
XLA Modules:
  0.0 58.5 jit_solution(9932777594703154558)
XLA Ops:
  0.7 1.1 %constant_dynamic-slice_fusion.3 = bf16[2,256,512]{2,1,0:T(8,128)(2,1)S(1)} fusion(bf16[2,512,512]{2,1,0:T(8,128)(2,1)} %param.9, s32[]{:T(128)S(6)} %select_n.56), kind=kLoop, calls=%fused_computation.47 | loop fusion | bytes 1048580 | tf_op jit(solution)/shard_map/dynamic_slice | solution.py:178
  2.4 0.7 %broadcast_multiply_fusion = (f32[512]{0:T(512)S(1)}, f32[512]{0:T(512)S(1)}, f32[512]{0:T(512)S(1)}, f32[512]{0:T(512)S(1)}, f32[512]{0:T(512)S(1)}, /*index=5*/f32[512]{0:T(512)S(1)}, f32[512]{0:T(512)S(1)}) fusion(f32[512]{0:T(512)} %param.10, f32[512]{0:T(512)} %param.11), kind=kLoop, calls=%fused_computation.50 | loop fusion | flops 10752 | bytes 18432 | tf_op jit(solution)/shard_map/div | solution.py:203
  3.1 0.8 %collective-permute-done = bf16[2,256,512]{2,1,0:T(8,128)(2,1)S(1)} collective-permute-done((bf16[2,256,512]{2,1,0:T(8,128)(2,1)S(1)}, bf16[2,256,512]{2,1,0:T(8,128)(2,1)S(1)}, u32[]{:S(2)}, u32[]{:S(2)}) %collective-permute-start) | collective-permute-done | bytes 524320 | tf_op jit(solution)/shard_map/ppermute | solution.py:19
  3.8 1.2 %broadcast_select_fusion = (bf16[2,256,512]{2,1,0:T(8,128)(2,1)S(1)}, bf16[2,256,512]{2,1,0:T(8,128)(2,1)S(1)}) fusion(bf16[2,256,512]{2,1,0:T(8,128)(2,1)S(1)} %collective-permute-done, pred[]{:T(512)S(6)} %eq.22, bf16[2,512,512]{2,1,0:T(8,128)(2,1)} %param.9, s32[]{:T(128)S(6)} %select_n.55), kind=kLoop, calls=%fused_computation.28 | loop fusion | flops 524288 | bytes 2097157 | tf_op jit(solution)/shard_map/jit(_where)/select_n | solution.py:183
  5.1 1.1 %round-nearest-even_convert_fusion.1 = s16[256,512]{1,0:T(8,128)(2,1)S(1)} fusion(f32[512]{0:T(512)S(1)} %get-tuple-element.25, f32[512]{0:T(512)S(1)} %get-tuple-element.28, bf16[2,256,512]{2,1,0:T(8,128)(2,1)S(1)} %get-tuple-element.20.second_ref, bf16[2,256,512]{2,1,0:T(8,128)(2,1)S(1)} %get-tuple-element.21.first_ref, f32[512]{0:T(512)} %param.11, ...), kind=kLoop, calls=%fused_computation.27 | loop fusion | flops 2490368 | bytes 1320960 | tf_op jit(solution)/shard_map/convert_element_type | solution.py:202
  6.2 4.9 %collective-permute-start.1 = (s16[256,512]{1,0:T(8,128)(2,1)S(1)}, s16[256,512]{1,0:T(8,128)(2,1)S(1)}, u32[]{:S(2)}, u32[]{:S(2)}) collective-permute-start(s16[256,512]{1,0:T(8,128)(2,1)S(1)} %round-nearest-even_convert_fusion.1), channel_id=1, source_target_pairs={{0,8},{4,12},{8,16},{12,20},{16,24},{20,28},{1,9},{5,13},{9,17},{1... | collective-permute-start | bytes 786440 | tf_op jit(solution)/shard_map/ppermute | solution.py:25
  11.1 2.2 %copy-done = bf16[4096,512]{1,0:T(8,128)(2,1)S(1)} copy-done((bf16[4096,512]{1,0:T(8,128)(2,1)S(1)}, bf16[4096,512]{1,0:T(8,128)(2,1)}, u32[]{:S(2)}) %copy-start) | copy-done | bytes 4194328
  13.2 2.6 %weights.1 = (f32[256,512]{1,0:T(8,128)S(1)}, bf16[256,512]{1,0:T(8,128)(2,1)S(1)}, bf16[256,512]{1,0:T(8,128)(2,1)S(1)}, bf16[256,512]{1,0:T(8,128)(2,1)S(1)}) custom-call(s32[2]{0:T(128)S(1)} %pad_add_fusion.here_ref, s32[16]{0:T(128)S(1)} %bitcast.46, s32[4,1,1024]{2,1,0:T(1,128)S(1)} %bitcast.45, bf16[4096,512]{1,0:T(8,128)(2,1)S(1)} %copy-done), custom_call_target="tpu_custom_call" | custom-call | flops 1073741824 | bytes 4194304 | tf_op jit(solution)/shard_map/weights/pallas_call | solution.py:73
  15.9 1.6 %collective-permute-start.3 = (bf16[256,512]{1,0:T(8,128)(2,1)S(1)}, bf16[256,512]{1,0:T(8,128)(2,1)S(1)}, u32[]{:S(2)}, u32[]{:S(2)}) collective-permute-start(bf16[256,512]{1,0:T(8,128)(2,1)S(1)} %get-tuple-element.11), channel_id=1, source_target_pairs={{0,1},{1,0},{2,3},{3,2},{4,5},{5,4},{6,7},{7,6},{8,9},{9,8},{10,11... | collective-permute-start | bytes 786440 | tf_op jit(solution)/shard_map/ppermute | solution.py:31
  17.4 1.5 %collective-permute-start.4 = (bf16[256,512]{1,0:T(8,128)(2,1)S(1)}, bf16[256,512]{1,0:T(8,128)(2,1)S(1)}, u32[]{:S(2)}, u32[]{:S(2)}) collective-permute-start(bf16[256,512]{1,0:T(8,128)(2,1)S(1)} %get-tuple-element.12), channel_id=1, source_target_pairs={{0,2},{1,3},{2,0},{3,1},{4,6},{5,7},{6,4},{7,5},{8,10},{9,11},{10,... | collective-permute-start | bytes 786440 | tf_op jit(solution)/shard_map/ppermute | solution.py:31
  19.9 4.5 %collective-permute-start.2 = (s16[256,512]{1,0:T(8,128)(2,1)S(1)}, s16[256,512]{1,0:T(8,128)(2,1)S(1)}, u32[]{:S(2)}, u32[]{:S(2)}) collective-permute-start(s16[256,512]{1,0:T(8,128)(2,1)S(1)} %round-nearest-even_convert_fusion), channel_id=1, source_target_pairs={{0,16},{4,20},{8,24},{12,28},{1,17},{5,21},{9,25},{13,29},{2,18},{... | collective-permute-start | bytes 786440 | tf_op jit(solution)/shard_map/ppermute | solution.py:25
  25.1 5.7 %collective-permute-done.4 = bf16[256,512]{1,0:T(8,128)(2,1)S(1)} collective-permute-done((bf16[256,512]{1,0:T(8,128)(2,1)S(1)}, bf16[256,512]{1,0:T(8,128)(2,1)S(1)}, u32[]{:S(2)}, u32[]{:S(2)}) %collective-permute-start.4) | collective-permute-done | bytes 262176 | tf_op jit(solution)/shard_map/ppermute | solution.py:31
  31.3 1.3 %collective-permute-done.6.other_ref = bf16[256,512]{1,0:T(8,128)(2,1)S(1)} collective-permute-done((bf16[256,512]{1,0:T(8,128)(2,1)S(1)}, bf16[256,512]{1,0:T(8,128)(2,1)S(1)}, u32[]{:S(2)}, u32[]{:S(2)}) %collective-permute-start.6) | collective-permute-done | bytes 262176 | tf_op jit(solution)/shard_map/ppermute | solution.py:19
  32.6 2.0 %values.1 = (f32[1024,128]{1,0:T(8,128)S(1)}, bf16[1024,128]{1,0:T(8,128)(2,1)S(1)}, bf16[1024,128]{1,0:T(8,128)(2,1)S(1)}, bf16[1024,128]{1,0:T(8,128)(2,1)S(1)}) custom-call(s32[2]{0:T(128)S(1)} %pad_add_fusion.here_ref, f32[3,512]{1,0:T(4,128)S(1)} %pad_maximum_fusion.2.par_ref, bf16[2,256,512]{2,1,0:T(8,128)(2,1)S(1)} %get-tuple-element.21.first_ref, ...), custom_call_target="tpu_custom_call" | custom-call | flops 536870912 | bytes 4194304 | tf_op jit(solution)/shard_map/values/pallas_call | solution.py:136
  34.6 1.3 %collective-permute-start.7 = (bf16[1024,128]{1,0:T(8,128)(2,1)S(1)}, bf16[1024,128]{1,0:T(8,128)(2,1)S(1)}, u32[]{:S(2)}, u32[]{:S(2)}) collective-permute-start(bf16[1024,128]{1,0:T(8,128)(2,1)S(1)} %get-tuple-element.15), channel_id=1, source_target_pairs={{0,1},{1,0},{2,3},{3,2},{4,5},{5,4},{6,7},{7,6},{8,9},{9,8},{10,11... | collective-permute-start | bytes 786440 | tf_op jit(solution)/shard_map/ppermute | solution.py:31
  35.9 0.8 %collective-permute-start.8 = (bf16[1024,128]{1,0:T(8,128)(2,1)S(1)}, bf16[1024,128]{1,0:T(8,128)(2,1)S(1)}, u32[]{:S(2)}, u32[]{:S(2)}) collective-permute-start(bf16[1024,128]{1,0:T(8,128)(2,1)S(1)} %get-tuple-element.16), channel_id=1, source_target_pairs={{0,2},{1,3},{2,0},{3,1},{4,6},{5,7},{6,4},{7,5},{8,10},{9,11},{10,... | collective-permute-start | bytes 786440 | tf_op jit(solution)/shard_map/ppermute | solution.py:31
  36.7 1.4 %collective-permute-start.9 = (bf16[1024,128]{1,0:T(8,128)(2,1)S(1)}, bf16[1024,128]{1,0:T(8,128)(2,1)S(1)}, u32[]{:S(2)}, u32[]{:S(2)}) collective-permute-start(bf16[1024,128]{1,0:T(8,128)(2,1)S(1)} %get-tuple-element.17), channel_id=1, source_target_pairs={{0,3},{1,2},{2,1},{3,0},{4,7},{5,6},{6,5},{7,4},{8,11},{9,10},{10,... | collective-permute-start | bytes 786440 | tf_op jit(solution)/shard_map/ppermute | solution.py:31
  38.1 5.7 %collective-permute-done.7 = bf16[1024,128]{1,0:T(8,128)(2,1)S(1)} collective-permute-done((bf16[1024,128]{1,0:T(8,128)(2,1)S(1)}, bf16[1024,128]{1,0:T(8,128)(2,1)S(1)}, u32[]{:S(2)}, u32[]{:S(2)}) %collective-permute-start.7) | collective-permute-done | bytes 262176 | tf_op jit(solution)/shard_map/ppermute | solution.py:31
  43.8 4.1 %collective-permute-done.8 = bf16[1024,128]{1,0:T(8,128)(2,1)S(1)} collective-permute-done((bf16[1024,128]{1,0:T(8,128)(2,1)S(1)}, bf16[1024,128]{1,0:T(8,128)(2,1)S(1)}, u32[]{:S(2)}, u32[]{:S(2)}) %collective-permute-start.8) | collective-permute-done | bytes 262176 | tf_op jit(solution)/shard_map/ppermute | solution.py:31
  47.9 1.6 %collective-permute-done.9 = bf16[1024,128]{1,0:T(8,128)(2,1)S(1)} collective-permute-done((bf16[1024,128]{1,0:T(8,128)(2,1)S(1)}, bf16[1024,128]{1,0:T(8,128)(2,1)S(1)}, u32[]{:S(2)}, u32[]{:S(2)}) %collective-permute-start.9) | collective-permute-done | bytes 262176 | tf_op jit(solution)/shard_map/ppermute | solution.py:31
  49.7 3.5 %collective-permute-start.11 = (bf16[2,256,128]{2,1,0:T(8,128)(2,1)S(1)}, bf16[2,256,128]{2,1,0:T(8,128)(2,1)S(1)}, u32[]{:S(2)}, u32[]{:S(2)}) collective-permute-start(bf16[2,256,128]{2,1,0:T(8,128)(2,1)S(1)} %bitcast.50), channel_id=1, source_target_pairs={{0,8},{4,12},{8,16},{12,20},{16,24},{20,28},{1,9},{5,13},{9,17},{1... | collective-permute-start | bytes 393224 | tf_op jit(solution)/shard_map/ppermute | solution.py:25
  53.4 2.4 %collective-permute-done.11 = bf16[2,256,128]{2,1,0:T(8,128)(2,1)S(1)} collective-permute-done((bf16[2,256,128]{2,1,0:T(8,128)(2,1)S(1)}, bf16[2,256,128]{2,1,0:T(8,128)(2,1)S(1)}, u32[]{:S(2)}, u32[]{:S(2)}) %collective-permute-start.11) | collective-permute-done | bytes 131104 | tf_op jit(solution)/shard_map/ppermute | solution.py:25
  56.0 1.1 %collective-permute-done.12 = f32[2,128]{1,0:T(2,128)S(1)} collective-permute-done((f32[2,128]{1,0:T(2,128)S(1)}, f32[2,128]{1,0:T(2,128)S(1)}, u32[]{:S(2)}, u32[]{:S(2)}) %collective-permute-start.12) | collective-permute-done | bytes 1056 | tf_op jit(solution)/shard_map/ppermute | solution.py:19
  57.7 0.8 %pad_maximum_fusion.1 = f32[2,512,128]{2,1,0:T(8,128)} fusion(f32[2,256,128]{2,1,0:T(8,128)S(1)} %get-tuple-element.23, f32[2,256,128]{2,1,0:T(8,128)S(1)} %get-tuple-element.22), kind=kLoop, calls=%fused_computation.10 | loop fusion | flops 131072 | bytes 1048576 | tf_op jit(solution)/shard_map/concatenate | solution.py:225
  (40 shorter events, 3.8 us)
Async XLA Ops:
  0.6 10.4 %copy-start.1 = (s32[4096]{0:T(1024)S(1)}, s32[4096]{0:T(1024)}, u32[]{:S(2)}) copy-start(s32[4096]{0:T(1024)} %param.15) | copy-start | bytes 49156
  0.6 10.4 %copy-start.2 = (s32[16,1]{0,1:T(1,128)S(1)}, s32[16,1]{0,1:T(1,128)}, u32[]{:S(2)}) copy-start(s32[16,1]{0,1:T(1,128)} %param.14) | copy-start | bytes 196
  0.7 18.7 %copy-start.3 = (f32[512]{0:T(512)S(1)}, f32[512]{0:T(512)}, u32[]{:S(2)}) copy-start(f32[512]{0:T(512)} %param.11) | copy-start | bytes 6148
  0.7 18.7 %copy-start.4 = (f32[512]{0:T(512)S(1)}, f32[512]{0:T(512)}, u32[]{:S(2)}) copy-start(f32[512]{0:T(512)} %param.10) | copy-start | bytes 6148
  1.8 2.1 %collective-permute-start = (bf16[2,256,512]{2,1,0:T(8,128)(2,1)S(1)}, bf16[2,256,512]{2,1,0:T(8,128)(2,1)S(1)}, u32[]{:S(2)}, u32[]{:S(2)}) collective-permute-start(bf16[2,256,512]{2,1,0:T(8,128)(2,1)S(1)} %constant_dynamic-slice_fusion.3), channel_id=1, source_target_pairs={{0,4},{4,0},{8,12},{12,8},{16,20},{20,16},{24,28},{28,24},{1,5},{5... | collective-permute-start | bytes 1572872 | tf_op jit(solution)/shard_map/ppermute | solution.py:19
  5.1 26.0 %copy-start.5 = (f32[512]{0:T(512)S(1)}, f32[512]{0:T(512)}, u32[]{:S(2)}) copy-start(f32[512]{0:T(512)} %param.12) | copy-start | bytes 6148
  6.2 13.3 %collective-permute-start.1 = (s16[256,512]{1,0:T(8,128)(2,1)S(1)}, s16[256,512]{1,0:T(8,128)(2,1)S(1)}, u32[]{:S(2)}, u32[]{:S(2)}) collective-permute-start(s16[256,512]{1,0:T(8,128)(2,1)S(1)} %round-nearest-even_convert_fusion.1), channel_id=1, source_target_pairs={{0,8},{4,12},{8,16},{12,20},{16,24},{20,28},{1,9},{5,13},{9,17},{1... | collective-permute-start | bytes 786440 | tf_op jit(solution)/shard_map/ppermute | solution.py:25
  11.0 2.2 %copy-start = (bf16[4096,512]{1,0:T(8,128)(2,1)S(1)}, bf16[4096,512]{1,0:T(8,128)(2,1)}, u32[]{:S(2)}) copy-start(bf16[4096,512]{1,0:T(8,128)(2,1)} %flows_ref.1) | copy-start | bytes 12582916
  15.9 9.3 %collective-permute-start.3 = (bf16[256,512]{1,0:T(8,128)(2,1)S(1)}, bf16[256,512]{1,0:T(8,128)(2,1)S(1)}, u32[]{:S(2)}, u32[]{:S(2)}) collective-permute-start(bf16[256,512]{1,0:T(8,128)(2,1)S(1)} %get-tuple-element.11), channel_id=1, source_target_pairs={{0,1},{1,0},{2,3},{3,2},{4,5},{5,4},{6,7},{7,6},{8,9},{9,8},{10,11... | collective-permute-start | bytes 786440 | tf_op jit(solution)/shard_map/ppermute | solution.py:31
  17.4 13.4 %collective-permute-start.4 = (bf16[256,512]{1,0:T(8,128)(2,1)S(1)}, bf16[256,512]{1,0:T(8,128)(2,1)S(1)}, u32[]{:S(2)}, u32[]{:S(2)}) collective-permute-start(bf16[256,512]{1,0:T(8,128)(2,1)S(1)} %get-tuple-element.12), channel_id=1, source_target_pairs={{0,2},{1,3},{2,0},{3,1},{4,6},{5,7},{6,4},{7,5},{8,10},{9,11},{10,... | collective-permute-start | bytes 786440 | tf_op jit(solution)/shard_map/ppermute | solution.py:31
  18.9 11.9 %collective-permute-start.5 = (bf16[256,512]{1,0:T(8,128)(2,1)S(1)}, bf16[256,512]{1,0:T(8,128)(2,1)S(1)}, u32[]{:S(2)}, u32[]{:S(2)}) collective-permute-start(bf16[256,512]{1,0:T(8,128)(2,1)S(1)} %get-tuple-element.13), channel_id=1, source_target_pairs={{0,3},{1,2},{2,1},{3,0},{4,7},{5,6},{6,5},{7,4},{8,11},{9,10},{10,... | collective-permute-start | bytes 786440 | tf_op jit(solution)/shard_map/ppermute | solution.py:31
  19.4 33.8 %copy-start.7 = (s32[128]{0:T(128)S(1)}, s32[128]{0:T(128)}, u32[]{:S(2)}) copy-start(s32[128]{0:T(128)} %param.17) | copy-start | bytes 1540
  19.9 35.8 %copy-start.6 = (f32[128]{0:T(128)S(1)}, f32[128]{0:T(128)}, u32[]{:S(2)}) copy-start(f32[128]{0:T(128)} %param.16) | copy-start | bytes 1540
  19.9 11.2 %collective-permute-start.2 = (s16[256,512]{1,0:T(8,128)(2,1)S(1)}, s16[256,512]{1,0:T(8,128)(2,1)S(1)}, u32[]{:S(2)}, u32[]{:S(2)}) collective-permute-start(s16[256,512]{1,0:T(8,128)(2,1)S(1)} %round-nearest-even_convert_fusion), channel_id=1, source_target_pairs={{0,16},{4,20},{8,24},{12,28},{1,17},{5,21},{9,25},{13,29},{2,18},{... | collective-permute-start | bytes 786440 | tf_op jit(solution)/shard_map/ppermute | solution.py:25
  31.0 1.6 %collective-permute-start.6 = (bf16[256,512]{1,0:T(8,128)(2,1)S(1)}, bf16[256,512]{1,0:T(8,128)(2,1)S(1)}, u32[]{:S(2)}, u32[]{:S(2)}) collective-permute-start(bf16[256,512]{1,0:T(8,128)(2,1)S(1)} %add_convert_fusion.mine_ref), channel_id=1, source_target_pairs={{0,4},{4,0},{8,12},{12,8},{16,20},{20,16},{24,28},{28,24},{1,5},{5... | collective-permute-start | bytes 786440 | tf_op jit(solution)/shard_map/ppermute | solution.py:19
  34.6 9.2 %collective-permute-start.7 = (bf16[1024,128]{1,0:T(8,128)(2,1)S(1)}, bf16[1024,128]{1,0:T(8,128)(2,1)S(1)}, u32[]{:S(2)}, u32[]{:S(2)}) collective-permute-start(bf16[1024,128]{1,0:T(8,128)(2,1)S(1)} %get-tuple-element.15), channel_id=1, source_target_pairs={{0,1},{1,0},{2,3},{3,2},{4,5},{5,4},{6,7},{7,6},{8,9},{9,8},{10,11... | collective-permute-start | bytes 786440 | tf_op jit(solution)/shard_map/ppermute | solution.py:31
  35.9 12.1 %collective-permute-start.8 = (bf16[1024,128]{1,0:T(8,128)(2,1)S(1)}, bf16[1024,128]{1,0:T(8,128)(2,1)S(1)}, u32[]{:S(2)}, u32[]{:S(2)}) collective-permute-start(bf16[1024,128]{1,0:T(8,128)(2,1)S(1)} %get-tuple-element.16), channel_id=1, source_target_pairs={{0,2},{1,3},{2,0},{3,1},{4,6},{5,7},{6,4},{7,5},{8,10},{9,11},{10,... | collective-permute-start | bytes 786440 | tf_op jit(solution)/shard_map/ppermute | solution.py:31
  36.7 12.9 %collective-permute-start.9 = (bf16[1024,128]{1,0:T(8,128)(2,1)S(1)}, bf16[1024,128]{1,0:T(8,128)(2,1)S(1)}, u32[]{:S(2)}, u32[]{:S(2)}) collective-permute-start(bf16[1024,128]{1,0:T(8,128)(2,1)S(1)} %get-tuple-element.17), channel_id=1, source_target_pairs={{0,3},{1,2},{2,1},{3,0},{4,7},{5,6},{6,5},{7,4},{8,11},{9,10},{10,... | collective-permute-start | bytes 786440 | tf_op jit(solution)/shard_map/ppermute | solution.py:31
  49.7 6.0 %collective-permute-start.11 = (bf16[2,256,128]{2,1,0:T(8,128)(2,1)S(1)}, bf16[2,256,128]{2,1,0:T(8,128)(2,1)S(1)}, u32[]{:S(2)}, u32[]{:S(2)}) collective-permute-start(bf16[2,256,128]{2,1,0:T(8,128)(2,1)S(1)} %bitcast.50), channel_id=1, source_target_pairs={{0,8},{4,12},{8,16},{12,20},{16,24},{20,28},{1,9},{5,13},{9,17},{1... | collective-permute-start | bytes 393224 | tf_op jit(solution)/shard_map/ppermute | solution.py:25
  53.3 4.4 %collective-permute-start.10 = (f32[2,256,128]{2,1,0:T(8,128)S(1)}, f32[2,256,128]{2,1,0:T(8,128)S(1)}, u32[]{:S(2)}, u32[]{:S(2)}) collective-permute-start(f32[2,256,128]{2,1,0:T(8,128)S(1)} %constant_dynamic-slice_fusion.2), channel_id=1, source_target_pairs={{0,4},{4,0},{8,12},{12,8},{16,20},{20,16},{24,28},{28,24},{1,5},{5... | collective-permute-start | bytes 786440 | tf_op jit(solution)/shard_map/ppermute | solution.py:19
  55.9 1.2 %collective-permute-start.12 = (f32[2,128]{1,0:T(2,128)S(1)}, f32[2,128]{1,0:T(2,128)S(1)}, u32[]{:S(2)}, u32[]{:S(2)}) collective-permute-start(f32[2,128]{1,0:T(2,128)S(1)} %constant_dynamic-slice_fusion), channel_id=1, source_target_pairs={{0,4},{4,0},{8,12},{12,8},{16,20},{20,16},{24,28},{28,24},{1,5},{5... | collective-permute-start | bytes 3080 | tf_op jit(solution)/shard_map/ppermute | solution.py:19

commit v2 on v1

--- a/solution.py
+++ b/solution.py
@@ -11,6 +11,7 @@
 CORES = 2
 SHOCK = 6.0
 TOP = 32760.0
+CHUNKS = 2
 MIB = 1 << 20
 
 
@@ -94,22 +95,49 @@
     )(here, owners, trade_set.reshape(steps, 1, per * rows), cashflows)
 
 
-def values_kernel(books, here_ref, par_ref, first_ref, second_ref, start_ref, mine_ref, other_ref, *refs):
-    outs, matrix, disc = refs[:books], refs[books], refs[books + 1]
+def matrix_kernel(here_ref, mine_ref, other_ref, high_ref, low_ref):
     core = here_ref[0]
-    dates, paths, width = first_ref.shape
     half = mine_ref.shape[0]
-    matrix[pl.ds(core * half, half), :] = mine_ref[...]
-    matrix[pl.ds((1 - core) * half, half), :] = other_ref[...]
+    for source, place in ((mine_ref, core), (other_ref, 1 - core)):
+        turned = source[...].T
+        high = turned.astype(jnp.bfloat16)
+        at = pl.ds(pl.multiple_of(place * half, half), half)
+        high_ref[:, at] = high
+        low_ref[:, at] = (turned - high.astype(jnp.float32)).astype(jnp.bfloat16)
+
+
+def matrix(here, mine, other):
+    half, width = mine.shape
+    whole = pl.BlockSpec(memory_space=pltpu.VMEM)
+    return pl.pallas_call(
+        matrix_kernel,
+        in_specs=[pl.BlockSpec(memory_space=pltpu.SMEM)] + [whole] * 2,
+        out_specs=[whole] * 2,
+        out_shape=[jax.ShapeDtypeStruct((width, CORES * half), jnp.bfloat16)] * 2,
+        compiler_params=pltpu.CompilerParams(vmem_limit_bytes=16 * MIB),
+        name="matrix",
+    )(here, mine, other)
+
+
+def values_kernel(books, chunk, here_ref, par_ref, kept_ref, got_ref, high_ref, low_ref, *refs):
+    codes, outs, disc = refs[: -books - 1], refs[-books - 1 : -1], refs[-1]
+    core = here_ref[0]
+    dates = kept_ref.shape[0]
+    paths = disc.shape[0] // (2 * dates)
     tile = 32
 
     def walk(i, _):
         at = pl.ds(i * tile, tile)
+        from_ = pl.ds(chunk * paths + i * tile, tile)
         pers, vol, base = par_ref[0:1, :], par_ref[1:2, :], par_ref[2:3, :]
-        state = start_ref[at, :]
+        state = jnp.zeros((tile, par_ref.shape[1]), jnp.float32)
+        for r, code in enumerate(codes):
+            state = state + par_ref[3 + r : 4 + r, :] * code[at, :].astype(jnp.float32)
         for t in range(2 * dates):
-            source = first_ref if t < dates else second_ref
-            state = pers * state + vol * source[t % dates, at, :].astype(jnp.float32)
+            kept = kept_ref[t % dates, from_, :].astype(jnp.float32)
+            got = got_ref[t % dates, from_, :].astype(jnp.float32)
+            early, late = (kept, got) if t < dates else (got, kept)
+            state = pers * state + vol * jnp.where(core == 0, early, late)
             disc[pl.ds(t * paths + i * tile, tile), :] = jnp.exp(-(base + state)).astype(jnp.bfloat16)
         return 0
 
@@ -117,40 +145,38 @@
     sets_here = SETS // books
     rows = 256
     for r in range(2 * dates * paths // rows):
-        part = lax.dot_general(
-            disc[r * rows : (r + 1) * rows, :],
-            matrix[...],
-            (((1,), (1,)), ((), ())),
-            preferred_element_type=jnp.float32,
-        )
+        price = disc[r * rows : (r + 1) * rows, :]
+        part = jnp.dot(price, high_ref[...], preferred_element_type=jnp.float32)
+        part = part + jnp.dot(price, low_ref[...], preferred_element_type=jnp.float32)
         for i in range(books):
             outs[i][r * rows : (r + 1) * rows, :] = part[:, i * sets_here : (i + 1) * sets_here].astype(
                 outs[i].dtype
             )
 
 
-def values(here, par, first, second, start, mine, other, books):
-    dates, paths, width = first.shape
-    rows = 2 * dates * paths
+def values(here, par, kept, got, high, low, codes, part, books, chunk):
+    dates, _, width = kept.shape
+    rows = 2 * dates * part
     whole = pl.BlockSpec(memory_space=pltpu.VMEM)
     return pl.pallas_call(
-        functools.partial(values_kernel, books),
-        in_specs=[pl.BlockSpec(memory_space=pltpu.SMEM)] + [whole] * 6,
+        functools.partial(values_kernel, books, chunk),
+        in_specs=[pl.BlockSpec(memory_space=pltpu.SMEM)] + [whole] * (5 + len(codes)),
         out_specs=[whole] * books,
         out_shape=[
             jax.ShapeDtypeStruct((rows, SETS // books), jnp.bfloat16 if i else jnp.float32)
             for i in range(books)
         ],
-        scratch_shapes=[
-            pltpu.VMEM((SETS, width), jnp.bfloat16),
-            pltpu.VMEM((rows, width), jnp.bfloat16),
-        ],
-        compiler_params=pltpu.CompilerParams(vmem_limit_bytes=32 * MIB),
+        scratch_shapes=[pltpu.VMEM((rows, width), jnp.bfloat16)],
+        compiler_params=pltpu.CompilerParams(vmem_limit_bytes=16 * MIB),
         cost_estimate=pl.CostEstimate(
-            flops=2 * rows * SETS * width, bytes_accessed=4 * MIB, transcendentals=rows * width
+            flops=4 * rows * SETS * width, bytes_accessed=2 * MIB, transcendentals=rows * width
         ),
         name="values",
-    )(here, par, first, second, start, mine, other)
+    )(here, par, kept, got, high, low, *codes)
+
+
+def after(array, *others):
+    return lax.optimization_barrier((array,) + others)[0]
 
 
 def on_device(
@@ -172,69 +198,95 @@
     here = jnp.stack([core, me]).astype(jnp.int32)
     half = paths // CORES
     span = CORES * dates
+    part = half // CHUNKS
+    sets_here = SETS // books
 
     def side(array, which, axis):
         size = array.shape[axis] // CORES
         return lax.dynamic_slice_in_dim(array, which * size, size, axis)
 
-    kept = side(shocks, core, 1)
-    got = swap(side(shocks, 1 - core, 1))
-    first = jnp.where(core == 0, kept, got)
-    second = jnp.where(core == 0, got, kept)
+    sent = side(shocks, 1 - core, 1)
+    got = swap(sent)
+    mats = weights(after(here, sent), block_owner[:, 0], trade_set, cashflows, books)
+    mats_arrived = exchange(mats)
+    kept = side(after(shocks, mats[0]), core, 1)
 
     power = [jnp.ones_like(persistence)]
     for _ in range(span * chips):
         power.append(power[-1] * persistence)
     decay = power[span]
-
-    gain = jnp.zeros((half, width), jnp.float32)
-    for t in range(span):
-        source = first if t < dates else second
-        gain = persistence * gain + volatility * source[t % dates].astype(jnp.float32)
-
-    mats = weights(here, block_owner[:, 0], trade_set, cashflows, books)
-
-    start = jnp.zeros((half, width), jnp.float32)
+    weigh_kept = jnp.where(core == 0, power[dates], power[0])
+    weigh_got = jnp.where(core == 0, power[0], power[dates])
+
+    def own_sum(array):
+        total = array[0].astype(jnp.float32)
+        for t in range(1, dates):
+            total = persistence * total + array[t].astype(jnp.float32)
+        return total
+
+    def gain(c):
+        rows = slice(c * part, (c + 1) * part)
+        return volatility * (weigh_kept * own_sum(kept[:, rows]) + weigh_got * own_sum(got[:, rows]))
+
+    codes = [[] for _ in range(CHUNKS)]
+    rates = []
     reach, fade = 1, jnp.ones_like(decay)
+    last = mats[0]
     while reach < chips:
         bound = SHOCK * volatility * sum(power[: min(reach, chips) * span])
-        upto = gain + decay * start
-        code = jnp.round(upto * (TOP / bound)).astype(jnp.int16)
-        came = later(code, reach).astype(jnp.float32) * (bound / TOP)
-        start = start + fade * came
+        for c in range(CHUNKS):
+            upto = gain(c)
+            for i in range(len(codes[c])):
+                came = after(codes[c][i], last)
+                upto = upto + (decay * rates[i]) * came.astype(jnp.float32)
+            if not codes[c]:
+                upto = after(upto, last)
+            code = jnp.round(upto * (TOP / bound)).astype(jnp.int16)
+            last = code
+            codes[c].append(later(code, reach))
+        rates.append(fade * (bound / TOP))
         fade = fade * power[reach * span]
         reach *= 2
 
-    mine = mats[0]
-    for part in exchange(mats):
-        mine = mine + part.astype(jnp.float32)
-    mine = mine.astype(jnp.bfloat16)
-    other = swap(mine)
-
-    par = jnp.stack([persistence, volatility, base_rate])
-    pieces = values(here, par, first, second, start, mine, other, books)
-    net = pieces[0]
-    for part in exchange(pieces):
-        net = net + part.astype(jnp.float32)
-    sets_here = SETS // books
-    net = net.reshape(span, half, sets_here)
-
-    before = later(net[span - dates :].astype(jnp.bfloat16), 1).astype(jnp.float32)
-    net_got = swap(side(net, 1 - core, 0))
-    net_kept = side(net, core, 0)
-    net_value = jnp.concatenate(
-        [jnp.where(core == 0, net_kept, net_got), jnp.where(core == 0, net_got, net_kept)], 1
-    )
-
-    joined = jnp.concatenate([before, net], 0)
-    collateral = jnp.zeros_like(net)
-    for lag in range(1, dates + 1):
-        collateral = jnp.where(
-            margin_lag[None, None, :] == lag, joined[dates - lag : dates - lag + span], collateral
-        )
-    exposure = jnp.sum(jnp.maximum(net - collateral - threshold[None, None, :], 0.0), axis=1)
-    exposure = side(exposure, core, 0) + swap(side(exposure, 1 - core, 0))
-    return (net_value, exposure / paths)
+    mine = after(mats[0], last, *codes[0])
+    for arrived in mats_arrived:
+        mine = mine + arrived.astype(jnp.float32)
+    high, low = matrix(here, mine, swap(mine))
+
+    par = jnp.stack([persistence, volatility, base_rate] + rates)
+    pieces, arrivals = [], []
+    last = high
+    for c in range(CHUNKS):
+        came = [after(code, last) for code in codes[c]]
+        pieces.append(values(here, par, kept, got, high, low, came, part, books, c))
+        arrivals.append(exchange(pieces[c]))
+        last = pieces[c][0]
+
+    kept_out, got_out, exposed = [], [], jnp.zeros((span, sets_here), jnp.float32)
+    for c in range(CHUNKS):
+        net = after(pieces[c][0], last)
+        for arrived in arrivals[c]:
+            net = net + arrived.astype(jnp.float32)
+        net = net.reshape(span, part, sets_here)
+        before = later(net[span - dates :].astype(jnp.bfloat16), 1).astype(jnp.float32)
+        got_out.append(swap(side(net, 1 - core, 0)))
+        kept_out.append(side(net, core, 0))
+        joined = jnp.concatenate([before, net], 0)
+        collateral = jnp.zeros_like(net)
+        for lag in range(1, dates + 1):
+            collateral = jnp.where(
+                margin_lag[None, None, :] == lag, joined[dates - lag : dates - lag + span], collateral
+            )
+        exposed = exposed + jnp.sum(jnp.maximum(net - collateral - threshold[None, None, :], 0.0), axis=1)
+        last = exposed
+
+    exposed_got = swap(side(exposed, 1 - core, 0))
+    kept_out[0] = after(kept_out[0], exposed)
+    low_half = [jnp.where(core == 0, a, b) for a, b in zip(kept_out, got_out)]
+    high_half = [jnp.where(core == 0, b, a) for a, b in zip(kept_out, got_out)]
+    net_value = jnp.concatenate(low_half + high_half, 1)
+    net_value, exposed_got = lax.optimization_barrier((net_value, exposed_got))
+    return (net_value, (side(exposed, core, 0) + exposed_got) / paths)
 
 
 def solution(mesh):

time: 59.3 us -> 69 us (1.16)
  starting transfers between devices: 20.7 us -> 39.7 us
  waiting for transfers between devices: 23.3 us -> 5.55 us
  local copies, waits for them, and re-layouts: 3.36 us -> 8.8 us
  Pallas kernels: 4.58 us -> 6.81 us
  other arithmetic: 5.66 us -> 6.58 us
    ppermute x6 -> x9, waiting for transfers between devices: 17.8 us -> 0.02 us  [exchange(): lax.ppermute(slots[i], 'book', [(j, j ^ i) for j in range(n)])]
    ppermute x3 -> x6, starting transfers between devices: 12.8 us -> 26.8 us  [later(): return lax.ppermute(block, 'date', [(i, i + hop) for i in range(n - hop)])]
    ppermute x6 -> x9, starting transfers between devices: 7.11 us -> 12.1 us  [exchange(): lax.ppermute(slots[i], 'book', [(j, j ^ i) for j in range(n)])]
    unnamed x16 -> x26, local copies, waits for them, and re-layouts: 2.22 us -> 6.44 us
    ppermute x3 -> x6, waiting for transfers between devices: 2.36 us -> 5.31 us  [later(): return lax.ppermute(block, 'date', [(i, i + hop) for i in range(n - hop)])]
    ppermute x4 -> x5, waiting for transfers between devices: 3.14 us -> 0.22 us  [swap(): return lax.ppermute(block, 'date', [(i, i ^ 1) for i in range(n)])]
    pallas_call x1 -> x3, Pallas kernels: 1.98 us -> 4.21 us  [the longest x2 3.33 us: values(): pl.pallas_call(functools.partial(values_kernel, books, chunk), in_specs=[...]
    add x2 -> x4, other arithmetic: 0.34 us -> 2.4 us  [the longest x1 1.24 us: on_device(): mine = mine + arrived.astype(jnp.float32)]
  transfers between devices with their start and end apart: 13 -> 20, of which waited for: 9 -> 4; matrix products, arithmetic and copies ran while one was open for 4% -> 9% of each run, Pallas kernels for 4% -> 10%
where the time goes in v2:
time: 69 us; the launch traced here: 68.5 us
  starting transfers between devices  39.7 us (58%)
  local copies, waits for them, and re-layouts  8.8 us (13%)
  Pallas kernels  6.81 us (10%)
  other arithmetic  6.58 us (10%)
  waiting for transfers between devices  5.55 us (8%)
  between operations  1.04 us (2%)
    ppermute x6, starting transfers between devices, later(): return lax.ppermute(block, 'date', [(i, i + hop) for i in range(n - hop)])  26.8 us
    ppermute x9, starting transfers between devices, exchange(): lax.ppermute(slots[i], 'book', [(j, j ^ i) for j in range(n)])  12.1 us
    unnamed x26, local copies, waits for them, and re-layouts  6.44 us
    ppermute x6, waiting for transfers between devices, later(): return lax.ppermute(block, 'date', [(i, i + hop) for i in range(n - hop)])  5.31 us
    pallas_call x2, Pallas kernels, values(): pl.pallas_call(functools.partial(values_kernel, books, chunk), in_specs=[...  3.33 us
    pallas_call x1, Pallas kernels, weights(): pl.pallas_call(functools.partial(weights_kernel, books, per), grid_spec=p...  2.6 us
    dynamic_slice x5, local copies, waits for them, and re-layouts, side(): return lax.dynamic_slice_in_dim(array, which * size, size, axis)  2.31 us
  transfers between devices with their start and end apart: 20, of which 4 were waited for; matrix products, arithmetic and copies ran while one was open for 9% of the time, Pallas kernels for 10%

profile of v2, /device:TPU:0, one launch (start us, length us, event | category | flops | bytes accessed | tf_op | source)
XLA Modules:
  0.0 68.5 jit_solution(13673769942027682372)
XLA Ops:
  0.7 1.2 %constant_dynamic-slice_fusion.6 = bf16[2,256,512]{2,1,0:T(8,128)(2,1)S(1)} fusion(bf16[2,512,512]{2,1,0:T(8,128)(2,1)} %param.9, s32[]{:T(128)S(6)} %select_n.70), kind=kLoop, calls=%fused_computation.64 | loop fusion | bytes 1048580 | tf_op jit(solution)/shard_map/dynamic_slice | solution.py:206
  2.4 2.2 %copy-done = bf16[4096,512]{1,0:T(8,128)(2,1)S(1)} copy-done((bf16[4096,512]{1,0:T(8,128)(2,1)S(1)}, bf16[4096,512]{1,0:T(8,128)(2,1)}, u32[]{:S(2)}) %copy-start) | copy-done | bytes 4194328
  6.0 2.6 %weights.1 = (f32[256,512]{1,0:T(8,128)S(1)}, bf16[256,512]{1,0:T(8,128)(2,1)S(1)}, bf16[256,512]{1,0:T(8,128)(2,1)S(1)}, bf16[256,512]{1,0:T(8,128)(2,1)S(1)}) custom-call(s32[2]{0:T(128)S(1)} %pad_add_fusion.here_ref, s32[16]{0:T(128)S(1)} %bitcast.54, s32[4,1,1024]{2,1,0:T(1,128)S(1)} %bitcast.53, bf16[4096,512]{1,0:T(8,128)(2,1)S(1)} %copy-done), custom_call_target="tpu_custom_call" | custom-call | flops 1073741824 | bytes 4194304 | tf_op jit(solution)/shard_map/weights/pallas_call | solution.py:74
  8.6 2.6 %collective-permute-start.4 = (bf16[256,512]{1,0:T(8,128)(2,1)S(1)}, bf16[256,512]{1,0:T(8,128)(2,1)}, u32[]{:S(2)}, u32[]{:S(2)}) collective-permute-start(bf16[256,512]{1,0:T(8,128)(2,1)S(1)} %get-tuple-element.40), channel_id=1, source_target_pairs={{0,1},{1,0},{2,3},{3,2},{4,5},{5,4},{6,7},{7,6},{8,9},{9,8},{10,11... | collective-permute-start | bytes 786440 | tf_op jit(solution)/shard_map/ppermute | solution.py:32
  11.2 1.5 %collective-permute-start.5 = (bf16[256,512]{1,0:T(8,128)(2,1)S(1)}, bf16[256,512]{1,0:T(8,128)(2,1)}, u32[]{:S(2)}, u32[]{:S(2)}) collective-permute-start(bf16[256,512]{1,0:T(8,128)(2,1)S(1)} %get-tuple-element.41), channel_id=1, source_target_pairs={{0,2},{1,3},{2,0},{3,1},{4,6},{5,7},{6,4},{7,5},{8,10},{9,11},{10,... | collective-permute-start | bytes 786440 | tf_op jit(solution)/shard_map/ppermute | solution.py:32
  13.1 3.9 %collective-permute-start.2 = (s16[128,512]{1,0:T(8,128)(2,1)S(1)}, s16[128,512]{1,0:T(8,128)(2,1)S(1)}, u32[]{:S(2)}, u32[]{:S(2)}) collective-permute-start(s16[128,512]{1,0:T(8,128)(2,1)S(1)} %round-nearest-even_convert_fusion.3), channel_id=1, source_target_pairs={{0,8},{4,12},{8,16},{12,20},{16,24},{20,28},{1,9},{5,13},{9,17},{1... | collective-permute-start | bytes 393224 | tf_op jit(solution)/shard_map/ppermute | solution.py:26
  17.1 3.5 %collective-permute-start.1 = (s16[128,512]{1,0:T(8,128)(2,1)S(1)}, s16[128,512]{1,0:T(8,128)(2,1)S(1)}, u32[]{:S(2)}, u32[]{:S(2)}) collective-permute-start(s16[128,512]{1,0:T(8,128)(2,1)S(1)} %round-nearest-even_convert_fusion.2), channel_id=1, source_target_pairs={{0,8},{4,12},{8,16},{12,20},{16,24},{20,28},{1,9},{5,13},{9,17},{1... | collective-permute-start | bytes 393224 | tf_op jit(solution)/shard_map/ppermute | solution.py:26
  20.7 4.4 %collective-permute-start.3 = (s16[128,512]{1,0:T(8,128)(2,1)S(1)}, s16[128,512]{1,0:T(8,128)(2,1)S(1)}, u32[]{:S(2)}, u32[]{:S(2)}) collective-permute-start(s16[128,512]{1,0:T(8,128)(2,1)S(1)} %round-nearest-even_convert_fusion.1), channel_id=1, source_target_pairs={{0,16},{4,20},{8,24},{12,28},{1,17},{5,21},{9,25},{13,29},{2,18},{... | collective-permute-start | bytes 393224 | tf_op jit(solution)/shard_map/ppermute | solution.py:26
  25.8 1.7 %collective-permute-done.3.refs_1_ = s16[128,512]{1,0:T(8,128)(2,1)S(1)} collective-permute-done((s16[128,512]{1,0:T(8,128)(2,1)S(1)}, s16[128,512]{1,0:T(8,128)(2,1)S(1)}, u32[]{:S(2)}, u32[]{:S(2)}) %collective-permute-start.3) | collective-permute-done | bytes 131104 | tf_op jit(solution)/shard_map/ppermute | solution.py:26
  28.2 1.2 %convert_add_fusion.mine_ref = f32[256,512]{1,0:T(8,128)S(1)} fusion(bf16[256,512]{1,0:T(8,128)(2,1)} %collective-permute-done.6, bf16[256,512]{1,0:T(8,128)(2,1)} %collective-permute-done.5, f32[256,512]{1,0:T(8,128)S(1)} %get-tuple-element.39, bf16[256,512]{1,0:T(8,128)(2,1)} %collective-permute-done.4), kind=kLoop, calls=%fused_computation.1 | loop fusion | flops 786432 | bytes 1835008 | tf_op jit(solution)/shard_map/add | solution.py:253
  29.6 1.1 %constant_dynamic-slice_fusion.5.kept_ref = bf16[2,256,512]{2,1,0:T(8,128)(2,1)S(1)} fusion(bf16[2,512,512]{2,1,0:T(8,128)(2,1)} %param.9, s32[]{:T(128)S(6)} %select_n.71), kind=kLoop, calls=%fused_computation.63 | loop fusion | bytes 1048580 | tf_op jit(solution)/shard_map/dynamic_slice | solution.py:206
  30.7 5.3 %collective-permute-start.8 = (s16[128,512]{1,0:T(8,128)(2,1)}, s16[128,512]{1,0:T(8,128)(2,1)S(1)}, u32[]{:S(2)}, u32[]{:S(2)}) collective-permute-start(s16[128,512]{1,0:T(8,128)(2,1)} %round-nearest-even_convert_fusion), channel_id=1, source_target_pairs={{0,16},{4,20},{8,24},{12,28},{1,17},{5,21},{9,25},{13,29},{2,18},{... | collective-permute-start | bytes 393224 | tf_op jit(solution)/shard_map/ppermute | solution.py:26
  38.5 1.7 %values.2 = (f32[512,128]{1,0:T(8,128)S(1)}, bf16[512,128]{1,0:T(8,128)(2,1)S(1)}, bf16[512,128]{1,0:T(8,128)(2,1)S(1)}, bf16[512,128]{1,0:T(8,128)(2,1)S(1)}) custom-call(s32[2]{0:T(128)S(1)} %copy-done.5, f32[5,512]{1,0:T(8,128)S(1)} %stack.35.par_ref, bf16[2,256,512]{2,1,0:T(8,128)(2,1)S(1)} %constant_dynamic-slice_fusion.5.kept_ref, ...), custom_call_target="tpu_custom_call" | custom-call | flops 536870912 | bytes 2097152 | tf_op jit(solution)/shard_map/values/pallas_call | solution.py:161
  40.2 1.6 %collective-permute-start.10 = (bf16[512,128]{1,0:T(8,128)(2,1)S(1)}, bf16[512,128]{1,0:T(8,128)(2,1)}, u32[]{:S(2)}, u32[]{:S(2)}) collective-permute-start(bf16[512,128]{1,0:T(8,128)(2,1)S(1)} %get-tuple-element.53), channel_id=1, source_target_pairs={{0,2},{1,3},{2,0},{3,1},{4,6},{5,7},{6,4},{7,5},{8,10},{9,11},{10,... | collective-permute-start | bytes 393224 | tf_op jit(solution)/shard_map/ppermute | solution.py:32
  41.8 1.4 %collective-permute-start.11 = (bf16[512,128]{1,0:T(8,128)(2,1)S(1)}, bf16[512,128]{1,0:T(8,128)(2,1)}, u32[]{:S(2)}, u32[]{:S(2)}) collective-permute-start(bf16[512,128]{1,0:T(8,128)(2,1)S(1)} %get-tuple-element.54), channel_id=1, source_target_pairs={{0,3},{1,2},{2,1},{3,0},{4,7},{5,6},{6,5},{7,4},{8,11},{9,10},{10,... | collective-permute-start | bytes 393224 | tf_op jit(solution)/shard_map/ppermute | solution.py:32
  45.1 1.7 %values.3 = (f32[512,128]{1,0:T(8,128)S(1)}, bf16[512,128]{1,0:T(8,128)(2,1)S(1)}, bf16[512,128]{1,0:T(8,128)(2,1)S(1)}, bf16[512,128]{1,0:T(8,128)(2,1)S(1)}) custom-call(s32[2]{0:T(128)S(1)} %copy-done.6, f32[5,512]{1,0:T(8,128)S(1)} %stack.35.par_ref, bf16[2,256,512]{2,1,0:T(8,128)(2,1)S(1)} %constant_dynamic-slice_fusion.5.kept_ref, ...), custom_call_target="tpu_custom_call" | custom-call | flops 536870912 | bytes 2097152 | tf_op jit(solution)/shard_map/values/pallas_call | solution.py:161
  46.7 1.6 %collective-permute-start.13 = (bf16[512,128]{1,0:T(8,128)(2,1)S(1)}, bf16[512,128]{1,0:T(8,128)(2,1)S(1)}, u32[]{:S(2)}, u32[]{:S(2)}) collective-permute-start(bf16[512,128]{1,0:T(8,128)(2,1)S(1)} %get-tuple-element.56), channel_id=1, source_target_pairs={{0,1},{1,0},{2,3},{3,2},{4,5},{5,4},{6,7},{7,6},{8,9},{9,8},{10,11... | collective-permute-start | bytes 393224 | tf_op jit(solution)/shard_map/ppermute | solution.py:32
  48.3 1.5 %collective-permute-start.14 = (bf16[512,128]{1,0:T(8,128)(2,1)S(1)}, bf16[512,128]{1,0:T(8,128)(2,1)S(1)}, u32[]{:S(2)}, u32[]{:S(2)}) collective-permute-start(bf16[512,128]{1,0:T(8,128)(2,1)S(1)} %get-tuple-element.57), channel_id=1, source_target_pairs={{0,2},{1,3},{2,0},{3,1},{4,6},{5,7},{6,4},{7,5},{8,10},{9,11},{10,... | collective-permute-start | bytes 393224 | tf_op jit(solution)/shard_map/ppermute | solution.py:32
  49.8 1.4 %collective-permute-start.15 = (bf16[512,128]{1,0:T(8,128)(2,1)S(1)}, bf16[512,128]{1,0:T(8,128)(2,1)S(1)}, u32[]{:S(2)}, u32[]{:S(2)}) collective-permute-start(bf16[512,128]{1,0:T(8,128)(2,1)S(1)} %get-tuple-element.58), channel_id=1, source_target_pairs={{0,3},{1,2},{2,1},{3,0},{4,7},{5,6},{6,5},{7,4},{8,11},{9,10},{10,... | collective-permute-start | bytes 393224 | tf_op jit(solution)/shard_map/ppermute | solution.py:32
  51.2 1.1 %convert_add_fusion.6 = f32[512,128]{1,0:T(8,128)S(1)} fusion(bf16[512,128]{1,0:T(8,128)(2,1)} %collective-permute-done.11, bf16[512,128]{1,0:T(8,128)(2,1)} %collective-permute-done.10, f32[512,128]{1,0:T(8,128)S(1)} %get-tuple-element.51, bf16[512,128]{1,0:T(8,128)(2,1)} %collective-permute-done.9), kind=kLoop, calls=%fused_computation.39 | loop fusion | flops 393216 | bytes 917504 | tf_op jit(solution)/shard_map/add | solution.py:269
  52.3 5.4 %collective-permute-start.12 = (bf16[2,128,128]{2,1,0:T(8,128)(2,1)S(1)}, bf16[2,128,128]{2,1,0:T(8,128)(2,1)S(1)}, u32[]{:S(2)}, u32[]{:S(2)}) collective-permute-start(bf16[2,128,128]{2,1,0:T(8,128)(2,1)S(1)} %bitcast.60), channel_id=1, source_target_pairs={{0,8},{4,12},{8,16},{12,20},{16,24},{20,28},{1,9},{5,13},{9,17},{1... | collective-permute-start | bytes 196616 | tf_op jit(solution)/shard_map/ppermute | solution.py:26
  57.8 1.8 %collective-permute-done.12 = bf16[2,128,128]{2,1,0:T(8,128)(2,1)S(1)} collective-permute-done((bf16[2,128,128]{2,1,0:T(8,128)(2,1)S(1)}, bf16[2,128,128]{2,1,0:T(8,128)(2,1)S(1)}, u32[]{:S(2)}, u32[]{:S(2)}) %collective-permute-start.12) | collective-permute-done | bytes 65568 | tf_op jit(solution)/shard_map/ppermute | solution.py:26
  60.5 4.3 %collective-permute-start.16 = (bf16[2,128,128]{2,1,0:T(8,128)(2,1)S(1)}, bf16[2,128,128]{2,1,0:T(8,128)(2,1)S(1)}, u32[]{:S(2)}, u32[]{:S(2)}) collective-permute-start(bf16[2,128,128]{2,1,0:T(8,128)(2,1)S(1)} %bitcast.61), channel_id=1, source_target_pairs={{0,8},{4,12},{8,16},{12,20},{16,24},{20,28},{1,9},{5,13},{9,17},{1... | collective-permute-start | bytes 196616 | tf_op jit(solution)/shard_map/ppermute | solution.py:26
  64.8 1.8 %collective-permute-done.16 = bf16[2,128,128]{2,1,0:T(8,128)(2,1)S(1)} collective-permute-done((bf16[2,128,128]{2,1,0:T(8,128)(2,1)S(1)}, bf16[2,128,128]{2,1,0:T(8,128)(2,1)S(1)}, u32[]{:S(2)}, u32[]{:S(2)}) %collective-permute-start.16) | collective-permute-done | bytes 65568 | tf_op jit(solution)/shard_map/ppermute | solution.py:26
  (75 shorter events, 11.1 us)
Async XLA Ops:
  0.6 12.1 %copy-start.8 = (bf16[2,512,512]{2,1,0:T(8,128)(2,1)S(1)}, bf16[2,512,512]{2,1,0:T(8,128)(2,1)}, u32[]{:S(2)}) copy-start(bf16[2,512,512]{2,1,0:T(8,128)(2,1)} %param.9) | copy-start | bytes 3145732
  0.6 12.1 %copy-start.9 = (f32[512]{0:T(512)S(1)}, f32[512]{0:T(512)}, u32[]{:S(2)}) copy-start(f32[512]{0:T(512)} %param.10) | copy-start | bytes 6148
  1.8 10.9 %collective-permute-start = (bf16[2,256,512]{2,1,0:T(8,128)(2,1)S(1)}, bf16[2,256,512]{2,1,0:T(8,128)(2,1)S(1)}, u32[]{:S(2)}, u32[]{:S(2)}) collective-permute-start(bf16[2,256,512]{2,1,0:T(8,128)(2,1)S(1)} %constant_dynamic-slice_fusion.6), channel_id=1, source_target_pairs={{0,4},{4,0},{8,12},{12,8},{16,20},{20,16},{24,28},{28,24},{1,5},{5... | collective-permute-start | bytes 1572872 | tf_op jit(solution)/shard_map/ppermute | solution.py:20
  6.0 23.6 %copy-start.12 = (f32[512]{0:T(512)S(1)}, f32[512]{0:T(512)}, u32[]{:S(2)}) copy-start(f32[512]{0:T(512)} %param.12) | copy-start | bytes 6148
  8.6 19.6 %collective-permute-start.4 = (bf16[256,512]{1,0:T(8,128)(2,1)S(1)}, bf16[256,512]{1,0:T(8,128)(2,1)}, u32[]{:S(2)}, u32[]{:S(2)}) collective-permute-start(bf16[256,512]{1,0:T(8,128)(2,1)S(1)} %get-tuple-element.40), channel_id=1, source_target_pairs={{0,1},{1,0},{2,3},{3,2},{4,5},{5,4},{6,7},{7,6},{8,9},{9,8},{10,11... | collective-permute-start | bytes 786440 | tf_op jit(solution)/shard_map/ppermute | solution.py:32
  11.2 17.0 %collective-permute-start.5 = (bf16[256,512]{1,0:T(8,128)(2,1)S(1)}, bf16[256,512]{1,0:T(8,128)(2,1)}, u32[]{:S(2)}, u32[]{:S(2)}) collective-permute-start(bf16[256,512]{1,0:T(8,128)(2,1)S(1)} %get-tuple-element.41), channel_id=1, source_target_pairs={{0,2},{1,3},{2,0},{3,1},{4,6},{5,7},{6,4},{7,5},{8,10},{9,11},{10,... | collective-permute-start | bytes 786440 | tf_op jit(solution)/shard_map/ppermute | solution.py:32
  12.7 15.5 %collective-permute-start.6 = (bf16[256,512]{1,0:T(8,128)(2,1)S(1)}, bf16[256,512]{1,0:T(8,128)(2,1)}, u32[]{:S(2)}, u32[]{:S(2)}) collective-permute-start(bf16[256,512]{1,0:T(8,128)(2,1)S(1)} %get-tuple-element.42), channel_id=1, source_target_pairs={{0,3},{1,2},{2,1},{3,0},{4,7},{5,6},{6,5},{7,4},{8,11},{9,10},{10,... | collective-permute-start | bytes 786440 | tf_op jit(solution)/shard_map/ppermute | solution.py:32
  13.1 7.5 %collective-permute-start.2 = (s16[128,512]{1,0:T(8,128)(2,1)S(1)}, s16[128,512]{1,0:T(8,128)(2,1)S(1)}, u32[]{:S(2)}, u32[]{:S(2)}) collective-permute-start(s16[128,512]{1,0:T(8,128)(2,1)S(1)} %round-nearest-even_convert_fusion.3), channel_id=1, source_target_pairs={{0,8},{4,12},{8,16},{12,20},{16,24},{20,28},{1,9},{5,13},{9,17},{1... | collective-permute-start | bytes 393224 | tf_op jit(solution)/shard_map/ppermute | solution.py:26
  17.1 8.0 %collective-permute-start.1 = (s16[128,512]{1,0:T(8,128)(2,1)S(1)}, s16[128,512]{1,0:T(8,128)(2,1)S(1)}, u32[]{:S(2)}, u32[]{:S(2)}) collective-permute-start(s16[128,512]{1,0:T(8,128)(2,1)S(1)} %round-nearest-even_convert_fusion.2), channel_id=1, source_target_pairs={{0,8},{4,12},{8,16},{12,20},{16,24},{20,28},{1,9},{5,13},{9,17},{1... | collective-permute-start | bytes 393224 | tf_op jit(solution)/shard_map/ppermute | solution.py:26
  20.7 6.9 %collective-permute-start.3 = (s16[128,512]{1,0:T(8,128)(2,1)S(1)}, s16[128,512]{1,0:T(8,128)(2,1)S(1)}, u32[]{:S(2)}, u32[]{:S(2)}) collective-permute-start(s16[128,512]{1,0:T(8,128)(2,1)S(1)} %round-nearest-even_convert_fusion.1), channel_id=1, source_target_pairs={{0,16},{4,20},{8,24},{12,28},{1,17},{5,21},{9,25},{13,29},{2,18},{... | collective-permute-start | bytes 393224 | tf_op jit(solution)/shard_map/ppermute | solution.py:26
  29.5 6.6 %collective-permute-start.7 = (f32[256,512]{1,0:T(8,128)S(1)}, f32[256,512]{1,0:T(8,128)S(1)}, u32[]{:S(2)}, u32[]{:S(2)}) collective-permute-start(f32[256,512]{1,0:T(8,128)S(1)} %convert_add_fusion.mine_ref), channel_id=1, source_target_pairs={{0,4},{4,0},{8,12},{12,8},{16,20},{20,16},{24,28},{28,24},{1,5},{5... | collective-permute-start | bytes 1572872 | tf_op jit(solution)/shard_map/ppermute | solution.py:20
  30.7 13.7 %collective-permute-start.8 = (s16[128,512]{1,0:T(8,128)(2,1)}, s16[128,512]{1,0:T(8,128)(2,1)S(1)}, u32[]{:S(2)}, u32[]{:S(2)}) collective-permute-start(s16[128,512]{1,0:T(8,128)(2,1)} %round-nearest-even_convert_fusion), channel_id=1, source_target_pairs={{0,16},{4,20},{8,24},{12,28},{1,17},{5,21},{9,25},{13,29},{2,18},{... | collective-permute-start | bytes 393224 | tf_op jit(solution)/shard_map/ppermute | solution.py:26
  40.2 26.4 %copy-start.11 = (f32[128]{0:T(128)S(1)}, f32[128]{0:T(128)}, u32[]{:S(2)}) copy-start(f32[128]{0:T(128)} %param.16) | copy-start | bytes 1540
  40.2 9.6 %collective-permute-start.10 = (bf16[512,128]{1,0:T(8,128)(2,1)S(1)}, bf16[512,128]{1,0:T(8,128)(2,1)}, u32[]{:S(2)}, u32[]{:S(2)}) collective-permute-start(bf16[512,128]{1,0:T(8,128)(2,1)S(1)} %get-tuple-element.53), channel_id=1, source_target_pairs={{0,2},{1,3},{2,0},{3,1},{4,6},{5,7},{6,4},{7,5},{8,10},{9,11},{10,... | collective-permute-start | bytes 393224 | tf_op jit(solution)/shard_map/ppermute | solution.py:32
  41.8 9.4 %collective-permute-start.11 = (bf16[512,128]{1,0:T(8,128)(2,1)S(1)}, bf16[512,128]{1,0:T(8,128)(2,1)}, u32[]{:S(2)}, u32[]{:S(2)}) collective-permute-start(bf16[512,128]{1,0:T(8,128)(2,1)S(1)} %get-tuple-element.54), channel_id=1, source_target_pairs={{0,3},{1,2},{2,1},{3,0},{4,7},{5,6},{6,5},{7,4},{8,11},{9,10},{10,... | collective-permute-start | bytes 393224 | tf_op jit(solution)/shard_map/ppermute | solution.py:32
  43.2 8.0 %collective-permute-start.9 = (bf16[512,128]{1,0:T(8,128)(2,1)S(1)}, bf16[512,128]{1,0:T(8,128)(2,1)}, u32[]{:S(2)}, u32[]{:S(2)}) collective-permute-start(bf16[512,128]{1,0:T(8,128)(2,1)S(1)} %get-tuple-element.52), channel_id=1, source_target_pairs={{0,1},{1,0},{2,3},{3,2},{4,5},{5,4},{6,7},{7,6},{8,9},{9,8},{10,11... | collective-permute-start | bytes 393224 | tf_op jit(solution)/shard_map/ppermute | solution.py:32
  46.7 13.6 %collective-permute-start.13 = (bf16[512,128]{1,0:T(8,128)(2,1)S(1)}, bf16[512,128]{1,0:T(8,128)(2,1)S(1)}, u32[]{:S(2)}, u32[]{:S(2)}) collective-permute-start(bf16[512,128]{1,0:T(8,128)(2,1)S(1)} %get-tuple-element.56), channel_id=1, source_target_pairs={{0,1},{1,0},{2,3},{3,2},{4,5},{5,4},{6,7},{7,6},{8,9},{9,8},{10,11... | collective-permute-start | bytes 393224 | tf_op jit(solution)/shard_map/ppermute | solution.py:32
  48.3 12.0 %collective-permute-start.14 = (bf16[512,128]{1,0:T(8,128)(2,1)S(1)}, bf16[512,128]{1,0:T(8,128)(2,1)S(1)}, u32[]{:S(2)}, u32[]{:S(2)}) collective-permute-start(bf16[512,128]{1,0:T(8,128)(2,1)S(1)} %get-tuple-element.57), channel_id=1, source_target_pairs={{0,2},{1,3},{2,0},{3,1},{4,6},{5,7},{6,4},{7,5},{8,10},{9,11},{10,... | collective-permute-start | bytes 393224 | tf_op jit(solution)/shard_map/ppermute | solution.py:32
  49.8 10.5 %collective-permute-start.15 = (bf16[512,128]{1,0:T(8,128)(2,1)S(1)}, bf16[512,128]{1,0:T(8,128)(2,1)S(1)}, u32[]{:S(2)}, u32[]{:S(2)}) collective-permute-start(bf16[512,128]{1,0:T(8,128)(2,1)S(1)} %get-tuple-element.58), channel_id=1, source_target_pairs={{0,3},{1,2},{2,1},{3,0},{4,7},{5,6},{6,5},{7,4},{8,11},{9,10},{10,... | collective-permute-start | bytes 393224 | tf_op jit(solution)/shard_map/ppermute | solution.py:32
  52.3 7.3 %collective-permute-start.12 = (bf16[2,128,128]{2,1,0:T(8,128)(2,1)S(1)}, bf16[2,128,128]{2,1,0:T(8,128)(2,1)S(1)}, u32[]{:S(2)}, u32[]{:S(2)}) collective-permute-start(bf16[2,128,128]{2,1,0:T(8,128)(2,1)S(1)} %bitcast.60), channel_id=1, source_target_pairs={{0,8},{4,12},{8,16},{12,20},{16,24},{20,28},{1,9},{5,13},{9,17},{1... | collective-permute-start | bytes 196616 | tf_op jit(solution)/shard_map/ppermute | solution.py:26
  57.8 9.1 %collective-permute-start.17 = (f32[2,128,128]{2,1,0:T(8,128)S(1)}, f32[2,128,128]{2,1,0:T(8,128)S(1)}, u32[]{:S(2)}, u32[]{:S(2)}) collective-permute-start(f32[2,128,128]{2,1,0:T(8,128)S(1)} %get-tuple-element.71), channel_id=1, source_target_pairs={{0,4},{4,0},{8,12},{12,8},{16,20},{20,16},{24,28},{28,24},{1,5},{5... | collective-permute-start | bytes 393224 | tf_op jit(solution)/shard_map/ppermute | solution.py:20
  60.5 6.2 %collective-permute-start.16 = (bf16[2,128,128]{2,1,0:T(8,128)(2,1)S(1)}, bf16[2,128,128]{2,1,0:T(8,128)(2,1)S(1)}, u32[]{:S(2)}, u32[]{:S(2)}) collective-permute-start(bf16[2,128,128]{2,1,0:T(8,128)(2,1)S(1)} %bitcast.61), channel_id=1, source_target_pairs={{0,8},{4,12},{8,16},{12,20},{16,24},{20,28},{1,9},{5,13},{9,17},{1... | collective-permute-start | bytes 196616 | tf_op jit(solution)/shard_map/ppermute | solution.py:26
  64.8 2.1 %collective-permute-start.18 = (f32[2,128,128]{2,1,0:T(8,128)S(1)}, f32[2,128,128]{2,1,0:T(8,128)S(1)}, u32[]{:S(2)}, u32[]{:S(2)}) collective-permute-start(f32[2,128,128]{2,1,0:T(8,128)S(1)} %constant_dynamic-slice_fusion.2), channel_id=1, source_target_pairs={{0,4},{4,0},{8,12},{12,8},{16,20},{20,16},{24,28},{28,24},{1,5},{5... | collective-permute-start | bytes 393224 | tf_op jit(solution)/shard_map/ppermute | solution.py:20
  66.7 1.2 %collective-permute-start.19 = (f32[2,128]{1,0:T(2,128)S(1)}, f32[2,128]{1,0:T(2,128)S(1)}, u32[]{:S(2)}, u32[]{:S(2)}) collective-permute-start(f32[2,128]{1,0:T(2,128)S(1)} %constant_dynamic-slice_fusion.1), channel_id=1, source_target_pairs={{0,4},{4,0},{8,12},{12,8},{16,20},{20,16},{24,28},{28,24},{1,5},{5... | collective-permute-start | bytes 3080 | tf_op jit(solution)/shard_map/ppermute | solution.py:20
  (9 other events, 24.7 us)

commit v3 on v1

v3 whole, which is shorter than its diff:
```python
import functools

import jax
import jax.numpy as jnp
from jax import lax
from jax.experimental import pallas as pl
from jax.experimental.pallas import tpu as pltpu
from jax.sharding import PartitionSpec as P

SETS = 512
CORES = 2
SHOCK = 6.0
TOP = 32760.0
MIB = 1 << 20
TURNED = (((1,), (1,)), ((), ()))


def swap(block):
    n = lax.axis_size("date")
    return lax.ppermute(block, "date", [(i, i ^ 1) for i in range(n)])


def across(block, chips):
    n = lax.axis_size("date")
    hop = CORES * chips
    return lax.ppermute(block, "date", [(i, i ^ hop) for i in range(n)])


def later(block):
    n = lax.axis_size("date")
    return lax.ppermute(block, "date", [(i, i + CORES) for i in range(n - CORES)])


def exchange(slots):
    n = len(slots)
    return [
        lax.ppermute(slots[i], "book", [(j, j ^ i) for j in range(n)])
        for i in range(1, n)
    ]


def weights_kernel(books, per, here_ref, owner_ref, sets_ref, flows_hbm, *refs):
    outs, total, flows, sems = refs[:books], refs[books], refs[books + 1], refs[books + 2]
    core, me = here_ref[0], here_ref[1]
    half = outs[0].shape[0]
    blocks, rows = sets_ref.shape
    sets_here = SETS // books
    size = per * rows
    copies = []
    for step in range(blocks // per):
        at = pl.ds(step * size, size)
        copies.append(pltpu.make_async_copy(flows_hbm.at[at], flows.at[at], sems.at[step]))
        copies[-1].start()
    total[...] = jnp.zeros_like(total)
    row = lax.broadcasted_iota(jnp.int32, (half, rows), 0) + core * half
    for b in range(blocks):
        if b % per == 0:
            copies[b // per].wait()
        owner = owner_ref[b]
        name = sets_ref[b : b + 1, :]
        name = ((name // sets_here) ^ owner) * sets_here + name % sets_here
        hot = jnp.where(name == row, 1.0, 0.0).astype(jnp.bfloat16)
        part = jnp.dot(
            hot, flows[b * rows : (b + 1) * rows, :], preferred_element_type=jnp.float32
        )
        slot = owner ^ me
        total[slot] = total[slot] + part
    for i in range(books):
        outs[i][...] = total[i].astype(outs[i].dtype)


def weights(here, owners, trade_set, cashflows, books):
    blocks = owners.shape[0]
    trades, width = cashflows.shape
    per = 4 if blocks % 4 == 0 else 1
    half = SETS // CORES
    whole = pl.BlockSpec(memory_space=pltpu.VMEM)
    scalars = pl.BlockSpec(memory_space=pltpu.SMEM)
    return pl.pallas_call(
        functools.partial(weights_kernel, books, per),
        in_specs=[scalars, scalars, whole, pl.BlockSpec(memory_space=pltpu.HBM)],
        out_specs=[whole] * books,
        scratch_shapes=[
            pltpu.VMEM((books, half, width), jnp.float32),
            pltpu.VMEM((trades, width), jnp.bfloat16),
            pltpu.SemaphoreType.DMA((blocks // per,)),
        ],
        out_shape=[
            jax.ShapeDtypeStruct((half, width), jnp.bfloat16 if i else jnp.float32)
            for i in range(books)
        ],
        compiler_params=pltpu.CompilerParams(vmem_limit_bytes=24 * MIB),
        cost_estimate=pl.CostEstimate(
            flops=2 * trades * half * width, bytes_accessed=2 * trades * width, transcendentals=0
        ),
        name="weights",
    )(here, owners, trade_set.reshape(blocks, trades // blocks), cashflows)


def price_rows(books, disc, high_ref, low_ref, outs):
    sets_here = SETS // books
    rows = 256
    for r in range(disc.shape[0] // rows):
        price = disc[r * rows : (r + 1) * rows, :]
        part = lax.dot_general(price, high_ref[...], TURNED, preferred_element_type=jnp.float32)
        part = part + lax.dot_general(price, low_ref[...], TURNED, preferred_element_type=jnp.float32)
        for i in range(books):
            outs[i][r * rows : (r + 1) * rows, :] = part[:, i * sets_here : (i + 1) * sets_here].astype(
                outs[i].dtype
            )


def late_kernel(books, here_ref, par_ref, kept_ref, got_ref, start_ref, *refs):
    sources, outs, (early, high, low, late) = refs[:4], refs[4 : 4 + books], refs[4 + books :]
    core = here_ref[0]
    dates, paths, _ = kept_ref.shape
    half = sources[0].shape[0]
    tile = 32
    for i, source in enumerate(sources):
        place = core if i < 2 else 1 - core
        target = low if i % 2 else high
        target[pl.ds(pl.multiple_of(place * half, half), half), :] = source[...]

    def walk(i, _):
        at = pl.ds(i * tile, tile)
        pers, vol, base = par_ref[0:1, :], par_ref[1:2, :], par_ref[2:3, :]
        state = start_ref[at, :]
        for t in range(2 * dates):
            kept = kept_ref[t % dates, at, :].astype(jnp.float32)
            got = got_ref[t % dates, at, :].astype(jnp.float32)
            shock = jnp.where(core == 0, kept, got) if t < dates else jnp.where(core == 0, got, kept)
            state = pers * state + vol * shock
            disc = early if t < dates else late
            disc[pl.ds((t % dates) * paths + i * tile, tile), :] = jnp.exp(-(base + state)).astype(jnp.bfloat16)
        return 0

    lax.fori_loop(0, paths // tile, walk, 0)
    price_rows(books, late, high, low, outs)


def late_values(here, par, kept, got, start, mats, books):
    dates, paths, width = kept.shape
    rows = dates * paths
    whole = pl.BlockSpec(memory_space=pltpu.VMEM)
    *pieces, early, high, low = pl.pallas_call(
        functools.partial(late_kernel, books),
        in_specs=[pl.BlockSpec(memory_space=pltpu.SMEM)] + [whole] * 8,
        out_specs=[whole] * (books + 3),
        out_shape=[
            jax.ShapeDtypeStruct((rows, SETS // books), jnp.bfloat16 if i else jnp.float32)
            for i in range(books)
        ]
        + [jax.ShapeDtypeStruct((rows, width), jnp.bfloat16)]
        + [jax.ShapeDtypeStruct((SETS, width), jnp.bfloat16)] * 2,
        scratch_shapes=[pltpu.VMEM((rows, width), jnp.bfloat16)],
        compiler_params=pltpu.CompilerParams(vmem_limit_bytes=16 * MIB),
        cost_estimate=pl.CostEstimate(
            flops=4 * rows * SETS * width, bytes_accessed=2 * MIB, transcendentals=2 * rows * width
        ),
        name="late_values",
    )(here, par, kept, got, start, *mats)
    return pieces, (early, high, low)


def early_kernel(books, early_ref, high_ref, low_ref, *outs):
    price_rows(books, early_ref, high_ref, low_ref, outs)


def early_values(early, high, low, books):
    rows, width = early.shape
    whole = pl.BlockSpec(memory_space=pltpu.VMEM)
    return pl.pallas_call(
        functools.partial(early_kernel, books),
        in_specs=[whole] * 3,
        out_specs=[whole] * books,
        out_shape=[
            jax.ShapeDtypeStruct((rows, SETS // books), jnp.bfloat16 if i else jnp.float32)
            for i in range(books)
        ],
        compiler_params=pltpu.CompilerParams(vmem_limit_bytes=12 * MIB),
        cost_estimate=pl.CostEstimate(
            flops=4 * rows * SETS * width, bytes_accessed=2 * MIB, transcendentals=0
        ),
        name="early_values",
    )(early, high, low)


def after(array, *others):
    return lax.optimization_barrier((array,) + others)[0]


def on_device(
    shocks,
    persistence,
    volatility,
    base_rate,
    cashflows,
    block_owner,
    trade_set,
    threshold,
    margin_lag,
):
    dates, paths, width = shocks.shape
    books = lax.axis_size("book")
    chips = lax.axis_size("date") // CORES
    me = lax.axis_index("book")
    core = lax.axis_index("date") % CORES
    chip = lax.axis_index("date") // CORES
    here = jnp.stack([core, me]).astype(jnp.int32)
    half = paths // CORES
    span = CORES * dates
    sets_here = SETS // books

    def side(array, which, axis):
        size = array.shape[axis] // CORES
        return lax.dynamic_slice_in_dim(array, which * size, size, axis)

    sent = side(shocks, 1 - core, 1)
    got = swap(sent)
    kept = side(after(shocks, sent), core, 1)

    power = [jnp.ones_like(persistence)]
    for _ in range(span * chips):
        power.append(power[-1] * persistence)

    def own_sum(array):
        total = array[0].astype(jnp.float32)
        for t in range(1, dates):
            total = persistence * total + array[t].astype(jnp.float32)
        return total

    weigh_kept = volatility * jnp.where(core == 0, power[dates], power[0])
    weigh_got = volatility * jnp.where(core == 0, power[0], power[dates])
    group = weigh_kept * own_sum(kept) + weigh_got * own_sum(got)

    codes, rates = [], []
    reach, inside = 1, power[0]
    while reach < chips:
        bound = SHOCK * volatility * sum(power[: reach * span])
        code = jnp.round(group * (TOP / bound)).astype(jnp.int16)
        if reach == 1:
            mats = weights(after(here, code), block_owner[:, 0], trade_set, cashflows, books)
            mats_arrived = exchange(mats)
        came = across(code, reach)
        odd = (chip // reach) % 2 == 1
        fall = power[reach * span]
        rates.append(jnp.where(odd, inside, 0.0) * (bound / TOP))
        codes.append(came)
        came = after(came, mats[0]).astype(jnp.float32) * (bound / TOP)
        group = jnp.where(odd, power[0], fall) * group + jnp.where(odd, fall, power[0]) * came
        inside = inside * jnp.where(odd, fall, power[0])
        reach *= 2

    mine = after(mats[0], code)
    for arrived in mats_arrived:
        mine = mine + arrived.astype(jnp.float32)
    high = mine.astype(jnp.bfloat16)
    low = (mine - high.astype(jnp.float32)).astype(jnp.bfloat16)
    start = jnp.zeros((half, width), jnp.float32)
    for came, rate in zip(codes, rates):
        start = start + rate * came.astype(jnp.float32)

    par = jnp.stack([persistence, volatility, base_rate])
    late_pieces, rest = late_values(here, par, kept, got, start, [high, low, swap(high), swap(low)], books)
    late_arrived = exchange(late_pieces)
    early_pieces = early_values(*rest, books)
    early_arrived = exchange(early_pieces)

    def gathered(piece, others):
        net = piece
        for arrived in others:
            net = net + arrived.astype(jnp.float32)
        return net.reshape(dates, half, sets_here)

    late_net = gathered(after(late_pieces[0], early_pieces[0]), late_arrived)
    before = later(late_net.astype(jnp.bfloat16))
    early_net = gathered(after(early_pieces[0], late_net), early_arrived)
    net_got = swap(jnp.where(core == 0, late_net, early_net))
    net_kept = jnp.where(core == 0, early_net, late_net)

    joined = jnp.concatenate([before.astype(jnp.float32), early_net, late_net], 0)
    now = joined[dates:]
    collateral = jnp.zeros_like(now)
    for lag in range(1, dates + 1):
        collateral = jnp.where(
            margin_lag[None, None, :] == lag, joined[dates - lag : dates - lag + span], collateral
        )
    exposed = jnp.sum(jnp.maximum(now - collateral - threshold[None, None, :], 0.0), axis=1)
    exposed_got = swap(side(exposed, 1 - core, 0))
    net_kept = after(net_kept, exposed)
    net_value = jnp.concatenate(
        [jnp.where(core == 0, net_kept, net_got), jnp.where(core == 0, net_got, net_kept)], 1
    )
    net_value, exposed_got = lax.optimization_barrier((net_value, exposed_got))
    return (net_value, (side(exposed, core, 0) + exposed_got) / paths)


def solution(mesh):
    return jax.shard_map(
        on_device,
        mesh=mesh,
        in_specs=(
            P("date", None, "book"),
            P("book"),
            P("book"),
            P("book"),
            P("book", None),
            P("book", None),
            P("book"),
            P("book"),
            P("book"),
        ),
        out_specs=(P("date", None, "book"), P("date", "book")),
        check_vma=False,
    )
```

time: 59.3 us -> 53.1 us (0.90)
  waiting for transfers between devices: 23.3 us -> 15 us
  local copies, waits for them, and re-layouts: 3.36 us -> 4.8 us
  Pallas kernels: 4.58 us -> 5.75 us
  other arithmetic: 5.66 us -> 4.62 us
  starting transfers between devices: 20.7 us -> 21.7 us
    ppermute x6 -> x9, waiting for transfers between devices: 17.8 us -> 11.5 us  [exchange(): lax.ppermute(slots[i], 'book', [(j, j ^ i) for j in range(n)])]
    ppermute x6 -> x9, starting transfers between devices: 7.11 us -> 12.6 us  [exchange(): lax.ppermute(slots[i], 'book', [(j, j ^ i) for j in range(n)])]
    ppermute x3, starting transfers between devices: 12.8 us -> 7.36 us  [the longest x2 5.66 us: across(): return lax.ppermute(block, 'date', [(i, i ^ hop) for i in range(n)])]
    ppermute x4 -> x5, waiting for transfers between devices: 3.14 us -> 1.61 us  [swap(): return lax.ppermute(block, 'date', [(i, i ^ 1) for i in range(n)])]
    pallas_call x2 -> x3, Pallas kernels: 4.58 us -> 5.75 us  [the longest x1 2.87 us: weights(): pl.pallas_call(functools.partial(weights_kernel, books, per), in_specs=[s...]
    select_n x1 -> x2, other arithmetic: 1.24 us -> 0.09 us  [the longest x1 0.06 us: on_device(): net_kept = jnp.where(core == 0, early_net, late_net)]
    ppermute x4 -> x5, starting transfers between devices: 0.73 us -> 1.71 us  [swap(): return lax.ppermute(block, 'date', [(i, i ^ 1) for i in range(n)])]
    reshape x0 -> x1, local copies, waits for them, and re-layouts: none -> 0.72 us  [weights(): trade_set.reshape(blocks, trades // blocks)]
  transfers between devices with their start and end apart: 13 -> 17, of which waited for: 9 -> 8; matrix products, arithmetic and copies ran while one was open for 4% -> 7% of each run, Pallas kernels for 4% -> 7%
where the time goes in v3:
time: 53.1 us; the launch traced here: 52.8 us
  starting transfers between devices  21.7 us (41%)
  waiting for transfers between devices  15 us (28%)
  Pallas kernels  5.75 us (11%)
  local copies, waits for them, and re-layouts  4.8 us (9%)
  other arithmetic  4.62 us (9%)
  between operations  0.86 us (2%)
    ppermute x9, starting transfers between devices, exchange(): lax.ppermute(slots[i], 'book', [(j, j ^ i) for j in range(n)])  12.6 us
    ppermute x9, waiting for transfers between devices, exchange(): lax.ppermute(slots[i], 'book', [(j, j ^ i) for j in range(n)])  11.5 us
    ppermute x2, starting transfers between devices, across(): return lax.ppermute(block, 'date', [(i, i ^ hop) for i in range(n)])  5.66 us
    unnamed x16, local copies, waits for them, and re-layouts  2.87 us
    pallas_call x1, Pallas kernels, weights(): pl.pallas_call(functools.partial(weights_kernel, books, per), in_specs=[s...  2.87 us
    pallas_call x1, Pallas kernels, late_values(): pl.pallas_call(functools.partial(late_kernel, books), in_specs=[pl.BlockS...  2.14 us
    ppermute x2, waiting for transfers between devices, across(): return lax.ppermute(block, 'date', [(i, i ^ hop) for i in range(n)])  1.94 us
    convert_element_type x2, other arithmetic, on_device(): code = jnp.round(group * (TOP / bound)).astype(jnp.int16)  1.71 us
  transfers between devices with their start and end apart: 17, of which 8 were waited for; matrix products, arithmetic and copies ran while one was open for 7% of the time, Pallas kernels for 7%

profile of v3, /device:TPU:0, one launch (start us, length us, event | category | flops | bytes accessed | tf_op | source)
XLA Modules:
  0.0 52.8 jit_solution(12236266943091306071)
XLA Ops:
  0.7 1.2 %constant_dynamic-slice_fusion.3 = bf16[2,256,512]{2,1,0:T(8,128)(2,1)S(1)} fusion(bf16[2,512,512]{2,1,0:T(8,128)(2,1)} %param.9, s32[]{:T(128)S(6)} %select_n.101), kind=kLoop, calls=%fused_computation.49 | loop fusion | bytes 1048580 | tf_op jit(solution)/shard_map/dynamic_slice | solution.py:216
  3.1 0.8 %collective-permute-done.got_ref = bf16[2,256,512]{2,1,0:T(8,128)(2,1)S(1)} collective-permute-done((bf16[2,256,512]{2,1,0:T(8,128)(2,1)S(1)}, bf16[2,256,512]{2,1,0:T(8,128)(2,1)S(1)}, u32[]{:S(2)}, u32[]{:S(2)}) %collective-permute-start) | collective-permute-done | bytes 524320 | tf_op jit(solution)/shard_map/ppermute | solution.py:20
  3.9 1.3 %round-nearest-even_convert_fusion.1 = s16[256,512]{1,0:T(8,128)(2,1)S(1)} fusion(f32[512]{0:T(512)S(1)} %get-tuple-element.62, bf16[2,256,512]{2,1,0:T(8,128)(2,1)S(1)} %collective-permute-done.got_ref, f32[512]{0:T(512)S(1)} %get-tuple-element.68, bf16[2,512,512]{2,1,0:T(8,128)(2,1)} %param.9, s32[]{:T(128)S(6)} %add.119, s32[]{:T(128)S(6)} %select_n.102, ...), kind=kLoop, calls=%fused_computation.20 | loop fusion | flops 1835008 | bytes 1318920 | tf_op jit(solution)/shard_map/convert_element_type | solution.py:240
  5.2 3.0 %collective-permute-start.1 = (s16[256,512]{1,0:T(8,128)(2,1)S(1)}, s16[256,512]{1,0:T(8,128)(2,1)S(1)}, u32[]{:S(2)}, u32[]{:S(2)}) collective-permute-start(s16[256,512]{1,0:T(8,128)(2,1)S(1)} %round-nearest-even_convert_fusion.1), channel_id=1, source_target_pairs={{0,8},{4,12},{8,0},{12,4},{16,24},{20,28},{24,16},{28,20},{1,9},{5... | collective-permute-start | bytes 786440 | tf_op jit(solution)/shard_map/ppermute | solution.py:26
  8.3 0.7 %reshape.36.sets_ref = s32[16,256]{1,0:T(8,128)S(1)} reshape(s32[4096]{0:T(1024)} %param.15) | data formatting | bytes 32768 | tf_op jit(solution)/shard_map/reshape | solution.py:97
  9.0 2.2 %copy-done = bf16[4096,512]{1,0:T(8,128)(2,1)S(1)} copy-done((bf16[4096,512]{1,0:T(8,128)(2,1)S(1)}, bf16[4096,512]{1,0:T(8,128)(2,1)}, u32[]{:S(2)}) %copy-start) | copy-done | bytes 4194328
  11.9 2.9 %weights.1 = (f32[256,512]{1,0:T(8,128)S(1)}, bf16[256,512]{1,0:T(8,128)(2,1)S(1)}, bf16[256,512]{1,0:T(8,128)(2,1)S(1)}, bf16[256,512]{1,0:T(8,128)(2,1)S(1)}) custom-call(s32[2]{0:T(128)S(1)} %pad_add_fusion.here_ref, s32[16]{0:T(128)S(1)} %bitcast.49, s32[16,256]{1,0:T(8,128)S(1)} %reshape.36.sets_ref, bf16[4096,512]{1,0:T(8,128)(2,1)S(1)} %copy-done), custom_call_target="tpu_custom_call" | custom-call | flops 1073741824 | bytes 4194304 | tf_op jit(solution)/shard_map/weights/pallas_call | solution.py:79
  14.7 1.6 %collective-permute-start.3 = (bf16[256,512]{1,0:T(8,128)(2,1)S(1)}, bf16[256,512]{1,0:T(8,128)(2,1)S(1)}, u32[]{:S(2)}, u32[]{:S(2)}) collective-permute-start(bf16[256,512]{1,0:T(8,128)(2,1)S(1)} %get-tuple-element.31), channel_id=1, source_target_pairs={{0,1},{1,0},{2,3},{3,2},{4,5},{5,4},{6,7},{7,6},{8,9},{9,8},{10,11... | collective-permute-start | bytes 786440 | tf_op jit(solution)/shard_map/ppermute | solution.py:37
  16.3 1.5 %collective-permute-start.4 = (bf16[256,512]{1,0:T(8,128)(2,1)S(1)}, bf16[256,512]{1,0:T(8,128)(2,1)S(1)}, u32[]{:S(2)}, u32[]{:S(2)}) collective-permute-start(bf16[256,512]{1,0:T(8,128)(2,1)S(1)} %get-tuple-element.32), channel_id=1, source_target_pairs={{0,2},{1,3},{2,0},{3,1},{4,6},{5,7},{6,4},{7,5},{8,10},{9,11},{10,... | collective-permute-start | bytes 786440 | tf_op jit(solution)/shard_map/ppermute | solution.py:37
  18.8 2.7 %collective-permute-start.2 = (s16[256,512]{1,0:T(8,128)(2,1)S(1)}, s16[256,512]{1,0:T(8,128)(2,1)S(1)}, u32[]{:S(2)}, u32[]{:S(2)}) collective-permute-start(s16[256,512]{1,0:T(8,128)(2,1)S(1)} %round-nearest-even_convert_fusion), channel_id=1, source_target_pairs={{0,16},{4,20},{8,24},{12,28},{16,0},{20,4},{24,8},{28,12},{1,17},{... | collective-permute-start | bytes 786440 | tf_op jit(solution)/shard_map/ppermute | solution.py:26
  21.4 2.6 %collective-permute-done.3 = bf16[256,512]{1,0:T(8,128)(2,1)S(1)} collective-permute-done((bf16[256,512]{1,0:T(8,128)(2,1)S(1)}, bf16[256,512]{1,0:T(8,128)(2,1)S(1)}, u32[]{:S(2)}, u32[]{:S(2)}) %collective-permute-start.3) | collective-permute-done | bytes 262176 | tf_op jit(solution)/shard_map/ppermute | solution.py:37
  24.0 5.7 %collective-permute-done.4 = bf16[256,512]{1,0:T(8,128)(2,1)S(1)} collective-permute-done((bf16[256,512]{1,0:T(8,128)(2,1)S(1)}, bf16[256,512]{1,0:T(8,128)(2,1)S(1)}, u32[]{:S(2)}, u32[]{:S(2)}) %collective-permute-start.4) | collective-permute-done | bytes 262176 | tf_op jit(solution)/shard_map/ppermute | solution.py:37
  30.5 1.9 %collective-permute-done.2 = s16[256,512]{1,0:T(8,128)(2,1)S(1)} collective-permute-done((s16[256,512]{1,0:T(8,128)(2,1)S(1)}, s16[256,512]{1,0:T(8,128)(2,1)S(1)}, u32[]{:S(2)}, u32[]{:S(2)}) %collective-permute-start.2) | collective-permute-done | bytes 262176 | tf_op jit(solution)/shard_map/ppermute | solution.py:26
  32.6 2.1 %late_values.1 = (f32[512,128]{1,0:T(8,128)S(1)}, bf16[512,128]{1,0:T(8,128)(2,1)S(1)}, bf16[512,128]{1,0:T(8,128)(2,1)S(1)}, bf16[512,128]{1,0:T(8,128)(2,1)S(1...) custom-call(s32[2]{0:T(128)S(1)} %pad_add_fusion.here_ref, ...), custom_call_target="tpu_custom_call" | custom-call | flops 536870912 | bytes 2097152 | tf_op jit(solution)/shard_map/late_values/pallas_call | solution.py:145
  34.8 2.6 %collective-permute-start.10 = (bf16[512,128]{1,0:T(8,128)(2,1)S(1)}, bf16[512,128]{1,0:T(8,128)(2,1)S(1)}, u32[]{:S(2)}, u32[]{:S(2)}) collective-permute-start(bf16[512,128]{1,0:T(8,128)(2,1)S(1)} %get-tuple-element.42), channel_id=1, source_target_pairs={{0,3},{1,2},{2,1},{3,0},{4,7},{5,6},{6,5},{7,4},{8,11},{9,10},{10,... | collective-permute-start | bytes 393224 | tf_op jit(solution)/shard_map/ppermute | solution.py:37
  38.4 0.7 %early_values.1 = (f32[512,128]{1,0:T(8,128)S(1)}, bf16[512,128]{1,0:T(8,128)(2,1)S(1)}, bf16[512,128]{1,0:T(8,128)(2,1)S(1)}, bf16[512,128]{1,0:T(8,128)(2,1)S(1)}) custom-call(bf16[512,512]{1,0:T(8,128)(2,1)S(1)} %get-tuple-element.34.early_ref, bf16[512,512]{1,0:T(8,128)(2,1)S(1)} %get-tuple-element.35.high_ref, ...), custom_call_target="tpu_custom_call" | custom-call | flops 536870912 | bytes 2097152 | tf_op jit(solution)/shard_map/early_values/pallas_call | solution.py:172
  39.1 1.6 %collective-permute-start.11 = (bf16[512,128]{1,0:T(8,128)(2,1)S(1)}, bf16[512,128]{1,0:T(8,128)(2,1)S(1)}, u32[]{:S(2)}, u32[]{:S(2)}) collective-permute-start(bf16[512,128]{1,0:T(8,128)(2,1)S(1)} %get-tuple-element.44), channel_id=1, source_target_pairs={{0,1},{1,0},{2,3},{3,2},{4,5},{5,4},{6,7},{7,6},{8,9},{9,8},{10,11... | collective-permute-start | bytes 393224 | tf_op jit(solution)/shard_map/ppermute | solution.py:37
  40.7 1.5 %collective-permute-start.12 = (bf16[512,128]{1,0:T(8,128)(2,1)S(1)}, bf16[512,128]{1,0:T(8,128)(2,1)S(1)}, u32[]{:S(2)}, u32[]{:S(2)}) collective-permute-start(bf16[512,128]{1,0:T(8,128)(2,1)S(1)} %get-tuple-element.45), channel_id=1, source_target_pairs={{0,2},{1,3},{2,0},{3,1},{4,6},{5,7},{6,4},{7,5},{8,10},{9,11},{10,... | collective-permute-start | bytes 393224 | tf_op jit(solution)/shard_map/ppermute | solution.py:37
  42.2 2.4 %collective-permute-start.13 = (bf16[512,128]{1,0:T(8,128)(2,1)S(1)}, bf16[512,128]{1,0:T(8,128)(2,1)S(1)}, u32[]{:S(2)}, u32[]{:S(2)}) collective-permute-start(bf16[512,128]{1,0:T(8,128)(2,1)S(1)} %get-tuple-element.46), channel_id=1, source_target_pairs={{0,3},{1,2},{2,1},{3,0},{4,7},{5,6},{6,5},{7,4},{8,11},{9,10},{10,... | collective-permute-start | bytes 393224 | tf_op jit(solution)/shard_map/ppermute | solution.py:37
  45.1 1.7 %collective-permute-start.14 = (bf16[2,256,128]{2,1,0:T(8,128)(2,1)S(1)}, bf16[2,256,128]{2,1,0:T(8,128)(2,1)S(1)}, u32[]{:S(2)}, u32[]{:S(2)}) collective-permute-start(bf16[2,256,128]{2,1,0:T(8,128)(2,1)S(1)} %get-tuple-element.50), channel_id=1, source_target_pairs={{0,8},{4,12},{8,16},{12,20},{16,24},{20,28},{1,9},{5,13},{9,17},{1... | collective-permute-start | bytes 393224 | tf_op jit(solution)/shard_map/ppermute | solution.py:31
  46.8 1.0 %collective-permute-done.11 = bf16[512,128]{1,0:T(8,128)(2,1)S(1)} collective-permute-done((bf16[512,128]{1,0:T(8,128)(2,1)S(1)}, bf16[512,128]{1,0:T(8,128)(2,1)S(1)}, u32[]{:S(2)}, u32[]{:S(2)}) %collective-permute-start.11) | collective-permute-done | bytes 131104 | tf_op jit(solution)/shard_map/ppermute | solution.py:37
  47.9 1.8 %collective-permute-done.13 = bf16[512,128]{1,0:T(8,128)(2,1)S(1)} collective-permute-done((bf16[512,128]{1,0:T(8,128)(2,1)S(1)}, bf16[512,128]{1,0:T(8,128)(2,1)S(1)}, u32[]{:S(2)}, u32[]{:S(2)}) %collective-permute-start.13) | collective-permute-done | bytes 131104 | tf_op jit(solution)/shard_map/ppermute | solution.py:37
  50.5 0.8 %collective-permute-done.15 = f32[2,256,128]{2,1,0:T(8,128)S(1)} collective-permute-done((f32[2,256,128]{2,1,0:T(8,128)S(1)}, f32[2,256,128]{2,1,0:T(8,128)S(1)}, u32[]{:S(2)}, u32[]{:S(2)}) %collective-permute-start.15) | collective-permute-done | bytes 262176 | tf_op jit(solution)/shard_map/ppermute | solution.py:20
  51.4 0.8 %pad_maximum_fusion.2 = f32[2,512,128]{2,1,0:T(8,128)} fusion(f32[2,256,128]{2,1,0:T(8,128)S(1)} %get-tuple-element.60, f32[2,256,128]{2,1,0:T(8,128)S(1)} %get-tuple-element.59), kind=kLoop, calls=%fused_computation.8 | loop fusion | flops 131072 | bytes 1048576 | tf_op jit(solution)/shard_map/concatenate | solution.py:291
  (50 shorter events, 6.8 us)
Async XLA Ops:
  0.6 17.7 %copy-start.2 = (bf16[2,512,512]{2,1,0:T(8,128)(2,1)S(1)}, bf16[2,512,512]{2,1,0:T(8,128)(2,1)}, u32[]{:S(2)}) copy-start(bf16[2,512,512]{2,1,0:T(8,128)(2,1)} %param.9) | copy-start | bytes 3145732
  0.6 17.7 %copy-start.3 = (f32[512]{0:T(512)S(1)}, f32[512]{0:T(512)}, u32[]{:S(2)}) copy-start(f32[512]{0:T(512)} %param.10) | copy-start | bytes 6148
  1.8 2.1 %collective-permute-start = (bf16[2,256,512]{2,1,0:T(8,128)(2,1)S(1)}, bf16[2,256,512]{2,1,0:T(8,128)(2,1)S(1)}, u32[]{:S(2)}, u32[]{:S(2)}) collective-permute-start(bf16[2,256,512]{2,1,0:T(8,128)(2,1)S(1)} %constant_dynamic-slice_fusion.3), channel_id=1, source_target_pairs={{0,4},{4,0},{8,12},{12,8},{16,20},{20,16},{24,28},{28,24},{1,5},{5... | collective-permute-start | bytes 1572872 | tf_op jit(solution)/shard_map/ppermute | solution.py:20
  5.2 13.1 %collective-permute-start.1 = (s16[256,512]{1,0:T(8,128)(2,1)S(1)}, s16[256,512]{1,0:T(8,128)(2,1)S(1)}, u32[]{:S(2)}, u32[]{:S(2)}) collective-permute-start(s16[256,512]{1,0:T(8,128)(2,1)S(1)} %round-nearest-even_convert_fusion.1), channel_id=1, source_target_pairs={{0,8},{4,12},{8,0},{12,4},{16,24},{20,28},{24,16},{28,20},{1,9},{5... | collective-permute-start | bytes 786440 | tf_op jit(solution)/shard_map/ppermute | solution.py:26
  9.0 2.2 %copy-start = (bf16[4096,512]{1,0:T(8,128)(2,1)S(1)}, bf16[4096,512]{1,0:T(8,128)(2,1)}, u32[]{:S(2)}) copy-start(bf16[4096,512]{1,0:T(8,128)(2,1)} %flows_hbm.1) | copy-start | bytes 12582916
  11.8 18.6 %copy-start.4 = (f32[512]{0:T(512)S(1)}, f32[512]{0:T(512)}, u32[]{:S(2)}) copy-start(f32[512]{0:T(512)} %param.11) | copy-start | bytes 6148
  11.9 18.6 %copy-start.5 = (f32[512]{0:T(512)S(1)}, f32[512]{0:T(512)}, u32[]{:S(2)}) copy-start(f32[512]{0:T(512)} %param.12) | copy-start | bytes 6148
  14.7 23.6 %copy-start.7 = (s32[128]{0:T(128)S(1)}, s32[128]{0:T(128)}, u32[]{:S(2)}) copy-start(s32[128]{0:T(128)} %param.17) | copy-start | bytes 1540
  14.7 9.3 %collective-permute-start.3 = (bf16[256,512]{1,0:T(8,128)(2,1)S(1)}, bf16[256,512]{1,0:T(8,128)(2,1)S(1)}, u32[]{:S(2)}, u32[]{:S(2)}) collective-permute-start(bf16[256,512]{1,0:T(8,128)(2,1)S(1)} %get-tuple-element.31), channel_id=1, source_target_pairs={{0,1},{1,0},{2,3},{3,2},{4,5},{5,4},{6,7},{7,6},{8,9},{9,8},{10,11... | collective-permute-start | bytes 786440 | tf_op jit(solution)/shard_map/ppermute | solution.py:37
  16.3 13.4 %collective-permute-start.4 = (bf16[256,512]{1,0:T(8,128)(2,1)S(1)}, bf16[256,512]{1,0:T(8,128)(2,1)S(1)}, u32[]{:S(2)}, u32[]{:S(2)}) collective-permute-start(bf16[256,512]{1,0:T(8,128)(2,1)S(1)} %get-tuple-element.32), channel_id=1, source_target_pairs={{0,2},{1,3},{2,0},{3,1},{4,6},{5,7},{6,4},{7,5},{8,10},{9,11},{10,... | collective-permute-start | bytes 786440 | tf_op jit(solution)/shard_map/ppermute | solution.py:37
  17.8 11.9 %collective-permute-start.5 = (bf16[256,512]{1,0:T(8,128)(2,1)S(1)}, bf16[256,512]{1,0:T(8,128)(2,1)S(1)}, u32[]{:S(2)}, u32[]{:S(2)}) collective-permute-start(bf16[256,512]{1,0:T(8,128)(2,1)S(1)} %get-tuple-element.33), channel_id=1, source_target_pairs={{0,3},{1,2},{2,1},{3,0},{4,7},{5,6},{6,5},{7,4},{8,11},{9,10},{10,... | collective-permute-start | bytes 786440 | tf_op jit(solution)/shard_map/ppermute | solution.py:37
  18.8 13.6 %collective-permute-start.2 = (s16[256,512]{1,0:T(8,128)(2,1)S(1)}, s16[256,512]{1,0:T(8,128)(2,1)S(1)}, u32[]{:S(2)}, u32[]{:S(2)}) collective-permute-start(s16[256,512]{1,0:T(8,128)(2,1)S(1)} %round-nearest-even_convert_fusion), channel_id=1, source_target_pairs={{0,16},{4,20},{8,24},{12,28},{16,0},{20,4},{24,8},{28,12},{1,17},{... | collective-permute-start | bytes 786440 | tf_op jit(solution)/shard_map/ppermute | solution.py:26
  29.9 2.7 %collective-permute-start.6 = (bf16[256,512]{1,0:T(8,128)(2,1)S(1)}, bf16[256,512]{1,0:T(8,128)(2,1)S(1)}, u32[]{:S(2)}, u32[]{:S(2)}) collective-permute-start(bf16[256,512]{1,0:T(8,128)(2,1)S(1)} %get-tuple-element.58.refs_0_), channel_id=1, source_target_pairs={{0,4},{4,0},{8,12},{12,8},{16,20},{20,16},{24,28},{28,24},{1,5},{5... | collective-permute-start | bytes 786440 | tf_op jit(solution)/shard_map/ppermute | solution.py:20
  30.0 2.7 %collective-permute-start.7 = (bf16[256,512]{1,0:T(8,128)(2,1)S(1)}, bf16[256,512]{1,0:T(8,128)(2,1)S(1)}, u32[]{:S(2)}, u32[]{:S(2)}) collective-permute-start(bf16[256,512]{1,0:T(8,128)(2,1)S(1)} %get-tuple-element.57.refs_1_), channel_id=1, source_target_pairs={{0,4},{4,0},{8,12},{12,8},{16,20},{20,16},{24,28},{28,24},{1,5},{5... | collective-permute-start | bytes 786440 | tf_op jit(solution)/shard_map/ppermute | solution.py:20
  32.6 17.2 %copy-start.6 = (f32[128]{0:T(128)S(1)}, f32[128]{0:T(128)}, u32[]{:S(2)}) copy-start(f32[128]{0:T(128)} %param.16) | copy-start | bytes 1540
  34.8 7.4 %collective-permute-start.10 = (bf16[512,128]{1,0:T(8,128)(2,1)S(1)}, bf16[512,128]{1,0:T(8,128)(2,1)S(1)}, u32[]{:S(2)}, u32[]{:S(2)}) collective-permute-start(bf16[512,128]{1,0:T(8,128)(2,1)S(1)} %get-tuple-element.42), channel_id=1, source_target_pairs={{0,3},{1,2},{2,1},{3,0},{4,7},{5,6},{6,5},{7,4},{8,11},{9,10},{10,... | collective-permute-start | bytes 393224 | tf_op jit(solution)/shard_map/ppermute | solution.py:37
  37.4 7.7 %collective-permute-start.8 = (bf16[512,128]{1,0:T(8,128)(2,1)S(1)}, bf16[512,128]{1,0:T(8,128)(2,1)S(1)}, u32[]{:S(2)}, u32[]{:S(2)}) collective-permute-start(bf16[512,128]{1,0:T(8,128)(2,1)S(1)} %get-tuple-element.40), channel_id=1, source_target_pairs={{0,1},{1,0},{2,3},{3,2},{4,5},{5,4},{6,7},{7,6},{8,9},{9,8},{10,11... | collective-permute-start | bytes 393224 | tf_op jit(solution)/shard_map/ppermute | solution.py:37
  37.9 7.1 %collective-permute-start.9 = (bf16[512,128]{1,0:T(8,128)(2,1)S(1)}, bf16[512,128]{1,0:T(8,128)(2,1)S(1)}, u32[]{:S(2)}, u32[]{:S(2)}) collective-permute-start(bf16[512,128]{1,0:T(8,128)(2,1)S(1)} %get-tuple-element.41), channel_id=1, source_target_pairs={{0,2},{1,3},{2,0},{3,1},{4,6},{5,7},{6,4},{7,5},{8,10},{9,11},{10,... | collective-permute-start | bytes 393224 | tf_op jit(solution)/shard_map/ppermute | solution.py:37
  39.1 8.7 %collective-permute-start.11 = (bf16[512,128]{1,0:T(8,128)(2,1)S(1)}, bf16[512,128]{1,0:T(8,128)(2,1)S(1)}, u32[]{:S(2)}, u32[]{:S(2)}) collective-permute-start(bf16[512,128]{1,0:T(8,128)(2,1)S(1)} %get-tuple-element.44), channel_id=1, source_target_pairs={{0,1},{1,0},{2,3},{3,2},{4,5},{5,4},{6,7},{7,6},{8,9},{9,8},{10,11... | collective-permute-start | bytes 393224 | tf_op jit(solution)/shard_map/ppermute | solution.py:37
  40.7 7.1 %collective-permute-start.12 = (bf16[512,128]{1,0:T(8,128)(2,1)S(1)}, bf16[512,128]{1,0:T(8,128)(2,1)S(1)}, u32[]{:S(2)}, u32[]{:S(2)}) collective-permute-start(bf16[512,128]{1,0:T(8,128)(2,1)S(1)} %get-tuple-element.45), channel_id=1, source_target_pairs={{0,2},{1,3},{2,0},{3,1},{4,6},{5,7},{6,4},{7,5},{8,10},{9,11},{10,... | collective-permute-start | bytes 393224 | tf_op jit(solution)/shard_map/ppermute | solution.py:37
  42.2 7.4 %collective-permute-start.13 = (bf16[512,128]{1,0:T(8,128)(2,1)S(1)}, bf16[512,128]{1,0:T(8,128)(2,1)S(1)}, u32[]{:S(2)}, u32[]{:S(2)}) collective-permute-start(bf16[512,128]{1,0:T(8,128)(2,1)S(1)} %get-tuple-element.46), channel_id=1, source_target_pairs={{0,3},{1,2},{2,1},{3,0},{4,7},{5,6},{6,5},{7,4},{8,11},{9,10},{10,... | collective-permute-start | bytes 393224 | tf_op jit(solution)/shard_map/ppermute | solution.py:37
  45.1 4.7 %collective-permute-start.14 = (bf16[2,256,128]{2,1,0:T(8,128)(2,1)S(1)}, bf16[2,256,128]{2,1,0:T(8,128)(2,1)S(1)}, u32[]{:S(2)}, u32[]{:S(2)}) collective-permute-start(bf16[2,256,128]{2,1,0:T(8,128)(2,1)S(1)} %get-tuple-element.50), channel_id=1, source_target_pairs={{0,8},{4,12},{8,16},{12,20},{16,24},{20,28},{1,9},{5,13},{9,17},{1... | collective-permute-start | bytes 393224 | tf_op jit(solution)/shard_map/ppermute | solution.py:31
  49.7 1.6 %collective-permute-start.15 = (f32[2,256,128]{2,1,0:T(8,128)S(1)}, f32[2,256,128]{2,1,0:T(8,128)S(1)}, u32[]{:S(2)}, u32[]{:S(2)}) collective-permute-start(f32[2,256,128]{2,1,0:T(8,128)S(1)} %broadcast_select_fusion.2), channel_id=1, source_target_pairs={{0,4},{4,0},{8,12},{12,8},{16,20},{20,16},{24,28},{28,24},{1,5},{5... | collective-permute-start | bytes 786440 | tf_op jit(solution)/shard_map/ppermute | solution.py:20
  50.0 2.2 %collective-permute-start.16 = (f32[2,128]{1,0:T(2,128)S(1)}, f32[2,128]{1,0:T(2,128)S(1)}, u32[]{:S(2)}, u32[]{:S(2)}) collective-permute-start(f32[2,128]{1,0:T(2,128)S(1)} %constant_dynamic-slice_fusion.1), channel_id=1, source_target_pairs={{0,4},{4,0},{8,12},{12,8},{16,20},{20,16},{24,28},{28,24},{1,5},{5... | collective-permute-start | bytes 3080 | tf_op jit(solution)/shard_map/ppermute | solution.py:20
  (1 other events, 0.7 us)

commit v4 on v3

--- a/solution.py
+++ b/solution.py
@@ -94,7 +94,12 @@
             flops=2 * trades * half * width, bytes_accessed=2 * trades * width, transcendentals=0
         ),
         name="weights",
-    )(here, owners, trade_set.reshape(blocks, trades // blocks), cashflows)
+    )(
+        here,
+        pltpu.with_memory_space_constraint(owners, pltpu.HBM),
+        trade_set.reshape(blocks, trades // blocks),
+        pltpu.with_memory_space_constraint(cashflows, pltpu.HBM),
+    )
 
 
 def price_rows(books, disc, high_ref, low_ref, outs):
@@ -110,8 +115,8 @@
             )
 
 
-def late_kernel(books, here_ref, par_ref, kept_ref, got_ref, start_ref, *refs):
-    sources, outs, (early, high, low, late) = refs[:4], refs[4 : 4 + books], refs[4 + books :]
+def values_kernel(books, here_ref, par_ref, kept_ref, got_ref, start_ref, *refs):
+    sources, outs, (disc, high, low) = refs[:4], refs[4:-3], refs[-3:]
     core = here_ref[0]
     dates, paths, _ = kept_ref.shape
     half = sources[0].shape[0]
@@ -130,59 +135,98 @@
             got = got_ref[t % dates, at, :].astype(jnp.float32)
             shock = jnp.where(core == 0, kept, got) if t < dates else jnp.where(core == 0, got, kept)
             state = pers * state + vol * shock
-            disc = early if t < dates else late
-            disc[pl.ds((t % dates) * paths + i * tile, tile), :] = jnp.exp(-(base + state)).astype(jnp.bfloat16)
+            disc[pl.ds(t * paths + i * tile, tile), :] = jnp.exp(-(base + state)).astype(jnp.bfloat16)
         return 0
 
     lax.fori_loop(0, paths // tile, walk, 0)
-    price_rows(books, late, high, low, outs)
-
-
-def late_values(here, par, kept, got, start, mats, books):
+    rows = dates * paths
+    price_rows(books, disc.at[rows:], high, low, outs[:books])
+    price_rows(books, disc.at[:rows], high, low, outs[books:])
+
+
+def values(here, par, kept, got, start, mats, books):
     dates, paths, width = kept.shape
     rows = dates * paths
     whole = pl.BlockSpec(memory_space=pltpu.VMEM)
-    *pieces, early, high, low = pl.pallas_call(
-        functools.partial(late_kernel, books),
+    pieces = pl.pallas_call(
+        functools.partial(values_kernel, books),
         in_specs=[pl.BlockSpec(memory_space=pltpu.SMEM)] + [whole] * 8,
-        out_specs=[whole] * (books + 3),
+        out_specs=[whole] * (2 * books),
         out_shape=[
             jax.ShapeDtypeStruct((rows, SETS // books), jnp.bfloat16 if i else jnp.float32)
             for i in range(books)
         ]
-        + [jax.ShapeDtypeStruct((rows, width), jnp.bfloat16)]
-        + [jax.ShapeDtypeStruct((SETS, width), jnp.bfloat16)] * 2,
-        scratch_shapes=[pltpu.VMEM((rows, width), jnp.bfloat16)],
+        * 2,
+        scratch_shapes=[pltpu.VMEM((2 * rows, width), jnp.bfloat16)]
+        + [pltpu.VMEM((SETS, width), jnp.bfloat16)] * 2,
         compiler_params=pltpu.CompilerParams(vmem_limit_bytes=16 * MIB),
         cost_estimate=pl.CostEstimate(
-            flops=4 * rows * SETS * width, bytes_accessed=2 * MIB, transcendentals=2 * rows * width
+            flops=8 * rows * SETS * width, bytes_accessed=2 * MIB, transcendentals=2 * rows * width
         ),
-        name="late_values",
+        name="values",
     )(here, par, kept, got, start, *mats)
-    return pieces, (early, high, low)
-
-
-def early_kernel(books, early_ref, high_ref, low_ref, *outs):
-    price_rows(books, early_ref, high_ref, low_ref, outs)
-
-
-def early_values(early, high, low, books):
-    rows, width = early.shape
+    return pieces[:books], pieces[books:]
+
+
+def code_kernel(chips, here_ref, par_ref, kept_ref, got_ref, code_ref, group_ref, rows_ref):
+    core, chip = here_ref[0], here_ref[2]
+    dates, paths, _ = kept_ref.shape
+    pers, vol = par_ref[0:1, :], par_ref[1:2, :]
+    one = jnp.ones_like(pers)
+    span = CORES * dates
+    fall, block, reach = one, jnp.zeros_like(pers), 1
+    for _ in range(span):
+        block = block + fall
+        fall = fall * pers
+    inside, count = one, 0
+    while reach < chips:
+        bound = SHOCK * vol * block
+        odd = (chip // reach) % 2 == 1
+        rows_ref[4 * count : 4 * count + 1, :] = TOP / bound
+        rows_ref[4 * count + 1 : 4 * count + 2, :] = jnp.where(odd, inside, 0.0) * (bound / TOP)
+        rows_ref[4 * count + 2 : 4 * count + 3, :] = jnp.where(odd, one, fall)
+        rows_ref[4 * count + 3 : 4 * count + 4, :] = jnp.where(odd, fall, one) * (bound / TOP)
+        inside = inside * jnp.where(odd, fall, one)
+        block = block + fall * block
+        fall = fall * fall
+        reach, count = 2 * reach, count + 1
+    tile = 32
+    scale = rows_ref[0:1, :]
+
+    def walk(i, _):
+        at = pl.ds(i * tile, tile)
+        state = jnp.zeros((tile, pers.shape[1]), jnp.float32)
+        for t in range(2 * dates):
+            kept = kept_ref[t % dates, at, :].astype(jnp.float32)
+            got = got_ref[t % dates, at, :].astype(jnp.float32)
+            shock = jnp.where(core == 0, kept, got) if t < dates else jnp.where(core == 0, got, kept)
+            state = pers * state + vol * shock
+        group_ref[at, :] = state
+        code_ref[at, :] = jnp.round(state * scale).astype(jnp.int16)
+        return 0
+
+    lax.fori_loop(0, paths // tile, walk, 0)
+
+
+def first_code(here, par, kept, got, chips):
+    dates, paths, width = kept.shape
     whole = pl.BlockSpec(memory_space=pltpu.VMEM)
+    rounds = max(1, (chips - 1).bit_length())
     return pl.pallas_call(
-        functools.partial(early_kernel, books),
-        in_specs=[whole] * 3,
-        out_specs=[whole] * books,
+        functools.partial(code_kernel, chips),
+        in_specs=[pl.BlockSpec(memory_space=pltpu.SMEM)] + [whole] * 3,
+        out_specs=[whole] * 3,
         out_shape=[
-            jax.ShapeDtypeStruct((rows, SETS // books), jnp.bfloat16 if i else jnp.float32)
-            for i in range(books)
+            jax.ShapeDtypeStruct((paths, width), jnp.int16),
+            jax.ShapeDtypeStruct((paths, width), jnp.float32),
+            jax.ShapeDtypeStruct((4 * rounds, width), jnp.float32),
         ],
-        compiler_params=pltpu.CompilerParams(vmem_limit_bytes=12 * MIB),
+        compiler_params=pltpu.CompilerParams(vmem_limit_bytes=8 * MIB),
         cost_estimate=pl.CostEstimate(
-            flops=4 * rows * SETS * width, bytes_accessed=2 * MIB, transcendentals=0
+            flops=16 * paths * width, bytes_accessed=2 * MIB, transcendentals=0
         ),
-        name="early_values",
-    )(early, high, low)
+        name="first_code",
+    )(here, par, kept, got)
 
 
 def after(array, *others):
@@ -206,7 +250,7 @@
     me = lax.axis_index("book")
     core = lax.axis_index("date") % CORES
     chip = lax.axis_index("date") // CORES
-    here = jnp.stack([core, me]).astype(jnp.int32)
+    here = jnp.stack([core, me, chip]).astype(jnp.int32)
     half = paths // CORES
     span = CORES * dates
     sets_here = SETS // books
@@ -215,55 +259,36 @@
         size = array.shape[axis] // CORES
         return lax.dynamic_slice_in_dim(array, which * size, size, axis)
 
-    sent = side(shocks, 1 - core, 1)
+    par = jnp.stack([persistence, volatility, base_rate])
+    sent = side(after(shocks, par), 1 - core, 1)
     got = swap(sent)
     kept = side(after(shocks, sent), core, 1)
 
-    power = [jnp.ones_like(persistence)]
-    for _ in range(span * chips):
-        power.append(power[-1] * persistence)
-
-    def own_sum(array):
-        total = array[0].astype(jnp.float32)
-        for t in range(1, dates):
-            total = persistence * total + array[t].astype(jnp.float32)
-        return total
-
-    weigh_kept = volatility * jnp.where(core == 0, power[dates], power[0])
-    weigh_got = volatility * jnp.where(core == 0, power[0], power[dates])
-    group = weigh_kept * own_sum(kept) + weigh_got * own_sum(got)
-
-    codes, rates = [], []
-    reach, inside = 1, power[0]
+    code, group, table = first_code(here, par, kept, got, chips)
+    start = jnp.zeros((half, width), jnp.float32)
+    reach, count = 1, 0
     while reach < chips:
-        bound = SHOCK * volatility * sum(power[: reach * span])
-        code = jnp.round(group * (TOP / bound)).astype(jnp.int16)
-        if reach == 1:
+        scale, rate, ours, theirs = (table[4 * count + i] for i in range(4))
+        if count:
+            code = jnp.round(group * scale).astype(jnp.int16)
+        else:
             mats = weights(after(here, code), block_owner[:, 0], trade_set, cashflows, books)
             mats_arrived = exchange(mats)
         came = across(code, reach)
-        odd = (chip // reach) % 2 == 1
-        fall = power[reach * span]
-        rates.append(jnp.where(odd, inside, 0.0) * (bound / TOP))
-        codes.append(came)
-        came = after(came, mats[0]).astype(jnp.float32) * (bound / TOP)
-        group = jnp.where(odd, power[0], fall) * group + jnp.where(odd, fall, power[0]) * came
-        inside = inside * jnp.where(odd, fall, power[0])
-        reach *= 2
+        start = start + rate * came.astype(jnp.float32)
+        group = ours * group + theirs * after(came, mats[0]).astype(jnp.float32)
+        reach, count = 2 * reach, count + 1
 
     mine = after(mats[0], code)
     for arrived in mats_arrived:
         mine = mine + arrived.astype(jnp.float32)
-    high = mine.astype(jnp.bfloat16)
-    low = (mine - high.astype(jnp.float32)).astype(jnp.bfloat16)
-    start = jnp.zeros((half, width), jnp.float32)
-    for came, rate in zip(codes, rates):
-        start = start + rate * came.astype(jnp.float32)
-
-    par = jnp.stack([persistence, volatility, base_rate])
-    late_pieces, rest = late_values(here, par, kept, got, start, [high, low, swap(high), swap(low)], books)
+    rounded = lax.reduce_precision(mine, 8, 7)
+    high, low = rounded.astype(jnp.bfloat16), (mine - rounded).astype(jnp.bfloat16)
+
+    late_pieces, early_pieces = values(
+        here, par, kept, got, start, [high, low, swap(high), swap(low)], books
+    )
     late_arrived = exchange(late_pieces)
-    early_pieces = early_values(*rest, books)
     early_arrived = exchange(early_pieces)
 
     def gathered(piece, others):
@@ -272,7 +297,7 @@
             net = net + arrived.astype(jnp.float32)
         return net.reshape(dates, half, sets_here)
 
-    late_net = gathered(after(late_pieces[0], early_pieces[0]), late_arrived)
+    late_net = gathered(late_pieces[0], late_arrived)
     before = later(late_net.astype(jnp.bfloat16))
     early_net = gathered(after(early_pieces[0], late_net), early_arrived)
     net_got = swap(jnp.where(core == 0, late_net, early_net))

time: 53.1 us -> 52.2 us (0.983)
  local copies, waits for them, and re-layouts: 4.8 us -> 1.25 us
  Pallas kernels: 5.75 us -> 7.45 us
    unnamed x16 -> x6, local copies, waits for them, and re-layouts: 2.87 us -> 0.44 us
    dynamic_slice x3, local copies, waits for them, and re-layouts: 1.21 us -> 0.08 us  [side(): return lax.dynamic_slice_in_dim(array, which * size, size, axis)]
    add x1, other arithmetic: 0.19 us -> 1.15 us  [on_device(): start = start + rate * came.astype(jnp.float32)]
    pallas_call x1, Pallas kernels: 2.87 us -> 3.81 us  [weights(): pl.pallas_call(functools.partial(weights_kernel, books, per), in_specs=[s...]
    ppermute x2, waiting for transfers between devices: 1.94 us -> 2.82 us  [across(): return lax.ppermute(block, 'date', [(i, i ^ hop) for i in range(n)])]
    ppermute x9, waiting for transfers between devices: 11.5 us -> 10.7 us  [exchange(): lax.ppermute(slots[i], 'book', [(j, j ^ i) for j in range(n)])]
    another operation x1, other arithmetic: 0.01 us -> 0.81 us  [on_device(): par = jnp.stack([persistence, volatility, base_rate])]
    convert_element_type x3 -> x2, other arithmetic: 1.88 us -> 1.09 us  [the longest x1 0.91 us: on_device(): code = jnp.round(group * scale).astype(jnp.int16)]
  transfers between devices with their start and end apart: 17 -> 17, of which waited for: 8 -> 10; matrix products, arithmetic and copies ran while one was open for 7% -> 8% of each run, Pallas kernels for 7% -> 7%
where the time goes in v4:
time: 52.2 us; the launch traced here: 51.6 us
  starting transfers between devices  21.7 us (42%)
  waiting for transfers between devices  15.5 us (30%)
  Pallas kernels  7.45 us (14%)
  other arithmetic  4.91 us (9%)
  local copies, waits for them, and re-layouts  1.25 us (2%)
  between operations  0.82 us (2%)
    ppermute x9, starting transfers between devices, exchange(): lax.ppermute(slots[i], 'book', [(j, j ^ i) for j in range(n)])  12.6 us
    ppermute x9, waiting for transfers between devices, exchange(): lax.ppermute(slots[i], 'book', [(j, j ^ i) for j in range(n)])  10.7 us
    ppermute x2, starting transfers between devices, across(): return lax.ppermute(block, 'date', [(i, i ^ hop) for i in range(n)])  5.6 us
    pallas_call x1, Pallas kernels, weights(): pl.pallas_call(functools.partial(weights_kernel, books, per), in_specs=[s...  3.81 us
    ppermute x2, waiting for transfers between devices, across(): return lax.ppermute(block, 'date', [(i, i ^ hop) for i in range(n)])  2.82 us
    pallas_call x1, Pallas kernels, values(): pl.pallas_call(functools.partial(values_kernel, books), in_specs=[pl.Bloc...  2.62 us
    ppermute x1, starting transfers between devices, later(): lax.ppermute(block, 'date', [(i, i + CORES) for i in range(n - CORES)])  2.31 us
    ppermute x5, starting transfers between devices, swap(): return lax.ppermute(block, 'date', [(i, i ^ 1) for i in range(n)])  1.22 us
  transfers between devices with their start and end apart: 17, of which 10 were waited for; matrix products, arithmetic and copies ran while one was open for 8% of the time, Pallas kernels for 7%

profile of v4, /device:TPU:0, one launch (start us, length us, event | category | flops | bytes accessed | tf_op | source)
XLA Modules:
  0.0 51.6 jit_solution(13575019601661084382)
XLA Ops:
  0.7 0.8 %pad_maximum_fusion.3.par_ref = f32[3,512]{1,0:T(4,128)S(1)} fusion(f32[1,512]{1,0:T(1,128)} %bitcast.26, f32[1,512]{1,0:T(1,128)} %bitcast.27, f32[1,512]{1,0:T(1,128)} %bitcast.28), kind=kLoop, calls=%fused_computation.21 | loop fusion | flops 3072 | bytes 12288 | tf_op jit(solution)/shard_map/stack | solution.py:262
  2.5 0.7 %reshape.18.sets_ref = s32[16,256]{1,0:T(8,128)S(1)} reshape(s32[4096]{0:T(1024)} %param.15) | data formatting | bytes 32768 | tf_op jit(solution)/shard_map/reshape | solution.py:100
  3.3 0.7 %collective-permute-done.got_ref = bf16[2,256,512]{2,1,0:T(8,128)(2,1)S(1)} collective-permute-done((bf16[2,256,512]{2,1,0:T(8,128)(2,1)S(1)}, bf16[2,256,512]{2,1,0:T(8,128)(2,1)S(1)}, u32[]{:S(2)}, u32[]{:S(2)}) %collective-permute-start) | collective-permute-done | bytes 524320 | tf_op jit(solution)/shard_map/ppermute | solution.py:20
  4.0 1.0 %first_code.1 = (s16[256,512]{1,0:T(8,128)(2,1)S(1)}, f32[256,512]{1,0:T(8,128)S(1)}, f32[8,512]{1,0:T(8,128)S(1)}) custom-call(s32[3]{0:T(128)S(1)} %pad_add_fusion.here_ref, f32[3,512]{1,0:T(4,128)S(1)} %pad_maximum_fusion.3.par_ref, bf16[2,256,512]{2,1,0:T(8,128)(2,1)S(1)} %constant_dynamic-slice_fusion.1.kept_ref, ...), custom_call_target="tpu_custom_call" | custom-call | flops 2097152 | bytes 2097152 | tf_op jit(solution)/shard_map/first_code/pallas_call | solution.py:215
  5.0 3.0 %collective-permute-start.1 = (s16[256,512]{1,0:T(8,128)(2,1)S(1)}, s16[256,512]{1,0:T(8,128)(2,1)S(1)}, u32[]{:S(2)}, u32[]{:S(2)}) collective-permute-start(s16[256,512]{1,0:T(8,128)(2,1)S(1)} %get-tuple-element.29), channel_id=1, source_target_pairs={{0,8},{4,12},{8,0},{12,4},{16,24},{20,28},{24,16},{28,20},{1,9},{5... | collective-permute-start | bytes 786440 | tf_op jit(solution)/shard_map/ppermute | solution.py:26
  8.0 3.8 %weights.1 = (f32[256,512]{1,0:T(8,128)S(1)}, bf16[256,512]{1,0:T(8,128)(2,1)S(1)}, bf16[256,512]{1,0:T(8,128)(2,1)S(1)}, bf16[256,512]{1,0:T(8,128)(2,1)S(1)}) custom-call(s32[3]{0:T(128)S(1)} %pad_add_fusion.here_ref, s32[16]{0:T(128)} %bitcast.29, s32[16,256]{1,0:T(8,128)S(1)} %reshape.18.sets_ref, bf16[4096,512]{1,0:T(8,128)(2,1)} %flows_hbm.1), custom_call_target="tpu_custom_call" | custom-call | flops 1073741824 | bytes 4194304 | tf_op jit(solution)/shard_map/weights/pallas_call | solution.py:79
  11.9 1.6 %collective-permute-start.3 = (bf16[256,512]{1,0:T(8,128)(2,1)S(1)}, bf16[256,512]{1,0:T(8,128)(2,1)S(1)}, u32[]{:S(2)}, u32[]{:S(2)}) collective-permute-start(bf16[256,512]{1,0:T(8,128)(2,1)S(1)} %get-tuple-element.35), channel_id=1, source_target_pairs={{0,1},{1,0},{2,3},{3,2},{4,5},{5,4},{6,7},{7,6},{8,9},{9,8},{10,11... | collective-permute-start | bytes 786440 | tf_op jit(solution)/shard_map/ppermute | solution.py:37
  13.4 1.5 %collective-permute-start.4 = (bf16[256,512]{1,0:T(8,128)(2,1)S(1)}, bf16[256,512]{1,0:T(8,128)(2,1)S(1)}, u32[]{:S(2)}, u32[]{:S(2)}) collective-permute-start(bf16[256,512]{1,0:T(8,128)(2,1)S(1)} %get-tuple-element.36), channel_id=1, source_target_pairs={{0,2},{1,3},{2,0},{3,1},{4,6},{5,7},{6,4},{7,5},{8,10},{9,11},{10,... | collective-permute-start | bytes 786440 | tf_op jit(solution)/shard_map/ppermute | solution.py:37
  15.4 0.9 %round-nearest-even_convert_fusion = s16[256,512]{1,0:T(8,128)(2,1)} fusion(s16[256,512]{1,0:T(8,128)(2,1)S(1)} %collective-permute-done.1, f32[256,512]{1,0:T(8,128)S(1)} %get-tuple-element.30, f32[512]{0:T(512)S(1)} %bitcast.23, f32[512]{0:T(512)S(1)} %bitcast.24, f32[512]{0:T(512)S(1)} %bitcast.25), kind=kLoop, calls=%fused_computation.14 | loop fusion | flops 917504 | bytes 1054720 | tf_op jit(solution)/shard_map/convert_element_type | solution.py:273
  16.3 2.6 %collective-permute-start.2 = (s16[256,512]{1,0:T(8,128)(2,1)}, s16[256,512]{1,0:T(8,128)(2,1)}, u32[]{:S(2)}, u32[]{:S(2)}) collective-permute-start(s16[256,512]{1,0:T(8,128)(2,1)} %round-nearest-even_convert_fusion), channel_id=1, source_target_pairs={{0,16},{4,20},{8,24},{12,28},{16,0},{20,4},{24,8},{28,12},{1,17},{... | collective-permute-start | bytes 786440 | tf_op jit(solution)/shard_map/ppermute | solution.py:26
  18.9 2.2 %collective-permute-done.3 = bf16[256,512]{1,0:T(8,128)(2,1)S(1)} collective-permute-done((bf16[256,512]{1,0:T(8,128)(2,1)S(1)}, bf16[256,512]{1,0:T(8,128)(2,1)S(1)}, u32[]{:S(2)}, u32[]{:S(2)}) %collective-permute-start.3) | collective-permute-done | bytes 262176 | tf_op jit(solution)/shard_map/ppermute | solution.py:37
  21.1 5.7 %collective-permute-done.4 = bf16[256,512]{1,0:T(8,128)(2,1)S(1)} collective-permute-done((bf16[256,512]{1,0:T(8,128)(2,1)S(1)}, bf16[256,512]{1,0:T(8,128)(2,1)S(1)}, u32[]{:S(2)}, u32[]{:S(2)}) %collective-permute-start.4) | collective-permute-done | bytes 262176 | tf_op jit(solution)/shard_map/ppermute | solution.py:37
  27.6 2.8 %collective-permute-done.2 = s16[256,512]{1,0:T(8,128)(2,1)} collective-permute-done((s16[256,512]{1,0:T(8,128)(2,1)}, s16[256,512]{1,0:T(8,128)(2,1)}, u32[]{:S(2)}, u32[]{:S(2)}) %collective-permute-start.2) | collective-permute-done | bytes 262176 | tf_op jit(solution)/shard_map/ppermute | solution.py:26
  30.4 1.2 %multiply_add_fusion.start_ref = f32[256,512]{1,0:T(8,128)S(1)} fusion(s16[256,512]{1,0:T(8,128)(2,1)} %collective-permute-done.2, s16[256,512]{1,0:T(8,128)(2,1)S(1)} %collective-permute-done.1, f32[512]{0:T(512)S(1)} %bitcast.22, f32[512]{0:T(512)S(1)} %bitcast.21), kind=kLoop, calls=%fused_computation.13 | loop fusion | flops 655360 | bytes 1052672 | tf_op jit(solution)/shard_map/add | solution.py:278
  31.6 2.6 %values.1 = (f32[512,128]{1,0:T(8,128)S(1)}, bf16[512,128]{1,0:T(8,128)(2,1)S(1)}, bf16[512,128]{1,0:T(8,128)(2,1)S(1)}, bf16[512,128]{1,0:T(8,128)(2,1)S(1)}, f...) custom-call(s32[3]{0:T(128)S(1)} %pad_add_fusion.here_ref, ...), custom_call_target="tpu_custom_call" | custom-call | flops 1073741824 | bytes 2097152 | tf_op jit(solution)/shard_map/values/pallas_call | solution.py:151
  34.2 2.5 %collective-permute-start.10 = (bf16[512,128]{1,0:T(8,128)(2,1)S(1)}, bf16[512,128]{1,0:T(8,128)(2,1)S(1)}, u32[]{:S(2)}, u32[]{:S(2)}) collective-permute-start(bf16[512,128]{1,0:T(8,128)(2,1)S(1)} %get-tuple-element.42), channel_id=1, source_target_pairs={{0,3},{1,2},{2,1},{3,0},{4,7},{5,6},{6,5},{7,4},{8,11},{9,10},{10,... | collective-permute-start | bytes 393224 | tf_op jit(solution)/shard_map/ppermute | solution.py:37
  37.8 1.5 %collective-permute-start.11 = (bf16[512,128]{1,0:T(8,128)(2,1)S(1)}, bf16[512,128]{1,0:T(8,128)(2,1)S(1)}, u32[]{:S(2)}, u32[]{:S(2)}) collective-permute-start(bf16[512,128]{1,0:T(8,128)(2,1)S(1)} %get-tuple-element.44), channel_id=1, source_target_pairs={{0,1},{1,0},{2,3},{3,2},{4,5},{5,4},{6,7},{7,6},{8,9},{9,8},{10,11... | collective-permute-start | bytes 393224 | tf_op jit(solution)/shard_map/ppermute | solution.py:37
  39.3 1.5 %collective-permute-start.12 = (bf16[512,128]{1,0:T(8,128)(2,1)S(1)}, bf16[512,128]{1,0:T(8,128)(2,1)S(1)}, u32[]{:S(2)}, u32[]{:S(2)}) collective-permute-start(bf16[512,128]{1,0:T(8,128)(2,1)S(1)} %get-tuple-element.45), channel_id=1, source_target_pairs={{0,2},{1,3},{2,0},{3,1},{4,6},{5,7},{6,4},{7,5},{8,10},{9,11},{10,... | collective-permute-start | bytes 393224 | tf_op jit(solution)/shard_map/ppermute | solution.py:37
  40.8 0.8 %collective-permute-done.10 = bf16[512,128]{1,0:T(8,128)(2,1)S(1)} collective-permute-done((bf16[512,128]{1,0:T(8,128)(2,1)S(1)}, bf16[512,128]{1,0:T(8,128)(2,1)S(1)}, u32[]{:S(2)}, u32[]{:S(2)}) %collective-permute-start.10) | collective-permute-done | bytes 131104 | tf_op jit(solution)/shard_map/ppermute | solution.py:37
  41.6 2.4 %collective-permute-start.13 = (bf16[512,128]{1,0:T(8,128)(2,1)S(1)}, bf16[512,128]{1,0:T(8,128)(2,1)S(1)}, u32[]{:S(2)}, u32[]{:S(2)}) collective-permute-start(bf16[512,128]{1,0:T(8,128)(2,1)S(1)} %get-tuple-element.46), channel_id=1, source_target_pairs={{0,3},{1,2},{2,1},{3,0},{4,7},{5,6},{6,5},{7,4},{8,11},{9,10},{10,... | collective-permute-start | bytes 393224 | tf_op jit(solution)/shard_map/ppermute | solution.py:37
  44.6 2.3 %collective-permute-start.14 = (bf16[2,256,128]{2,1,0:T(8,128)(2,1)S(1)}, bf16[2,256,128]{2,1,0:T(8,128)(2,1)S(1)}, u32[]{:S(2)}, u32[]{:S(2)}) collective-permute-start(bf16[2,256,128]{2,1,0:T(8,128)(2,1)S(1)} %get-tuple-element.50), channel_id=1, source_target_pairs={{0,8},{4,12},{8,16},{12,20},{16,24},{20,28},{1,9},{5,13},{9,17},{1... | collective-permute-start | bytes 393224 | tf_op jit(solution)/shard_map/ppermute | solution.py:31
  46.9 1.5 %collective-permute-done.12 = bf16[512,128]{1,0:T(8,128)(2,1)S(1)} collective-permute-done((bf16[512,128]{1,0:T(8,128)(2,1)S(1)}, bf16[512,128]{1,0:T(8,128)(2,1)S(1)}, u32[]{:S(2)}, u32[]{:S(2)}) %collective-permute-start.12) | collective-permute-done | bytes 131104 | tf_op jit(solution)/shard_map/ppermute | solution.py:37
  48.6 0.8 %collective-permute-done.14 = bf16[2,256,128]{2,1,0:T(8,128)(2,1)S(1)} collective-permute-done((bf16[2,256,128]{2,1,0:T(8,128)(2,1)S(1)}, bf16[2,256,128]{2,1,0:T(8,128)(2,1)S(1)}, u32[]{:S(2)}, u32[]{:S(2)}) %collective-permute-start.14) | collective-permute-done | bytes 131104 | tf_op jit(solution)/shard_map/ppermute | solution.py:31
  50.2 0.8 %pad_maximum_fusion.2 = f32[2,512,128]{2,1,0:T(8,128)} fusion(f32[2,256,128]{2,1,0:T(8,128)S(1)} %get-tuple-element.57, f32[2,256,128]{2,1,0:T(8,128)S(1)} %get-tuple-element.56), kind=kLoop, calls=%fused_computation.11 | loop fusion | flops 131072 | bytes 1048576 | tf_op jit(solution)/shard_map/concatenate | solution.py:316
  (38 shorter events, 5.5 us)
Async XLA Ops:
  0.6 1.3 %copy-start = (bf16[2,512,512]{2,1,0:T(8,128)(2,1)S(1)}, bf16[2,512,512]{2,1,0:T(8,128)(2,1)}, u32[]{:S(2)}) copy-start(bf16[2,512,512]{2,1,0:T(8,128)(2,1)} %param.9) | copy-start | bytes 3145732
  1.9 2.1 %collective-permute-start = (bf16[2,256,512]{2,1,0:T(8,128)(2,1)S(1)}, bf16[2,256,512]{2,1,0:T(8,128)(2,1)S(1)}, u32[]{:S(2)}, u32[]{:S(2)}) collective-permute-start(bf16[2,256,512]{2,1,0:T(8,128)(2,1)S(1)} %constant_dynamic-slice_fusion.2), channel_id=1, source_target_pairs={{0,4},{4,0},{8,12},{12,8},{16,20},{20,16},{24,28},{28,24},{1,5},{5... | collective-permute-start | bytes 1572872 | tf_op jit(solution)/shard_map/ppermute | solution.py:20
  5.0 10.4 %collective-permute-start.1 = (s16[256,512]{1,0:T(8,128)(2,1)S(1)}, s16[256,512]{1,0:T(8,128)(2,1)S(1)}, u32[]{:S(2)}, u32[]{:S(2)}) collective-permute-start(s16[256,512]{1,0:T(8,128)(2,1)S(1)} %get-tuple-element.29), channel_id=1, source_target_pairs={{0,8},{4,12},{8,0},{12,4},{16,24},{20,28},{24,16},{28,20},{1,9},{5... | collective-permute-start | bytes 786440 | tf_op jit(solution)/shard_map/ppermute | solution.py:26
  11.9 25.9 %copy-start.2 = (s32[128]{0:T(128)S(1)}, s32[128]{0:T(128)}, u32[]{:S(2)}) copy-start(s32[128]{0:T(128)} %param.17) | copy-start | bytes 1540
  11.9 9.3 %collective-permute-start.3 = (bf16[256,512]{1,0:T(8,128)(2,1)S(1)}, bf16[256,512]{1,0:T(8,128)(2,1)S(1)}, u32[]{:S(2)}, u32[]{:S(2)}) collective-permute-start(bf16[256,512]{1,0:T(8,128)(2,1)S(1)} %get-tuple-element.35), channel_id=1, source_target_pairs={{0,1},{1,0},{2,3},{3,2},{4,5},{5,4},{6,7},{7,6},{8,9},{9,8},{10,11... | collective-permute-start | bytes 786440 | tf_op jit(solution)/shard_map/ppermute | solution.py:37
  13.4 13.4 %collective-permute-start.4 = (bf16[256,512]{1,0:T(8,128)(2,1)S(1)}, bf16[256,512]{1,0:T(8,128)(2,1)S(1)}, u32[]{:S(2)}, u32[]{:S(2)}) collective-permute-start(bf16[256,512]{1,0:T(8,128)(2,1)S(1)} %get-tuple-element.36), channel_id=1, source_target_pairs={{0,2},{1,3},{2,0},{3,1},{4,6},{5,7},{6,4},{7,5},{8,10},{9,11},{10,... | collective-permute-start | bytes 786440 | tf_op jit(solution)/shard_map/ppermute | solution.py:37
  14.9 11.9 %collective-permute-start.5 = (bf16[256,512]{1,0:T(8,128)(2,1)S(1)}, bf16[256,512]{1,0:T(8,128)(2,1)S(1)}, u32[]{:S(2)}, u32[]{:S(2)}) collective-permute-start(bf16[256,512]{1,0:T(8,128)(2,1)S(1)} %get-tuple-element.37), channel_id=1, source_target_pairs={{0,3},{1,2},{2,1},{3,0},{4,7},{5,6},{6,5},{7,4},{8,11},{9,10},{10,... | collective-permute-start | bytes 786440 | tf_op jit(solution)/shard_map/ppermute | solution.py:37
  16.3 14.1 %collective-permute-start.2 = (s16[256,512]{1,0:T(8,128)(2,1)}, s16[256,512]{1,0:T(8,128)(2,1)}, u32[]{:S(2)}, u32[]{:S(2)}) collective-permute-start(s16[256,512]{1,0:T(8,128)(2,1)} %round-nearest-even_convert_fusion), channel_id=1, source_target_pairs={{0,16},{4,20},{8,24},{12,28},{16,0},{20,4},{24,8},{28,12},{1,17},{... | collective-permute-start | bytes 786440 | tf_op jit(solution)/shard_map/ppermute | solution.py:26
  27.0 4.6 %collective-permute-start.6 = (bf16[256,512]{1,0:T(8,128)(2,1)S(1)}, bf16[256,512]{1,0:T(8,128)(2,1)S(1)}, u32[]{:S(2)}, u32[]{:S(2)}) collective-permute-start(bf16[256,512]{1,0:T(8,128)(2,1)S(1)} %get-tuple-element.55.refs_0_), channel_id=1, source_target_pairs={{0,4},{4,0},{8,12},{12,8},{16,20},{20,16},{24,28},{28,24},{1,5},{5... | collective-permute-start | bytes 786440 | tf_op jit(solution)/shard_map/ppermute | solution.py:20
  27.1 4.5 %collective-permute-start.7 = (bf16[256,512]{1,0:T(8,128)(2,1)S(1)}, bf16[256,512]{1,0:T(8,128)(2,1)S(1)}, u32[]{:S(2)}, u32[]{:S(2)}) collective-permute-start(bf16[256,512]{1,0:T(8,128)(2,1)S(1)} %get-tuple-element.54.refs_1_), channel_id=1, source_target_pairs={{0,4},{4,0},{8,12},{12,8},{16,20},{20,16},{24,28},{28,24},{1,5},{5... | collective-permute-start | bytes 786440 | tf_op jit(solution)/shard_map/ppermute | solution.py:20
  30.4 19.0 %copy-start.1 = (f32[128]{0:T(128)S(1)}, f32[128]{0:T(128)}, u32[]{:S(2)}) copy-start(f32[128]{0:T(128)} %param.16) | copy-start | bytes 1540
  34.2 7.4 %collective-permute-start.10 = (bf16[512,128]{1,0:T(8,128)(2,1)S(1)}, bf16[512,128]{1,0:T(8,128)(2,1)S(1)}, u32[]{:S(2)}, u32[]{:S(2)}) collective-permute-start(bf16[512,128]{1,0:T(8,128)(2,1)S(1)} %get-tuple-element.42), channel_id=1, source_target_pairs={{0,3},{1,2},{2,1},{3,0},{4,7},{5,6},{6,5},{7,4},{8,11},{9,10},{10,... | collective-permute-start | bytes 393224 | tf_op jit(solution)/shard_map/ppermute | solution.py:37
  36.7 7.7 %collective-permute-start.8 = (bf16[512,128]{1,0:T(8,128)(2,1)S(1)}, bf16[512,128]{1,0:T(8,128)(2,1)S(1)}, u32[]{:S(2)}, u32[]{:S(2)}) collective-permute-start(bf16[512,128]{1,0:T(8,128)(2,1)S(1)} %get-tuple-element.40), channel_id=1, source_target_pairs={{0,1},{1,0},{2,3},{3,2},{4,5},{5,4},{6,7},{7,6},{8,9},{9,8},{10,11... | collective-permute-start | bytes 393224 | tf_op jit(solution)/shard_map/ppermute | solution.py:37
  37.3 7.2 %collective-permute-start.9 = (bf16[512,128]{1,0:T(8,128)(2,1)S(1)}, bf16[512,128]{1,0:T(8,128)(2,1)S(1)}, u32[]{:S(2)}, u32[]{:S(2)}) collective-permute-start(bf16[512,128]{1,0:T(8,128)(2,1)S(1)} %get-tuple-element.41), channel_id=1, source_target_pairs={{0,2},{1,3},{2,0},{3,1},{4,6},{5,7},{6,4},{7,5},{8,10},{9,11},{10,... | collective-permute-start | bytes 393224 | tf_op jit(solution)/shard_map/ppermute | solution.py:37
  37.8 9.2 %collective-permute-start.11 = (bf16[512,128]{1,0:T(8,128)(2,1)S(1)}, bf16[512,128]{1,0:T(8,128)(2,1)S(1)}, u32[]{:S(2)}, u32[]{:S(2)}) collective-permute-start(bf16[512,128]{1,0:T(8,128)(2,1)S(1)} %get-tuple-element.44), channel_id=1, source_target_pairs={{0,1},{1,0},{2,3},{3,2},{4,5},{5,4},{6,7},{7,6},{8,9},{9,8},{10,11... | collective-permute-start | bytes 393224 | tf_op jit(solution)/shard_map/ppermute | solution.py:37
  39.3 9.1 %collective-permute-start.12 = (bf16[512,128]{1,0:T(8,128)(2,1)S(1)}, bf16[512,128]{1,0:T(8,128)(2,1)S(1)}, u32[]{:S(2)}, u32[]{:S(2)}) collective-permute-start(bf16[512,128]{1,0:T(8,128)(2,1)S(1)} %get-tuple-element.45), channel_id=1, source_target_pairs={{0,2},{1,3},{2,0},{3,1},{4,6},{5,7},{6,4},{7,5},{8,10},{9,11},{10,... | collective-permute-start | bytes 393224 | tf_op jit(solution)/shard_map/ppermute | solution.py:37
  41.6 6.8 %collective-permute-start.13 = (bf16[512,128]{1,0:T(8,128)(2,1)S(1)}, bf16[512,128]{1,0:T(8,128)(2,1)S(1)}, u32[]{:S(2)}, u32[]{:S(2)}) collective-permute-start(bf16[512,128]{1,0:T(8,128)(2,1)S(1)} %get-tuple-element.46), channel_id=1, source_target_pairs={{0,3},{1,2},{2,1},{3,0},{4,7},{5,6},{6,5},{7,4},{8,11},{9,10},{10,... | collective-permute-start | bytes 393224 | tf_op jit(solution)/shard_map/ppermute | solution.py:37
  44.6 4.8 %collective-permute-start.14 = (bf16[2,256,128]{2,1,0:T(8,128)(2,1)S(1)}, bf16[2,256,128]{2,1,0:T(8,128)(2,1)S(1)}, u32[]{:S(2)}, u32[]{:S(2)}) collective-permute-start(bf16[2,256,128]{2,1,0:T(8,128)(2,1)S(1)} %get-tuple-element.50), channel_id=1, source_target_pairs={{0,8},{4,12},{8,16},{12,20},{16,24},{20,28},{1,9},{5,13},{9,17},{1... | collective-permute-start | bytes 393224 | tf_op jit(solution)/shard_map/ppermute | solution.py:31
  48.5 1.6 %collective-permute-start.15 = (f32[2,256,128]{2,1,0:T(8,128)S(1)}, f32[2,256,128]{2,1,0:T(8,128)S(1)}, u32[]{:S(2)}, u32[]{:S(2)}) collective-permute-start(f32[2,256,128]{2,1,0:T(8,128)S(1)} %broadcast_select_fusion.2), channel_id=1, source_target_pairs={{0,4},{4,0},{8,12},{12,8},{16,20},{20,16},{24,28},{28,24},{1,5},{5... | collective-permute-start | bytes 786440 | tf_op jit(solution)/shard_map/ppermute | solution.py:20
  49.5 1.5 %collective-permute-start.16 = (f32[2,128]{1,0:T(2,128)S(1)}, f32[2,128]{1,0:T(2,128)S(1)}, u32[]{:S(2)}, u32[]{:S(2)}) collective-permute-start(f32[2,128]{1,0:T(2,128)S(1)} %constant_dynamic-slice_fusion), channel_id=1, source_target_pairs={{0,4},{4,0},{8,12},{12,8},{16,20},{20,16},{24,28},{28,24},{1,5},{5... | collective-permute-start | bytes 3080 | tf_op jit(solution)/shard_map/ppermute | solution.py:20

commit v5 on v4

--- a/solution.py
+++ b/solution.py
@@ -299,7 +299,7 @@
 
     late_net = gathered(late_pieces[0], late_arrived)
     before = later(late_net.astype(jnp.bfloat16))
-    early_net = gathered(after(early_pieces[0], late_net), early_arrived)
+    early_net = gathered(after(early_pieces[0], late_net, before), early_arrived)
     net_got = swap(jnp.where(core == 0, late_net, early_net))
     net_kept = jnp.where(core == 0, early_net, late_net)
 

time: 52.2 us -> 51.5 us (0.987)
  other arithmetic: 4.91 us -> 3.25 us
  starting transfers between devices: 21.7 us -> 22.3 us
    ppermute x1, waiting for transfers between devices: 0.76 us -> 2.47 us  [later(): lax.ppermute(block, 'date', [(i, i + CORES) for i in range(n - CORES)])]
    add x1, other arithmetic: 1.15 us -> 0.19 us  [on_device(): start = start + rate * came.astype(jnp.float32)]
    ppermute x2, waiting for transfers between devices: 2.82 us -> 1.87 us  [across(): return lax.ppermute(block, 'date', [(i, i ^ hop) for i in range(n)])]
    ppermute x9, waiting for transfers between devices: 10.7 us -> 9.77 us  [exchange(): lax.ppermute(slots[i], 'book', [(j, j ^ i) for j in range(n)])]
    convert_element_type x1, other arithmetic: 0.91 us -> 0.21 us  [on_device(): code = jnp.round(group * scale).astype(jnp.int16)]
  transfers between devices with their start and end apart: 17 -> 17, of which waited for: 10 -> 8; matrix products, arithmetic and copies ran while one was open for 8% -> 5% of each run, Pallas kernels for 7% -> 8%
where the time goes in v5:
time: 51.5 us; the launch traced here: 50.7 us
  starting transfers between devices  22.3 us (43%)
  waiting for transfers between devices  15.6 us (30%)
  Pallas kernels  7.46 us (14%)
  other arithmetic  3.25 us (6%)
  local copies, waits for them, and re-layouts  1.25 us (2%)
  between operations  0.84 us (2%)
    ppermute x9, starting transfers between devices, exchange(): lax.ppermute(slots[i], 'book', [(j, j ^ i) for j in range(n)])  12.6 us
    ppermute x9, waiting for transfers between devices, exchange(): lax.ppermute(slots[i], 'book', [(j, j ^ i) for j in range(n)])  9.77 us
    ppermute x2, starting transfers between devices, across(): return lax.ppermute(block, 'date', [(i, i ^ hop) for i in range(n)])  5.67 us
    pallas_call x1, Pallas kernels, weights(): pl.pallas_call(functools.partial(weights_kernel, books, per), in_specs=[s...  3.81 us
    pallas_call x1, Pallas kernels, values(): pl.pallas_call(functools.partial(values_kernel, books), in_specs=[pl.Bloc...  2.64 us
    ppermute x1, waiting for transfers between devices, later(): lax.ppermute(block, 'date', [(i, i + CORES) for i in range(n - CORES)])  2.47 us
    ppermute x1, starting transfers between devices, later(): lax.ppermute(block, 'date', [(i, i + CORES) for i in range(n - CORES)])  2.32 us
    ppermute x2, waiting for transfers between devices, across(): return lax.ppermute(block, 'date', [(i, i ^ hop) for i in range(n)])  1.87 us
  transfers between devices with their start and end apart: 17, of which 8 were waited for; matrix products, arithmetic and copies ran while one was open for 5% of the time, Pallas kernels for 8%

profile of v5, /device:TPU:0, one launch (start us, length us, event | category | flops | bytes accessed | tf_op | source)
XLA Modules:
  0.0 50.7 jit_solution(12903083128750387738)
XLA Ops:
  0.7 0.8 %pad_maximum_fusion.3.par_ref = f32[3,512]{1,0:T(4,128)S(1)} fusion(f32[1,512]{1,0:T(1,128)} %bitcast.26, f32[1,512]{1,0:T(1,128)} %bitcast.27, f32[1,512]{1,0:T(1,128)} %bitcast.28), kind=kLoop, calls=%fused_computation.21 | loop fusion | flops 3072 | bytes 12288 | tf_op jit(solution)/shard_map/stack | solution.py:262
  2.5 0.7 %reshape.18.sets_ref = s32[16,256]{1,0:T(8,128)S(1)} reshape(s32[4096]{0:T(1024)} %param.15) | data formatting | bytes 32768 | tf_op jit(solution)/shard_map/reshape | solution.py:100
  3.3 0.7 %collective-permute-done.got_ref = bf16[2,256,512]{2,1,0:T(8,128)(2,1)S(1)} collective-permute-done((bf16[2,256,512]{2,1,0:T(8,128)(2,1)S(1)}, bf16[2,256,512]{2,1,0:T(8,128)(2,1)S(1)}, u32[]{:S(2)}, u32[]{:S(2)}) %collective-permute-start) | collective-permute-done | bytes 524320 | tf_op jit(solution)/shard_map/ppermute | solution.py:20
  4.0 1.0 %first_code.1 = (s16[256,512]{1,0:T(8,128)(2,1)S(1)}, f32[256,512]{1,0:T(8,128)S(1)}, f32[8,512]{1,0:T(8,128)S(1)}) custom-call(s32[3]{0:T(128)S(1)} %pad_add_fusion.here_ref, f32[3,512]{1,0:T(4,128)S(1)} %pad_maximum_fusion.3.par_ref, bf16[2,256,512]{2,1,0:T(8,128)(2,1)S(1)} %constant_dynamic-slice_fusion.1.kept_ref, ...), custom_call_target="tpu_custom_call" | custom-call | flops 2097152 | bytes 2097152 | tf_op jit(solution)/shard_map/first_code/pallas_call | solution.py:215
  5.0 3.0 %collective-permute-start.1 = (s16[256,512]{1,0:T(8,128)(2,1)S(1)}, s16[256,512]{1,0:T(8,128)(2,1)S(1)}, u32[]{:S(2)}, u32[]{:S(2)}) collective-permute-start(s16[256,512]{1,0:T(8,128)(2,1)S(1)} %get-tuple-element.29), channel_id=1, source_target_pairs={{0,8},{4,12},{8,0},{12,4},{16,24},{20,28},{24,16},{28,20},{1,9},{5... | collective-permute-start | bytes 786440 | tf_op jit(solution)/shard_map/ppermute | solution.py:26
  8.0 3.8 %weights.1 = (f32[256,512]{1,0:T(8,128)S(1)}, bf16[256,512]{1,0:T(8,128)(2,1)S(1)}, bf16[256,512]{1,0:T(8,128)(2,1)S(1)}, bf16[256,512]{1,0:T(8,128)(2,1)S(1)}) custom-call(s32[3]{0:T(128)S(1)} %pad_add_fusion.here_ref, s32[16]{0:T(128)} %bitcast.29, s32[16,256]{1,0:T(8,128)S(1)} %reshape.18.sets_ref, bf16[4096,512]{1,0:T(8,128)(2,1)} %flows_hbm.1), custom_call_target="tpu_custom_call" | custom-call | flops 1073741824 | bytes 4194304 | tf_op jit(solution)/shard_map/weights/pallas_call | solution.py:79
  11.9 1.6 %collective-permute-start.3 = (bf16[256,512]{1,0:T(8,128)(2,1)S(1)}, bf16[256,512]{1,0:T(8,128)(2,1)S(1)}, u32[]{:S(2)}, u32[]{:S(2)}) collective-permute-start(bf16[256,512]{1,0:T(8,128)(2,1)S(1)} %get-tuple-element.35), channel_id=1, source_target_pairs={{0,1},{1,0},{2,3},{3,2},{4,5},{5,4},{6,7},{7,6},{8,9},{9,8},{10,11... | collective-permute-start | bytes 786440 | tf_op jit(solution)/shard_map/ppermute | solution.py:37
  13.4 1.5 %collective-permute-start.4 = (bf16[256,512]{1,0:T(8,128)(2,1)S(1)}, bf16[256,512]{1,0:T(8,128)(2,1)S(1)}, u32[]{:S(2)}, u32[]{:S(2)}) collective-permute-start(bf16[256,512]{1,0:T(8,128)(2,1)S(1)} %get-tuple-element.36), channel_id=1, source_target_pairs={{0,2},{1,3},{2,0},{3,1},{4,6},{5,7},{6,4},{7,5},{8,10},{9,11},{10,... | collective-permute-start | bytes 786440 | tf_op jit(solution)/shard_map/ppermute | solution.py:37
  15.7 2.7 %collective-permute-start.2 = (s16[256,512]{1,0:T(8,128)(2,1)S(1)}, s16[256,512]{1,0:T(8,128)(2,1)S(1)}, u32[]{:S(2)}, u32[]{:S(2)}) collective-permute-start(s16[256,512]{1,0:T(8,128)(2,1)S(1)} %round-nearest-even_convert_fusion), channel_id=1, source_target_pairs={{0,16},{4,20},{8,24},{12,28},{16,0},{20,4},{24,8},{28,12},{1,17},{... | collective-permute-start | bytes 786440 | tf_op jit(solution)/shard_map/ppermute | solution.py:26
  18.3 2.8 %collective-permute-done.3 = bf16[256,512]{1,0:T(8,128)(2,1)S(1)} collective-permute-done((bf16[256,512]{1,0:T(8,128)(2,1)S(1)}, bf16[256,512]{1,0:T(8,128)(2,1)S(1)}, u32[]{:S(2)}, u32[]{:S(2)}) %collective-permute-start.3) | collective-permute-done | bytes 262176 | tf_op jit(solution)/shard_map/ppermute | solution.py:37
  21.1 5.7 %collective-permute-done.4 = bf16[256,512]{1,0:T(8,128)(2,1)S(1)} collective-permute-done((bf16[256,512]{1,0:T(8,128)(2,1)S(1)}, bf16[256,512]{1,0:T(8,128)(2,1)S(1)}, u32[]{:S(2)}, u32[]{:S(2)}) %collective-permute-start.4) | collective-permute-done | bytes 262176 | tf_op jit(solution)/shard_map/ppermute | solution.py:37
  27.6 1.9 %collective-permute-done.2 = s16[256,512]{1,0:T(8,128)(2,1)S(1)} collective-permute-done((s16[256,512]{1,0:T(8,128)(2,1)S(1)}, s16[256,512]{1,0:T(8,128)(2,1)S(1)}, u32[]{:S(2)}, u32[]{:S(2)}) %collective-permute-start.2) | collective-permute-done | bytes 262176 | tf_op jit(solution)/shard_map/ppermute | solution.py:26
  29.7 2.6 %values.1 = (f32[512,128]{1,0:T(8,128)S(1)}, bf16[512,128]{1,0:T(8,128)(2,1)S(1)}, bf16[512,128]{1,0:T(8,128)(2,1)S(1)}, bf16[512,128]{1,0:T(8,128)(2,1)S(1)}, f...) custom-call(s32[3]{0:T(128)S(1)} %pad_add_fusion.here_ref, ...), custom_call_target="tpu_custom_call" | custom-call | flops 1073741824 | bytes 2097152 | tf_op jit(solution)/shard_map/values/pallas_call | solution.py:151
  32.3 2.5 %collective-permute-start.10 = (bf16[512,128]{1,0:T(8,128)(2,1)S(1)}, bf16[512,128]{1,0:T(8,128)(2,1)S(1)}, u32[]{:S(2)}, u32[]{:S(2)}) collective-permute-start(bf16[512,128]{1,0:T(8,128)(2,1)S(1)} %get-tuple-element.42), channel_id=1, source_target_pairs={{0,3},{1,2},{2,1},{3,0},{4,7},{5,6},{6,5},{7,4},{8,11},{9,10},{10,... | collective-permute-start | bytes 393224 | tf_op jit(solution)/shard_map/ppermute | solution.py:37
  35.9 1.5 %collective-permute-start.12 = (bf16[512,128]{1,0:T(8,128)(2,1)S(1)}, bf16[512,128]{1,0:T(8,128)(2,1)S(1)}, u32[]{:S(2)}, u32[]{:S(2)}) collective-permute-start(bf16[512,128]{1,0:T(8,128)(2,1)S(1)} %get-tuple-element.44), channel_id=1, source_target_pairs={{0,1},{1,0},{2,3},{3,2},{4,5},{5,4},{6,7},{7,6},{8,9},{9,8},{10,11... | collective-permute-start | bytes 393224 | tf_op jit(solution)/shard_map/ppermute | solution.py:37
  37.4 1.5 %collective-permute-start.13 = (bf16[512,128]{1,0:T(8,128)(2,1)S(1)}, bf16[512,128]{1,0:T(8,128)(2,1)S(1)}, u32[]{:S(2)}, u32[]{:S(2)}) collective-permute-start(bf16[512,128]{1,0:T(8,128)(2,1)S(1)} %get-tuple-element.45), channel_id=1, source_target_pairs={{0,2},{1,3},{2,0},{3,1},{4,6},{5,7},{6,4},{7,5},{8,10},{9,11},{10,... | collective-permute-start | bytes 393224 | tf_op jit(solution)/shard_map/ppermute | solution.py:37
  38.9 0.8 %collective-permute-done.10 = bf16[512,128]{1,0:T(8,128)(2,1)S(1)} collective-permute-done((bf16[512,128]{1,0:T(8,128)(2,1)S(1)}, bf16[512,128]{1,0:T(8,128)(2,1)S(1)}, u32[]{:S(2)}, u32[]{:S(2)}) %collective-permute-start.10) | collective-permute-done | bytes 131104 | tf_op jit(solution)/shard_map/ppermute | solution.py:37
  39.7 2.4 %collective-permute-start.14 = (bf16[512,128]{1,0:T(8,128)(2,1)S(1)}, bf16[512,128]{1,0:T(8,128)(2,1)S(1)}, u32[]{:S(2)}, u32[]{:S(2)}) collective-permute-start(bf16[512,128]{1,0:T(8,128)(2,1)S(1)} %get-tuple-element.46), channel_id=1, source_target_pairs={{0,3},{1,2},{2,1},{3,0},{4,7},{5,6},{6,5},{7,4},{8,11},{9,10},{10,... | collective-permute-start | bytes 393224 | tf_op jit(solution)/shard_map/ppermute | solution.py:37
  42.7 2.3 %collective-permute-start.11 = (bf16[2,256,128]{2,1,0:T(8,128)(2,1)S(1)}, bf16[2,256,128]{2,1,0:T(8,128)(2,1)S(1)}, u32[]{:S(2)}, u32[]{:S(2)}) collective-permute-start(bf16[2,256,128]{2,1,0:T(8,128)(2,1)S(1)} %get-tuple-element.52), channel_id=1, source_target_pairs={{0,8},{4,12},{8,16},{12,20},{16,24},{20,28},{1,9},{5,13},{9,17},{1... | collective-permute-start | bytes 393224 | tf_op jit(solution)/shard_map/ppermute | solution.py:31
  45.0 2.5 %collective-permute-done.11 = bf16[2,256,128]{2,1,0:T(8,128)(2,1)S(1)} collective-permute-done((bf16[2,256,128]{2,1,0:T(8,128)(2,1)S(1)}, bf16[2,256,128]{2,1,0:T(8,128)(2,1)S(1)}, u32[]{:S(2)}, u32[]{:S(2)}) %collective-permute-start.11) | collective-permute-done | bytes 131104 | tf_op jit(solution)/shard_map/ppermute | solution.py:31
  47.9 0.6 %collective-permute-start.16 = (f32[2,128]{1,0:T(2,128)S(1)}, f32[2,128]{1,0:T(2,128)S(1)}, u32[]{:S(2)}, u32[]{:S(2)}) collective-permute-start(f32[2,128]{1,0:T(2,128)S(1)} %constant_dynamic-slice_fusion), channel_id=1, source_target_pairs={{0,4},{4,0},{8,12},{12,8},{16,20},{20,16},{24,28},{28,24},{1,5},{5... | collective-permute-start | bytes 3080 | tf_op jit(solution)/shard_map/ppermute | solution.py:20
  48.4 0.8 %collective-permute-done.15 = f32[2,256,128]{2,1,0:T(8,128)S(1)} collective-permute-done((f32[2,256,128]{2,1,0:T(8,128)S(1)}, f32[2,256,128]{2,1,0:T(8,128)S(1)}, u32[]{:S(2)}, u32[]{:S(2)}) %collective-permute-start.15) | collective-permute-done | bytes 262176 | tf_op jit(solution)/shard_map/ppermute | solution.py:20
  49.3 0.8 %pad_maximum_fusion.2 = f32[2,512,128]{2,1,0:T(8,128)} fusion(f32[2,256,128]{2,1,0:T(8,128)S(1)} %get-tuple-element.57, f32[2,256,128]{2,1,0:T(8,128)S(1)} %get-tuple-element.56), kind=kLoop, calls=%fused_computation.11 | loop fusion | flops 131072 | bytes 1048576 | tf_op jit(solution)/shard_map/concatenate | solution.py:316
  50.1 0.6 %add_multiply_fusion = f32[2,128]{1,0:T(2,128)} fusion(f32[2,128]{1,0:T(2,128)S(1)} %collective-permute-done.16, f32[4,128]{1,0:T(4,128)S(1)} %fusion.6, s32[]{:T(128)S(6)} %select_n.62), kind=kLoop, calls=%fused_computation.22 | loop fusion | flops 512 | bytes 3076 | tf_op jit(solution)/shard_map/div | solution.py:320
  (38 shorter events, 4.7 us)
Async XLA Ops:
  0.6 1.3 %copy-start = (bf16[2,512,512]{2,1,0:T(8,128)(2,1)S(1)}, bf16[2,512,512]{2,1,0:T(8,128)(2,1)}, u32[]{:S(2)}) copy-start(bf16[2,512,512]{2,1,0:T(8,128)(2,1)} %param.9) | copy-start | bytes 3145732
  1.9 2.1 %collective-permute-start = (bf16[2,256,512]{2,1,0:T(8,128)(2,1)S(1)}, bf16[2,256,512]{2,1,0:T(8,128)(2,1)S(1)}, u32[]{:S(2)}, u32[]{:S(2)}) collective-permute-start(bf16[2,256,512]{2,1,0:T(8,128)(2,1)S(1)} %constant_dynamic-slice_fusion.2), channel_id=1, source_target_pairs={{0,4},{4,0},{8,12},{12,8},{16,20},{20,16},{24,28},{28,24},{1,5},{5... | collective-permute-start | bytes 1572872 | tf_op jit(solution)/shard_map/ppermute | solution.py:20
  5.0 10.4 %collective-permute-start.1 = (s16[256,512]{1,0:T(8,128)(2,1)S(1)}, s16[256,512]{1,0:T(8,128)(2,1)S(1)}, u32[]{:S(2)}, u32[]{:S(2)}) collective-permute-start(s16[256,512]{1,0:T(8,128)(2,1)S(1)} %get-tuple-element.29), channel_id=1, source_target_pairs={{0,8},{4,12},{8,0},{12,4},{16,24},{20,28},{24,16},{28,20},{1,9},{5... | collective-permute-start | bytes 786440 | tf_op jit(solution)/shard_map/ppermute | solution.py:26
  11.9 9.3 %collective-permute-start.3 = (bf16[256,512]{1,0:T(8,128)(2,1)S(1)}, bf16[256,512]{1,0:T(8,128)(2,1)S(1)}, u32[]{:S(2)}, u32[]{:S(2)}) collective-permute-start(bf16[256,512]{1,0:T(8,128)(2,1)S(1)} %get-tuple-element.35), channel_id=1, source_target_pairs={{0,1},{1,0},{2,3},{3,2},{4,5},{5,4},{6,7},{7,6},{8,9},{9,8},{10,11... | collective-permute-start | bytes 786440 | tf_op jit(solution)/shard_map/ppermute | solution.py:37
  13.4 13.4 %collective-permute-start.4 = (bf16[256,512]{1,0:T(8,128)(2,1)S(1)}, bf16[256,512]{1,0:T(8,128)(2,1)S(1)}, u32[]{:S(2)}, u32[]{:S(2)}) collective-permute-start(bf16[256,512]{1,0:T(8,128)(2,1)S(1)} %get-tuple-element.36), channel_id=1, source_target_pairs={{0,2},{1,3},{2,0},{3,1},{4,6},{5,7},{6,4},{7,5},{8,10},{9,11},{10,... | collective-permute-start | bytes 786440 | tf_op jit(solution)/shard_map/ppermute | solution.py:37
  14.9 11.9 %collective-permute-start.5 = (bf16[256,512]{1,0:T(8,128)(2,1)S(1)}, bf16[256,512]{1,0:T(8,128)(2,1)S(1)}, u32[]{:S(2)}, u32[]{:S(2)}) collective-permute-start(bf16[256,512]{1,0:T(8,128)(2,1)S(1)} %get-tuple-element.37), channel_id=1, source_target_pairs={{0,3},{1,2},{2,1},{3,0},{4,7},{5,6},{6,5},{7,4},{8,11},{9,10},{10,... | collective-permute-start | bytes 786440 | tf_op jit(solution)/shard_map/ppermute | solution.py:37
  15.6 29.4 %copy-start.2 = (s32[128]{0:T(128)S(1)}, s32[128]{0:T(128)}, u32[]{:S(2)}) copy-start(s32[128]{0:T(128)} %param.17) | copy-start | bytes 1540
  15.7 13.8 %collective-permute-start.2 = (s16[256,512]{1,0:T(8,128)(2,1)S(1)}, s16[256,512]{1,0:T(8,128)(2,1)S(1)}, u32[]{:S(2)}, u32[]{:S(2)}) collective-permute-start(s16[256,512]{1,0:T(8,128)(2,1)S(1)} %round-nearest-even_convert_fusion), channel_id=1, source_target_pairs={{0,16},{4,20},{8,24},{12,28},{16,0},{20,4},{24,8},{28,12},{1,17},{... | collective-permute-start | bytes 786440 | tf_op jit(solution)/shard_map/ppermute | solution.py:26
  27.0 2.6 %collective-permute-start.6 = (bf16[256,512]{1,0:T(8,128)(2,1)S(1)}, bf16[256,512]{1,0:T(8,128)(2,1)S(1)}, u32[]{:S(2)}, u32[]{:S(2)}) collective-permute-start(bf16[256,512]{1,0:T(8,128)(2,1)S(1)} %get-tuple-element.55.refs_0_), channel_id=1, source_target_pairs={{0,4},{4,0},{8,12},{12,8},{16,20},{20,16},{24,28},{28,24},{1,5},{5... | collective-permute-start | bytes 786440 | tf_op jit(solution)/shard_map/ppermute | solution.py:20
  27.1 2.6 %collective-permute-start.7 = (bf16[256,512]{1,0:T(8,128)(2,1)S(1)}, bf16[256,512]{1,0:T(8,128)(2,1)S(1)}, u32[]{:S(2)}, u32[]{:S(2)}) collective-permute-start(bf16[256,512]{1,0:T(8,128)(2,1)S(1)} %get-tuple-element.54.refs_1_), channel_id=1, source_target_pairs={{0,4},{4,0},{8,12},{12,8},{16,20},{20,16},{24,28},{28,24},{1,5},{5... | collective-permute-start | bytes 786440 | tf_op jit(solution)/shard_map/ppermute | solution.py:20
  29.5 18.3 %copy-start.1 = (f32[128]{0:T(128)S(1)}, f32[128]{0:T(128)}, u32[]{:S(2)}) copy-start(f32[128]{0:T(128)} %param.16) | copy-start | bytes 1540
  32.3 7.4 %collective-permute-start.10 = (bf16[512,128]{1,0:T(8,128)(2,1)S(1)}, bf16[512,128]{1,0:T(8,128)(2,1)S(1)}, u32[]{:S(2)}, u32[]{:S(2)}) collective-permute-start(bf16[512,128]{1,0:T(8,128)(2,1)S(1)} %get-tuple-element.42), channel_id=1, source_target_pairs={{0,3},{1,2},{2,1},{3,0},{4,7},{5,6},{6,5},{7,4},{8,11},{9,10},{10,... | collective-permute-start | bytes 393224 | tf_op jit(solution)/shard_map/ppermute | solution.py:37
  34.8 7.8 %collective-permute-start.8 = (bf16[512,128]{1,0:T(8,128)(2,1)S(1)}, bf16[512,128]{1,0:T(8,128)(2,1)S(1)}, u32[]{:S(2)}, u32[]{:S(2)}) collective-permute-start(bf16[512,128]{1,0:T(8,128)(2,1)S(1)} %get-tuple-element.40), channel_id=1, source_target_pairs={{0,1},{1,0},{2,3},{3,2},{4,5},{5,4},{6,7},{7,6},{8,9},{9,8},{10,11... | collective-permute-start | bytes 393224 | tf_op jit(solution)/shard_map/ppermute | solution.py:37
  35.4 7.2 %collective-permute-start.9 = (bf16[512,128]{1,0:T(8,128)(2,1)S(1)}, bf16[512,128]{1,0:T(8,128)(2,1)S(1)}, u32[]{:S(2)}, u32[]{:S(2)}) collective-permute-start(bf16[512,128]{1,0:T(8,128)(2,1)S(1)} %get-tuple-element.41), channel_id=1, source_target_pairs={{0,2},{1,3},{2,0},{3,1},{4,6},{5,7},{6,4},{7,5},{8,10},{9,11},{10,... | collective-permute-start | bytes 393224 | tf_op jit(solution)/shard_map/ppermute | solution.py:37
  35.9 11.6 %collective-permute-start.12 = (bf16[512,128]{1,0:T(8,128)(2,1)S(1)}, bf16[512,128]{1,0:T(8,128)(2,1)S(1)}, u32[]{:S(2)}, u32[]{:S(2)}) collective-permute-start(bf16[512,128]{1,0:T(8,128)(2,1)S(1)} %get-tuple-element.44), channel_id=1, source_target_pairs={{0,1},{1,0},{2,3},{3,2},{4,5},{5,4},{6,7},{7,6},{8,9},{9,8},{10,11... | collective-permute-start | bytes 393224 | tf_op jit(solution)/shard_map/ppermute | solution.py:37
  37.4 10.1 %collective-permute-start.13 = (bf16[512,128]{1,0:T(8,128)(2,1)S(1)}, bf16[512,128]{1,0:T(8,128)(2,1)S(1)}, u32[]{:S(2)}, u32[]{:S(2)}) collective-permute-start(bf16[512,128]{1,0:T(8,128)(2,1)S(1)} %get-tuple-element.45), channel_id=1, source_target_pairs={{0,2},{1,3},{2,0},{3,1},{4,6},{5,7},{6,4},{7,5},{8,10},{9,11},{10,... | collective-permute-start | bytes 393224 | tf_op jit(solution)/shard_map/ppermute | solution.py:37
  39.7 7.8 %collective-permute-start.14 = (bf16[512,128]{1,0:T(8,128)(2,1)S(1)}, bf16[512,128]{1,0:T(8,128)(2,1)S(1)}, u32[]{:S(2)}, u32[]{:S(2)}) collective-permute-start(bf16[512,128]{1,0:T(8,128)(2,1)S(1)} %get-tuple-element.46), channel_id=1, source_target_pairs={{0,3},{1,2},{2,1},{3,0},{4,7},{5,6},{6,5},{7,4},{8,11},{9,10},{10,... | collective-permute-start | bytes 393224 | tf_op jit(solution)/shard_map/ppermute | solution.py:37
  42.7 4.8 %collective-permute-start.11 = (bf16[2,256,128]{2,1,0:T(8,128)(2,1)S(1)}, bf16[2,256,128]{2,1,0:T(8,128)(2,1)S(1)}, u32[]{:S(2)}, u32[]{:S(2)}) collective-permute-start(bf16[2,256,128]{2,1,0:T(8,128)(2,1)S(1)} %get-tuple-element.52), channel_id=1, source_target_pairs={{0,8},{4,12},{8,16},{12,20},{16,24},{20,28},{1,9},{5,13},{9,17},{1... | collective-permute-start | bytes 393224 | tf_op jit(solution)/shard_map/ppermute | solution.py:31
  47.6 1.6 %collective-permute-start.15 = (f32[2,256,128]{2,1,0:T(8,128)S(1)}, f32[2,256,128]{2,1,0:T(8,128)S(1)}, u32[]{:S(2)}, u32[]{:S(2)}) collective-permute-start(f32[2,256,128]{2,1,0:T(8,128)S(1)} %broadcast_select_fusion.2), channel_id=1, source_target_pairs={{0,4},{4,0},{8,12},{12,8},{16,20},{20,16},{24,28},{28,24},{1,5},{5... | collective-permute-start | bytes 786440 | tf_op jit(solution)/shard_map/ppermute | solution.py:20
  47.9 2.2 %collective-permute-start.16 = (f32[2,128]{1,0:T(2,128)S(1)}, f32[2,128]{1,0:T(2,128)S(1)}, u32[]{:S(2)}, u32[]{:S(2)}) collective-permute-start(f32[2,128]{1,0:T(2,128)S(1)} %constant_dynamic-slice_fusion), channel_id=1, source_target_pairs={{0,4},{4,0},{8,12},{12,8},{16,20},{20,16},{24,28},{28,24},{1,5},{5... | collective-permute-start | bytes 3080 | tf_op jit(solution)/shard_map/ppermute | solution.py:20

commit v6 on v4

--- a/solution.py
+++ b/solution.py
@@ -72,7 +72,7 @@
 def weights(here, owners, trade_set, cashflows, books):
     blocks = owners.shape[0]
     trades, width = cashflows.shape
-    per = 4 if blocks % 4 == 0 else 1
+    per = 8 if blocks % 8 == 0 else 1
     half = SETS // CORES
     whole = pl.BlockSpec(memory_space=pltpu.VMEM)
     scalars = pl.BlockSpec(memory_space=pltpu.SMEM)
@@ -126,19 +126,24 @@
         target = low if i % 2 else high
         target[pl.ds(pl.multiple_of(place * half, half), half), :] = source[...]
 
-    def walk(i, _):
+    def walk(first, second, i, _):
         at = pl.ds(i * tile, tile)
         pers, vol, base = par_ref[0:1, :], par_ref[1:2, :], par_ref[2:3, :]
         state = start_ref[at, :]
         for t in range(2 * dates):
-            kept = kept_ref[t % dates, at, :].astype(jnp.float32)
-            got = got_ref[t % dates, at, :].astype(jnp.float32)
-            shock = jnp.where(core == 0, kept, got) if t < dates else jnp.where(core == 0, got, kept)
-            state = pers * state + vol * shock
+            source = first if t < dates else second
+            state = pers * state + vol * source[t % dates, at, :].astype(jnp.float32)
             disc[pl.ds(t * paths + i * tile, tile), :] = jnp.exp(-(base + state)).astype(jnp.bfloat16)
         return 0
 
-    lax.fori_loop(0, paths // tile, walk, 0)
+    @pl.when(core == 0)
+    def _():
+        lax.fori_loop(0, paths // tile, functools.partial(walk, kept_ref, got_ref), 0)
+
+    @pl.when(core != 0)
+    def _():
+        lax.fori_loop(0, paths // tile, functools.partial(walk, got_ref, kept_ref), 0)
+
     rows = dates * paths
     price_rows(books, disc.at[rows:], high, low, outs[:books])
     price_rows(books, disc.at[:rows], high, low, outs[books:])
@@ -193,19 +198,24 @@
     tile = 32
     scale = rows_ref[0:1, :]
 
-    def walk(i, _):
+    def walk(first, second, i, _):
         at = pl.ds(i * tile, tile)
         state = jnp.zeros((tile, pers.shape[1]), jnp.float32)
         for t in range(2 * dates):
-            kept = kept_ref[t % dates, at, :].astype(jnp.float32)
-            got = got_ref[t % dates, at, :].astype(jnp.float32)
-            shock = jnp.where(core == 0, kept, got) if t < dates else jnp.where(core == 0, got, kept)
-            state = pers * state + vol * shock
+            source = first if t < dates else second
+            state = pers * state + source[t % dates, at, :].astype(jnp.float32)
+        state = vol * state
         group_ref[at, :] = state
         code_ref[at, :] = jnp.round(state * scale).astype(jnp.int16)
         return 0
 
-    lax.fori_loop(0, paths // tile, walk, 0)
+    @pl.when(core == 0)
+    def _():
+        lax.fori_loop(0, paths // tile, functools.partial(walk, kept_ref, got_ref), 0)
+
+    @pl.when(core != 0)
+    def _():
+        lax.fori_loop(0, paths // tile, functools.partial(walk, got_ref, kept_ref), 0)
 
 
 def first_code(here, par, kept, got, chips):
@@ -279,6 +289,7 @@
         group = ours * group + theirs * after(came, mats[0]).astype(jnp.float32)
         reach, count = 2 * reach, count + 1
 
+    kept = side(after(shocks, code), core, 1)
     mine = after(mats[0], code)
     for arrived in mats_arrived:
         mine = mine + arrived.astype(jnp.float32)
@@ -312,7 +323,6 @@
         )
     exposed = jnp.sum(jnp.maximum(now - collateral - threshold[None, None, :], 0.0), axis=1)
     exposed_got = swap(side(exposed, 1 - core, 0))
-    net_kept = after(net_kept, exposed)
     net_value = jnp.concatenate(
         [jnp.where(core == 0, net_kept, net_got), jnp.where(core == 0, net_got, net_kept)], 1
     )

time: 52.2 us -> 50.2 us (0.962)
  other arithmetic: 4.91 us -> 3.23 us
    ppermute x2, waiting for transfers between devices: 2.82 us -> 1.83 us  [across(): return lax.ppermute(block, 'date', [(i, i ^ hop) for i in range(n)])]
    add x1, other arithmetic: 1.15 us -> 0.19 us  [on_device(): start = start + rate * came.astype(jnp.float32)]
    ppermute x9, waiting for transfers between devices: 10.7 us -> 11.5 us  [exchange(): lax.ppermute(slots[i], 'book', [(j, j ^ i) for j in range(n)])]
    convert_element_type x1, other arithmetic: 0.91 us -> 0.21 us  [on_device(): code = jnp.round(group * scale).astype(jnp.int16)]
  transfers between devices with their start and end apart: 17 -> 17, of which waited for: 10 -> 10; matrix products, arithmetic and copies ran while one was open for 8% -> 5% of each run, Pallas kernels for 7% -> 8%
where the time goes in v6:
time: 50.2 us; the launch traced here: 49.6 us
  starting transfers between devices  21.8 us (43%)
  waiting for transfers between devices  15.3 us (30%)
  Pallas kernels  7.28 us (15%)
  other arithmetic  3.23 us (6%)
  local copies, waits for them, and re-layouts  1.29 us (3%)
  between operations  0.83 us (2%)
    ppermute x9, starting transfers between devices, exchange(): lax.ppermute(slots[i], 'book', [(j, j ^ i) for j in range(n)])  12.6 us
    ppermute x9, waiting for transfers between devices, exchange(): lax.ppermute(slots[i], 'book', [(j, j ^ i) for j in range(n)])  11.5 us
    ppermute x2, starting transfers between devices, across(): return lax.ppermute(block, 'date', [(i, i ^ hop) for i in range(n)])  5.66 us
    pallas_call x1, Pallas kernels, weights(): pl.pallas_call(functools.partial(weights_kernel, books, per), in_specs=[s...  3.82 us
    pallas_call x1, Pallas kernels, values(): pl.pallas_call(functools.partial(values_kernel, books), in_specs=[pl.Bloc...  2.56 us
    ppermute x1, starting transfers between devices, later(): lax.ppermute(block, 'date', [(i, i + CORES) for i in range(n - CORES)])  2.31 us
    ppermute x2, waiting for transfers between devices, across(): return lax.ppermute(block, 'date', [(i, i ^ hop) for i in range(n)])  1.83 us
    ppermute x5, waiting for transfers between devices, swap(): return lax.ppermute(block, 'date', [(i, i ^ 1) for i in range(n)])  1.34 us
  transfers between devices with their start and end apart: 17, of which 10 were waited for; matrix products, arithmetic and copies ran while one was open for 5% of the time, Pallas kernels for 8%

profile of v6, /device:TPU:0, one launch (start us, length us, event | category | flops | bytes accessed | tf_op | source)
XLA Modules:
  0.0 49.6 jit_solution(7128534334408833826)
XLA Ops:
  0.7 0.8 %pad_maximum_fusion.3.par_ref = f32[3,512]{1,0:T(4,128)S(1)} fusion(f32[1,512]{1,0:T(1,128)} %bitcast.28, f32[1,512]{1,0:T(1,128)} %bitcast.29, f32[1,512]{1,0:T(1,128)} %bitcast.30), kind=kLoop, calls=%fused_computation.21 | loop fusion | flops 3072 | bytes 12288 | tf_op jit(solution)/shard_map/stack | solution.py:272
  2.5 0.7 %reshape.18.sets_ref = s32[16,256]{1,0:T(8,128)S(1)} reshape(s32[4096]{0:T(1024)} %param.15) | data formatting | bytes 32768 | tf_op jit(solution)/shard_map/reshape | solution.py:100
  3.3 0.7 %collective-permute-done.got_ref = bf16[2,256,512]{2,1,0:T(8,128)(2,1)S(1)} collective-permute-done((bf16[2,256,512]{2,1,0:T(8,128)(2,1)S(1)}, bf16[2,256,512]{2,1,0:T(8,128)(2,1)S(1)}, u32[]{:S(2)}, u32[]{:S(2)}) %collective-permute-start) | collective-permute-done | bytes 524320 | tf_op jit(solution)/shard_map/ppermute | solution.py:20
  4.0 0.9 %first_code.1 = (s16[256,512]{1,0:T(8,128)(2,1)S(1)}, f32[256,512]{1,0:T(8,128)S(1)}, f32[8,512]{1,0:T(8,128)S(1)}) custom-call(s32[3]{0:T(128)S(1)} %pad_add_fusion.here_ref, f32[3,512]{1,0:T(4,128)S(1)} %pad_maximum_fusion.3.par_ref, bf16[2,256,512]{2,1,0:T(8,128)(2,1)S(1)} %constant_dynamic-slice_fusion.3.kept_ref, ...), custom_call_target="tpu_custom_call" | custom-call | flops 2097152 | bytes 2097152 | tf_op jit(solution)/shard_map/first_code/pallas_call | solution.py:225
  4.9 3.0 %collective-permute-start.1 = (s16[256,512]{1,0:T(8,128)(2,1)S(1)}, s16[256,512]{1,0:T(8,128)(2,1)S(1)}, u32[]{:S(2)}, u32[]{:S(2)}) collective-permute-start(s16[256,512]{1,0:T(8,128)(2,1)S(1)} %get-tuple-element.30), channel_id=1, source_target_pairs={{0,8},{4,12},{8,0},{12,4},{16,24},{20,28},{24,16},{28,20},{1,9},{5... | collective-permute-start | bytes 786440 | tf_op jit(solution)/shard_map/ppermute | solution.py:26
  7.9 3.8 %weights.1 = (f32[256,512]{1,0:T(8,128)S(1)}, bf16[256,512]{1,0:T(8,128)(2,1)S(1)}, bf16[256,512]{1,0:T(8,128)(2,1)S(1)}, bf16[256,512]{1,0:T(8,128)(2,1)S(1)}) custom-call(s32[3]{0:T(128)S(1)} %pad_add_fusion.here_ref, s32[16]{0:T(128)} %bitcast.31, s32[16,256]{1,0:T(8,128)S(1)} %reshape.18.sets_ref, bf16[4096,512]{1,0:T(8,128)(2,1)} %flows_hbm.1), custom_call_target="tpu_custom_call" | custom-call | flops 1073741824 | bytes 4194304 | tf_op jit(solution)/shard_map/weights/pallas_call | solution.py:79
  11.8 1.6 %collective-permute-start.3 = (bf16[256,512]{1,0:T(8,128)(2,1)S(1)}, bf16[256,512]{1,0:T(8,128)(2,1)S(1)}, u32[]{:S(2)}, u32[]{:S(2)}) collective-permute-start(bf16[256,512]{1,0:T(8,128)(2,1)S(1)} %get-tuple-element.36), channel_id=1, source_target_pairs={{0,1},{1,0},{2,3},{3,2},{4,5},{5,4},{6,7},{7,6},{8,9},{9,8},{10,11... | collective-permute-start | bytes 786440 | tf_op jit(solution)/shard_map/ppermute | solution.py:37
  13.3 1.5 %collective-permute-start.4 = (bf16[256,512]{1,0:T(8,128)(2,1)S(1)}, bf16[256,512]{1,0:T(8,128)(2,1)S(1)}, u32[]{:S(2)}, u32[]{:S(2)}) collective-permute-start(bf16[256,512]{1,0:T(8,128)(2,1)S(1)} %get-tuple-element.37), channel_id=1, source_target_pairs={{0,2},{1,3},{2,0},{3,1},{4,6},{5,7},{6,4},{7,5},{8,10},{9,11},{10,... | collective-permute-start | bytes 786440 | tf_op jit(solution)/shard_map/ppermute | solution.py:37
  15.6 2.7 %collective-permute-start.2 = (s16[256,512]{1,0:T(8,128)(2,1)S(1)}, s16[256,512]{1,0:T(8,128)(2,1)S(1)}, u32[]{:S(2)}, u32[]{:S(2)}) collective-permute-start(s16[256,512]{1,0:T(8,128)(2,1)S(1)} %round-nearest-even_convert_fusion), channel_id=1, source_target_pairs={{0,16},{4,20},{8,24},{12,28},{16,0},{20,4},{24,8},{28,12},{1,17},{... | collective-permute-start | bytes 786440 | tf_op jit(solution)/shard_map/ppermute | solution.py:26
  18.2 2.8 %collective-permute-done.3 = bf16[256,512]{1,0:T(8,128)(2,1)S(1)} collective-permute-done((bf16[256,512]{1,0:T(8,128)(2,1)S(1)}, bf16[256,512]{1,0:T(8,128)(2,1)S(1)}, u32[]{:S(2)}, u32[]{:S(2)}) %collective-permute-start.3) | collective-permute-done | bytes 262176 | tf_op jit(solution)/shard_map/ppermute | solution.py:37
  21.0 5.7 %collective-permute-done.4 = bf16[256,512]{1,0:T(8,128)(2,1)S(1)} collective-permute-done((bf16[256,512]{1,0:T(8,128)(2,1)S(1)}, bf16[256,512]{1,0:T(8,128)(2,1)S(1)}, u32[]{:S(2)}, u32[]{:S(2)}) %collective-permute-start.4) | collective-permute-done | bytes 262176 | tf_op jit(solution)/shard_map/ppermute | solution.py:37
  27.5 1.8 %collective-permute-done.2 = s16[256,512]{1,0:T(8,128)(2,1)S(1)} collective-permute-done((s16[256,512]{1,0:T(8,128)(2,1)S(1)}, s16[256,512]{1,0:T(8,128)(2,1)S(1)}, u32[]{:S(2)}, u32[]{:S(2)}) %collective-permute-start.2) | collective-permute-done | bytes 262176 | tf_op jit(solution)/shard_map/ppermute | solution.py:26
  29.6 2.6 %values.1 = (f32[512,128]{1,0:T(8,128)S(1)}, bf16[512,128]{1,0:T(8,128)(2,1)S(1)}, bf16[512,128]{1,0:T(8,128)(2,1)S(1)}, bf16[512,128]{1,0:T(8,128)(2,1)S(1)}, f...) custom-call(s32[3]{0:T(128)S(1)} %pad_add_fusion.here_ref, ...), custom_call_target="tpu_custom_call" | custom-call | flops 1073741824 | bytes 2097152 | tf_op jit(solution)/shard_map/values/pallas_call | solution.py:156
  32.1 2.5 %collective-permute-start.10 = (bf16[512,128]{1,0:T(8,128)(2,1)S(1)}, bf16[512,128]{1,0:T(8,128)(2,1)S(1)}, u32[]{:S(2)}, u32[]{:S(2)}) collective-permute-start(bf16[512,128]{1,0:T(8,128)(2,1)S(1)} %get-tuple-element.43), channel_id=1, source_target_pairs={{0,3},{1,2},{2,1},{3,0},{4,7},{5,6},{6,5},{7,4},{8,11},{9,10},{10,... | collective-permute-start | bytes 393224 | tf_op jit(solution)/shard_map/ppermute | solution.py:37
  35.7 1.5 %collective-permute-start.11 = (bf16[512,128]{1,0:T(8,128)(2,1)S(1)}, bf16[512,128]{1,0:T(8,128)(2,1)S(1)}, u32[]{:S(2)}, u32[]{:S(2)}) collective-permute-start(bf16[512,128]{1,0:T(8,128)(2,1)S(1)} %get-tuple-element.45), channel_id=1, source_target_pairs={{0,1},{1,0},{2,3},{3,2},{4,5},{5,4},{6,7},{7,6},{8,9},{9,8},{10,11... | collective-permute-start | bytes 393224 | tf_op jit(solution)/shard_map/ppermute | solution.py:37
  37.2 1.5 %collective-permute-start.12 = (bf16[512,128]{1,0:T(8,128)(2,1)S(1)}, bf16[512,128]{1,0:T(8,128)(2,1)S(1)}, u32[]{:S(2)}, u32[]{:S(2)}) collective-permute-start(bf16[512,128]{1,0:T(8,128)(2,1)S(1)} %get-tuple-element.46), channel_id=1, source_target_pairs={{0,2},{1,3},{2,0},{3,1},{4,6},{5,7},{6,4},{7,5},{8,10},{9,11},{10,... | collective-permute-start | bytes 393224 | tf_op jit(solution)/shard_map/ppermute | solution.py:37
  38.7 0.8 %collective-permute-done.10 = bf16[512,128]{1,0:T(8,128)(2,1)S(1)} collective-permute-done((bf16[512,128]{1,0:T(8,128)(2,1)S(1)}, bf16[512,128]{1,0:T(8,128)(2,1)S(1)}, u32[]{:S(2)}, u32[]{:S(2)}) %collective-permute-start.10) | collective-permute-done | bytes 131104 | tf_op jit(solution)/shard_map/ppermute | solution.py:37
  39.5 2.4 %collective-permute-start.13 = (bf16[512,128]{1,0:T(8,128)(2,1)S(1)}, bf16[512,128]{1,0:T(8,128)(2,1)S(1)}, u32[]{:S(2)}, u32[]{:S(2)}) collective-permute-start(bf16[512,128]{1,0:T(8,128)(2,1)S(1)} %get-tuple-element.47), channel_id=1, source_target_pairs={{0,3},{1,2},{2,1},{3,0},{4,7},{5,6},{6,5},{7,4},{8,11},{9,10},{10,... | collective-permute-start | bytes 393224 | tf_op jit(solution)/shard_map/ppermute | solution.py:37
  42.5 2.3 %collective-permute-start.15 = (bf16[2,256,128]{2,1,0:T(8,128)(2,1)S(1)}, bf16[2,256,128]{2,1,0:T(8,128)(2,1)S(1)}, u32[]{:S(2)}, u32[]{:S(2)}) collective-permute-start(bf16[2,256,128]{2,1,0:T(8,128)(2,1)S(1)} %get-tuple-element.50), channel_id=1, source_target_pairs={{0,8},{4,12},{8,16},{12,20},{16,24},{20,28},{1,9},{5,13},{9,17},{1... | collective-permute-start | bytes 393224 | tf_op jit(solution)/shard_map/ppermute | solution.py:31
  45.0 1.5 %collective-permute-done.12 = bf16[512,128]{1,0:T(8,128)(2,1)S(1)} collective-permute-done((bf16[512,128]{1,0:T(8,128)(2,1)S(1)}, bf16[512,128]{1,0:T(8,128)(2,1)S(1)}, u32[]{:S(2)}, u32[]{:S(2)}) %collective-permute-start.12) | collective-permute-done | bytes 131104 | tf_op jit(solution)/shard_map/ppermute | solution.py:37
  46.7 0.6 %collective-permute-done.15 = bf16[2,256,128]{2,1,0:T(8,128)(2,1)S(1)} collective-permute-done((bf16[2,256,128]{2,1,0:T(8,128)(2,1)S(1)}, bf16[2,256,128]{2,1,0:T(8,128)(2,1)S(1)}, u32[]{:S(2)}, u32[]{:S(2)}) %collective-permute-start.15) | collective-permute-done | bytes 131104 | tf_op jit(solution)/shard_map/ppermute | solution.py:31
  47.5 0.6 %collective-permute-done.14 = f32[2,256,128]{2,1,0:T(8,128)S(1)} collective-permute-done((f32[2,256,128]{2,1,0:T(8,128)S(1)}, f32[2,256,128]{2,1,0:T(8,128)S(1)}, u32[]{:S(2)}, u32[]{:S(2)}) %collective-permute-start.14) | collective-permute-done | bytes 262176 | tf_op jit(solution)/shard_map/ppermute | solution.py:20
  48.2 0.8 %pad_maximum_fusion.2 = f32[2,512,128]{2,1,0:T(8,128)} fusion(f32[2,256,128]{2,1,0:T(8,128)S(1)} %get-tuple-element.57, f32[2,256,128]{2,1,0:T(8,128)S(1)} %get-tuple-element.56), kind=kLoop, calls=%fused_computation.11 | loop fusion | flops 131072 | bytes 1048576 | tf_op jit(solution)/shard_map/concatenate | solution.py:326
  49.1 0.6 %fusion.8 = f32[2,128]{1,0:T(2,128)} fusion(f32[2,128]{1,0:T(2,128)S(1)} %collective-permute-done.16, f32[4,128]{1,0:T(4,128)S(1)} %fusion.6, s32[]{:T(128)S(6)} %select_n.63), kind=kLoop, calls=%fused_computation.28 | loop fusion | flops 512 | bytes 3076 | tf_op jit(solution)/shard_map/div | solution.py:330
  (38 shorter events, 5.0 us)
Async XLA Ops:
  0.6 1.3 %copy-start = (bf16[2,512,512]{2,1,0:T(8,128)(2,1)S(1)}, bf16[2,512,512]{2,1,0:T(8,128)(2,1)}, u32[]{:S(2)}) copy-start(bf16[2,512,512]{2,1,0:T(8,128)(2,1)} %param.9) | copy-start | bytes 3145732
  1.9 2.1 %collective-permute-start = (bf16[2,256,512]{2,1,0:T(8,128)(2,1)S(1)}, bf16[2,256,512]{2,1,0:T(8,128)(2,1)S(1)}, u32[]{:S(2)}, u32[]{:S(2)}) collective-permute-start(bf16[2,256,512]{2,1,0:T(8,128)(2,1)S(1)} %constant_dynamic-slice_fusion.4), channel_id=1, source_target_pairs={{0,4},{4,0},{8,12},{12,8},{16,20},{20,16},{24,28},{28,24},{1,5},{5... | collective-permute-start | bytes 1572872 | tf_op jit(solution)/shard_map/ppermute | solution.py:20
  4.9 10.4 %collective-permute-start.1 = (s16[256,512]{1,0:T(8,128)(2,1)S(1)}, s16[256,512]{1,0:T(8,128)(2,1)S(1)}, u32[]{:S(2)}, u32[]{:S(2)}) collective-permute-start(s16[256,512]{1,0:T(8,128)(2,1)S(1)} %get-tuple-element.30), channel_id=1, source_target_pairs={{0,8},{4,12},{8,0},{12,4},{16,24},{20,28},{24,16},{28,20},{1,9},{5... | collective-permute-start | bytes 786440 | tf_op jit(solution)/shard_map/ppermute | solution.py:26
  11.8 9.3 %collective-permute-start.3 = (bf16[256,512]{1,0:T(8,128)(2,1)S(1)}, bf16[256,512]{1,0:T(8,128)(2,1)S(1)}, u32[]{:S(2)}, u32[]{:S(2)}) collective-permute-start(bf16[256,512]{1,0:T(8,128)(2,1)S(1)} %get-tuple-element.36), channel_id=1, source_target_pairs={{0,1},{1,0},{2,3},{3,2},{4,5},{5,4},{6,7},{7,6},{8,9},{9,8},{10,11... | collective-permute-start | bytes 786440 | tf_op jit(solution)/shard_map/ppermute | solution.py:37
  13.3 13.4 %collective-permute-start.4 = (bf16[256,512]{1,0:T(8,128)(2,1)S(1)}, bf16[256,512]{1,0:T(8,128)(2,1)S(1)}, u32[]{:S(2)}, u32[]{:S(2)}) collective-permute-start(bf16[256,512]{1,0:T(8,128)(2,1)S(1)} %get-tuple-element.37), channel_id=1, source_target_pairs={{0,2},{1,3},{2,0},{3,1},{4,6},{5,7},{6,4},{7,5},{8,10},{9,11},{10,... | collective-permute-start | bytes 786440 | tf_op jit(solution)/shard_map/ppermute | solution.py:37
  14.8 11.9 %collective-permute-start.5 = (bf16[256,512]{1,0:T(8,128)(2,1)S(1)}, bf16[256,512]{1,0:T(8,128)(2,1)S(1)}, u32[]{:S(2)}, u32[]{:S(2)}) collective-permute-start(bf16[256,512]{1,0:T(8,128)(2,1)S(1)} %get-tuple-element.38), channel_id=1, source_target_pairs={{0,3},{1,2},{2,1},{3,0},{4,7},{5,6},{6,5},{7,4},{8,11},{9,10},{10,... | collective-permute-start | bytes 786440 | tf_op jit(solution)/shard_map/ppermute | solution.py:37
  15.5 20.2 %copy-start.2 = (s32[128]{0:T(128)S(1)}, s32[128]{0:T(128)}, u32[]{:S(2)}) copy-start(s32[128]{0:T(128)} %param.17) | copy-start | bytes 1540
  15.6 13.8 %collective-permute-start.2 = (s16[256,512]{1,0:T(8,128)(2,1)S(1)}, s16[256,512]{1,0:T(8,128)(2,1)S(1)}, u32[]{:S(2)}, u32[]{:S(2)}) collective-permute-start(s16[256,512]{1,0:T(8,128)(2,1)S(1)} %round-nearest-even_convert_fusion), channel_id=1, source_target_pairs={{0,16},{4,20},{8,24},{12,28},{16,0},{20,4},{24,8},{28,12},{1,17},{... | collective-permute-start | bytes 786440 | tf_op jit(solution)/shard_map/ppermute | solution.py:26
  26.9 2.6 %collective-permute-start.6 = (bf16[256,512]{1,0:T(8,128)(2,1)S(1)}, bf16[256,512]{1,0:T(8,128)(2,1)S(1)}, u32[]{:S(2)}, u32[]{:S(2)}) collective-permute-start(bf16[256,512]{1,0:T(8,128)(2,1)S(1)} %get-tuple-element.55.refs_0_), channel_id=1, source_target_pairs={{0,4},{4,0},{8,12},{12,8},{16,20},{20,16},{24,28},{28,24},{1,5},{5... | collective-permute-start | bytes 786440 | tf_op jit(solution)/shard_map/ppermute | solution.py:20
  27.0 2.6 %collective-permute-start.7 = (bf16[256,512]{1,0:T(8,128)(2,1)S(1)}, bf16[256,512]{1,0:T(8,128)(2,1)S(1)}, u32[]{:S(2)}, u32[]{:S(2)}) collective-permute-start(bf16[256,512]{1,0:T(8,128)(2,1)S(1)} %get-tuple-element.54.refs_1_), channel_id=1, source_target_pairs={{0,4},{4,0},{8,12},{12,8},{16,20},{20,16},{24,28},{28,24},{1,5},{5... | collective-permute-start | bytes 786440 | tf_op jit(solution)/shard_map/ppermute | solution.py:20
  27.5 19.8 %copy-start.1 = (f32[128]{0:T(128)S(1)}, f32[128]{0:T(128)}, u32[]{:S(2)}) copy-start(f32[128]{0:T(128)} %param.16) | copy-start | bytes 1540
  32.1 7.4 %collective-permute-start.10 = (bf16[512,128]{1,0:T(8,128)(2,1)S(1)}, bf16[512,128]{1,0:T(8,128)(2,1)S(1)}, u32[]{:S(2)}, u32[]{:S(2)}) collective-permute-start(bf16[512,128]{1,0:T(8,128)(2,1)S(1)} %get-tuple-element.43), channel_id=1, source_target_pairs={{0,3},{1,2},{2,1},{3,0},{4,7},{5,6},{6,5},{7,4},{8,11},{9,10},{10,... | collective-permute-start | bytes 393224 | tf_op jit(solution)/shard_map/ppermute | solution.py:37
  34.7 7.8 %collective-permute-start.8 = (bf16[512,128]{1,0:T(8,128)(2,1)S(1)}, bf16[512,128]{1,0:T(8,128)(2,1)S(1)}, u32[]{:S(2)}, u32[]{:S(2)}) collective-permute-start(bf16[512,128]{1,0:T(8,128)(2,1)S(1)} %get-tuple-element.41), channel_id=1, source_target_pairs={{0,1},{1,0},{2,3},{3,2},{4,5},{5,4},{6,7},{7,6},{8,9},{9,8},{10,11... | collective-permute-start | bytes 393224 | tf_op jit(solution)/shard_map/ppermute | solution.py:37
  35.2 7.2 %collective-permute-start.9 = (bf16[512,128]{1,0:T(8,128)(2,1)S(1)}, bf16[512,128]{1,0:T(8,128)(2,1)S(1)}, u32[]{:S(2)}, u32[]{:S(2)}) collective-permute-start(bf16[512,128]{1,0:T(8,128)(2,1)S(1)} %get-tuple-element.42), channel_id=1, source_target_pairs={{0,2},{1,3},{2,0},{3,1},{4,6},{5,7},{6,4},{7,5},{8,10},{9,11},{10,... | collective-permute-start | bytes 393224 | tf_op jit(solution)/shard_map/ppermute | solution.py:37
  35.7 9.3 %collective-permute-start.11 = (bf16[512,128]{1,0:T(8,128)(2,1)S(1)}, bf16[512,128]{1,0:T(8,128)(2,1)S(1)}, u32[]{:S(2)}, u32[]{:S(2)}) collective-permute-start(bf16[512,128]{1,0:T(8,128)(2,1)S(1)} %get-tuple-element.45), channel_id=1, source_target_pairs={{0,1},{1,0},{2,3},{3,2},{4,5},{5,4},{6,7},{7,6},{8,9},{9,8},{10,11... | collective-permute-start | bytes 393224 | tf_op jit(solution)/shard_map/ppermute | solution.py:37
  37.2 9.3 %collective-permute-start.12 = (bf16[512,128]{1,0:T(8,128)(2,1)S(1)}, bf16[512,128]{1,0:T(8,128)(2,1)S(1)}, u32[]{:S(2)}, u32[]{:S(2)}) collective-permute-start(bf16[512,128]{1,0:T(8,128)(2,1)S(1)} %get-tuple-element.46), channel_id=1, source_target_pairs={{0,2},{1,3},{2,0},{3,1},{4,6},{5,7},{6,4},{7,5},{8,10},{9,11},{10,... | collective-permute-start | bytes 393224 | tf_op jit(solution)/shard_map/ppermute | solution.py:37
  39.5 6.9 %collective-permute-start.13 = (bf16[512,128]{1,0:T(8,128)(2,1)S(1)}, bf16[512,128]{1,0:T(8,128)(2,1)S(1)}, u32[]{:S(2)}, u32[]{:S(2)}) collective-permute-start(bf16[512,128]{1,0:T(8,128)(2,1)S(1)} %get-tuple-element.47), channel_id=1, source_target_pairs={{0,3},{1,2},{2,1},{3,0},{4,7},{5,6},{6,5},{7,4},{8,11},{9,10},{10,... | collective-permute-start | bytes 393224 | tf_op jit(solution)/shard_map/ppermute | solution.py:37
  42.5 4.8 %collective-permute-start.15 = (bf16[2,256,128]{2,1,0:T(8,128)(2,1)S(1)}, bf16[2,256,128]{2,1,0:T(8,128)(2,1)S(1)}, u32[]{:S(2)}, u32[]{:S(2)}) collective-permute-start(bf16[2,256,128]{2,1,0:T(8,128)(2,1)S(1)} %get-tuple-element.50), channel_id=1, source_target_pairs={{0,8},{4,12},{8,16},{12,20},{16,24},{20,28},{1,9},{5,13},{9,17},{1... | collective-permute-start | bytes 393224 | tf_op jit(solution)/shard_map/ppermute | solution.py:31
  46.6 1.6 %collective-permute-start.14 = (f32[2,256,128]{2,1,0:T(8,128)S(1)}, f32[2,256,128]{2,1,0:T(8,128)S(1)}, u32[]{:S(2)}, u32[]{:S(2)}) collective-permute-start(f32[2,256,128]{2,1,0:T(8,128)S(1)} %get-tuple-element.52), channel_id=1, source_target_pairs={{0,4},{4,0},{8,12},{12,8},{16,20},{20,16},{24,28},{28,24},{1,5},{5... | collective-permute-start | bytes 786440 | tf_op jit(solution)/shard_map/ppermute | solution.py:20
  47.5 1.6 %collective-permute-start.16 = (f32[2,128]{1,0:T(2,128)S(1)}, f32[2,128]{1,0:T(2,128)S(1)}, u32[]{:S(2)}, u32[]{:S(2)}) collective-permute-start(f32[2,128]{1,0:T(2,128)S(1)} %constant_dynamic-slice_fusion.1), channel_id=1, source_target_pairs={{0,4},{4,0},{8,12},{12,8},{16,20},{20,16},{24,28},{28,24},{1,5},{5... | collective-permute-start | bytes 3080 | tf_op jit(solution)/shard_map/ppermute | solution.py:20

commit v7 on v6

--- a/solution.py
+++ b/solution.py
@@ -269,8 +269,8 @@
         size = array.shape[axis] // CORES
         return lax.dynamic_slice_in_dim(array, which * size, size, axis)
 
-    par = jnp.stack([persistence, volatility, base_rate])
-    sent = side(after(shocks, par), 1 - core, 1)
+    sent = side(shocks, 1 - core, 1)
+    par = jnp.stack([persistence, volatility, after(base_rate, sent)])
     got = swap(sent)
     kept = side(after(shocks, sent), core, 1)
 

time: 50.2 us -> 50.2 us (level)
  local copies, waits for them, and re-layouts: 1.29 us -> 2.07 us
  waiting for transfers between devices: 15.3 us -> 14.6 us
    unnamed x6, local copies, waits for them, and re-layouts: 0.45 us -> 1.22 us
    ppermute x5, waiting for transfers between devices: 1.34 us -> 0.6 us  [swap(): return lax.ppermute(block, 'date', [(i, i ^ 1) for i in range(n)])]
  transfers between devices with their start and end apart: 17 -> 17, of which waited for: 10 -> 9; matrix products, arithmetic and copies ran while one was open for 5% -> 7% of each run, Pallas kernels for 8% -> 8%
where the time goes in v7:
time: 50.2 us; the launch traced here: 49.6 us
  starting transfers between devices  21.8 us (43%)
  waiting for transfers between devices  14.6 us (29%)
  Pallas kernels  7.29 us (15%)
  other arithmetic  3.14 us (6%)
  local copies, waits for them, and re-layouts  2.07 us (4%)
  between operations  0.83 us (2%)
    ppermute x9, starting transfers between devices, exchange(): lax.ppermute(slots[i], 'book', [(j, j ^ i) for j in range(n)])  12.6 us
    ppermute x9, waiting for transfers between devices, exchange(): lax.ppermute(slots[i], 'book', [(j, j ^ i) for j in range(n)])  11.4 us
    ppermute x2, starting transfers between devices, across(): return lax.ppermute(block, 'date', [(i, i ^ hop) for i in range(n)])  5.61 us
    pallas_call x1, Pallas kernels, weights(): pl.pallas_call(functools.partial(weights_kernel, books, per), in_specs=[s...  3.82 us
    pallas_call x1, Pallas kernels, values(): pl.pallas_call(functools.partial(values_kernel, books), in_specs=[pl.Bloc...  2.56 us
    ppermute x1, starting transfers between devices, later(): lax.ppermute(block, 'date', [(i, i + CORES) for i in range(n - CORES)])  2.36 us
    ppermute x2, waiting for transfers between devices, across(): return lax.ppermute(block, 'date', [(i, i ^ hop) for i in range(n)])  1.82 us
    ppermute x5, starting transfers between devices, swap(): return lax.ppermute(block, 'date', [(i, i ^ 1) for i in range(n)])  1.23 us
  transfers between devices with their start and end apart: 17, of which 9 were waited for; matrix products, arithmetic and copies ran while one was open for 7% of the time, Pallas kernels for 8%

profile of v7, /device:TPU:0, one launch (start us, length us, event | category | flops | bytes accessed | tf_op | source)
XLA Modules:
  0.0 49.6 jit_solution(18332703007850481263)
XLA Ops:
  0.7 1.2 %copy-done = bf16[2,512,512]{2,1,0:T(8,128)(2,1)S(1)} copy-done((bf16[2,512,512]{2,1,0:T(8,128)(2,1)S(1)}, bf16[2,512,512]{2,1,0:T(8,128)(2,1)}, u32[]{:S(2)}) %copy-start) | copy-done | bytes 1048600
  2.4 0.7 %reshape.18.sets_ref = s32[16,256]{1,0:T(8,128)S(1)} reshape(s32[4096]{0:T(1024)} %param.15) | data formatting | bytes 32768 | tf_op jit(solution)/shard_map/reshape | solution.py:100
  3.2 0.7 %pad_maximum_fusion.3.par_ref = f32[3,512]{1,0:T(4,128)S(1)} fusion(f32[1,512]{1,0:T(1,128)} %bitcast.28, f32[1,512]{1,0:T(1,128)} %bitcast.29, f32[1,512]{1,0:T(1,128)} %bitcast.30), kind=kLoop, calls=%fused_computation.21 | loop fusion | flops 3072 | bytes 12288 | tf_op jit(solution)/shard_map/stack | solution.py:273
  4.0 0.9 %first_code.1 = (s16[256,512]{1,0:T(8,128)(2,1)S(1)}, f32[256,512]{1,0:T(8,128)S(1)}, f32[8,512]{1,0:T(8,128)S(1)}) custom-call(s32[3]{0:T(128)S(1)} %pad_add_fusion.here_ref, f32[3,512]{1,0:T(4,128)S(1)} %pad_maximum_fusion.3.par_ref, bf16[2,256,512]{2,1,0:T(8,128)(2,1)S(1)} %constant_dynamic-slice_fusion.3.kept_ref, ...), custom_call_target="tpu_custom_call" | custom-call | flops 2097152 | bytes 2097152 | tf_op jit(solution)/shard_map/first_code/pallas_call | solution.py:225
  4.9 3.0 %collective-permute-start.1 = (s16[256,512]{1,0:T(8,128)(2,1)S(1)}, s16[256,512]{1,0:T(8,128)(2,1)S(1)}, u32[]{:S(2)}, u32[]{:S(2)}) collective-permute-start(s16[256,512]{1,0:T(8,128)(2,1)S(1)} %get-tuple-element.30), channel_id=1, source_target_pairs={{0,8},{4,12},{8,0},{12,4},{16,24},{20,28},{24,16},{28,20},{1,9},{5... | collective-permute-start | bytes 786440 | tf_op jit(solution)/shard_map/ppermute | solution.py:26
  7.9 3.8 %weights.1 = (f32[256,512]{1,0:T(8,128)S(1)}, bf16[256,512]{1,0:T(8,128)(2,1)S(1)}, bf16[256,512]{1,0:T(8,128)(2,1)S(1)}, bf16[256,512]{1,0:T(8,128)(2,1)S(1)}) custom-call(s32[3]{0:T(128)S(1)} %pad_add_fusion.here_ref, s32[16]{0:T(128)} %bitcast.31, s32[16,256]{1,0:T(8,128)S(1)} %reshape.18.sets_ref, bf16[4096,512]{1,0:T(8,128)(2,1)} %flows_hbm.1), custom_call_target="tpu_custom_call" | custom-call | flops 1073741824 | bytes 4194304 | tf_op jit(solution)/shard_map/weights/pallas_call | solution.py:79
  11.7 1.6 %collective-permute-start.3 = (bf16[256,512]{1,0:T(8,128)(2,1)S(1)}, bf16[256,512]{1,0:T(8,128)(2,1)S(1)}, u32[]{:S(2)}, u32[]{:S(2)}) collective-permute-start(bf16[256,512]{1,0:T(8,128)(2,1)S(1)} %get-tuple-element.36), channel_id=1, source_target_pairs={{0,1},{1,0},{2,3},{3,2},{4,5},{5,4},{6,7},{7,6},{8,9},{9,8},{10,11... | collective-permute-start | bytes 786440 | tf_op jit(solution)/shard_map/ppermute | solution.py:37
  13.3 1.5 %collective-permute-start.4 = (bf16[256,512]{1,0:T(8,128)(2,1)S(1)}, bf16[256,512]{1,0:T(8,128)(2,1)S(1)}, u32[]{:S(2)}, u32[]{:S(2)}) collective-permute-start(bf16[256,512]{1,0:T(8,128)(2,1)S(1)} %get-tuple-element.37), channel_id=1, source_target_pairs={{0,2},{1,3},{2,0},{3,1},{4,6},{5,7},{6,4},{7,5},{8,10},{9,11},{10,... | collective-permute-start | bytes 786440 | tf_op jit(solution)/shard_map/ppermute | solution.py:37
  15.5 2.7 %collective-permute-start.2 = (s16[256,512]{1,0:T(8,128)(2,1)S(1)}, s16[256,512]{1,0:T(8,128)(2,1)S(1)}, u32[]{:S(2)}, u32[]{:S(2)}) collective-permute-start(s16[256,512]{1,0:T(8,128)(2,1)S(1)} %round-nearest-even_convert_fusion), channel_id=1, source_target_pairs={{0,16},{4,20},{8,24},{12,28},{16,0},{20,4},{24,8},{28,12},{1,17},{... | collective-permute-start | bytes 786440 | tf_op jit(solution)/shard_map/ppermute | solution.py:26
  18.2 2.8 %collective-permute-done.3 = bf16[256,512]{1,0:T(8,128)(2,1)S(1)} collective-permute-done((bf16[256,512]{1,0:T(8,128)(2,1)S(1)}, bf16[256,512]{1,0:T(8,128)(2,1)S(1)}, u32[]{:S(2)}, u32[]{:S(2)}) %collective-permute-start.3) | collective-permute-done | bytes 262176 | tf_op jit(solution)/shard_map/ppermute | solution.py:37
  21.0 5.8 %collective-permute-done.4 = bf16[256,512]{1,0:T(8,128)(2,1)S(1)} collective-permute-done((bf16[256,512]{1,0:T(8,128)(2,1)S(1)}, bf16[256,512]{1,0:T(8,128)(2,1)S(1)}, u32[]{:S(2)}, u32[]{:S(2)}) %collective-permute-start.4) | collective-permute-done | bytes 262176 | tf_op jit(solution)/shard_map/ppermute | solution.py:37
  27.5 1.8 %collective-permute-done.2 = s16[256,512]{1,0:T(8,128)(2,1)S(1)} collective-permute-done((s16[256,512]{1,0:T(8,128)(2,1)S(1)}, s16[256,512]{1,0:T(8,128)(2,1)S(1)}, u32[]{:S(2)}, u32[]{:S(2)}) %collective-permute-start.2) | collective-permute-done | bytes 262176 | tf_op jit(solution)/shard_map/ppermute | solution.py:26
  29.6 2.6 %values.1 = (f32[512,128]{1,0:T(8,128)S(1)}, bf16[512,128]{1,0:T(8,128)(2,1)S(1)}, bf16[512,128]{1,0:T(8,128)(2,1)S(1)}, bf16[512,128]{1,0:T(8,128)(2,1)S(1)}, f...) custom-call(s32[3]{0:T(128)S(1)} %pad_add_fusion.here_ref, ...), custom_call_target="tpu_custom_call" | custom-call | flops 1073741824 | bytes 2097152 | tf_op jit(solution)/shard_map/values/pallas_call | solution.py:156
  32.1 2.5 %collective-permute-start.10 = (bf16[512,128]{1,0:T(8,128)(2,1)S(1)}, bf16[512,128]{1,0:T(8,128)(2,1)S(1)}, u32[]{:S(2)}, u32[]{:S(2)}) collective-permute-start(bf16[512,128]{1,0:T(8,128)(2,1)S(1)} %get-tuple-element.43), channel_id=1, source_target_pairs={{0,3},{1,2},{2,1},{3,0},{4,7},{5,6},{6,5},{7,4},{8,11},{9,10},{10,... | collective-permute-start | bytes 393224 | tf_op jit(solution)/shard_map/ppermute | solution.py:37
  35.7 1.5 %collective-permute-start.11 = (bf16[512,128]{1,0:T(8,128)(2,1)S(1)}, bf16[512,128]{1,0:T(8,128)(2,1)S(1)}, u32[]{:S(2)}, u32[]{:S(2)}) collective-permute-start(bf16[512,128]{1,0:T(8,128)(2,1)S(1)} %get-tuple-element.45), channel_id=1, source_target_pairs={{0,1},{1,0},{2,3},{3,2},{4,5},{5,4},{6,7},{7,6},{8,9},{9,8},{10,11... | collective-permute-start | bytes 393224 | tf_op jit(solution)/shard_map/ppermute | solution.py:37
  37.2 1.5 %collective-permute-start.12 = (bf16[512,128]{1,0:T(8,128)(2,1)S(1)}, bf16[512,128]{1,0:T(8,128)(2,1)S(1)}, u32[]{:S(2)}, u32[]{:S(2)}) collective-permute-start(bf16[512,128]{1,0:T(8,128)(2,1)S(1)} %get-tuple-element.46), channel_id=1, source_target_pairs={{0,2},{1,3},{2,0},{3,1},{4,6},{5,7},{6,4},{7,5},{8,10},{9,11},{10,... | collective-permute-start | bytes 393224 | tf_op jit(solution)/shard_map/ppermute | solution.py:37
  38.7 0.8 %collective-permute-done.10 = bf16[512,128]{1,0:T(8,128)(2,1)S(1)} collective-permute-done((bf16[512,128]{1,0:T(8,128)(2,1)S(1)}, bf16[512,128]{1,0:T(8,128)(2,1)S(1)}, u32[]{:S(2)}, u32[]{:S(2)}) %collective-permute-start.10) | collective-permute-done | bytes 131104 | tf_op jit(solution)/shard_map/ppermute | solution.py:37
  39.6 2.4 %collective-permute-start.13 = (bf16[512,128]{1,0:T(8,128)(2,1)S(1)}, bf16[512,128]{1,0:T(8,128)(2,1)S(1)}, u32[]{:S(2)}, u32[]{:S(2)}) collective-permute-start(bf16[512,128]{1,0:T(8,128)(2,1)S(1)} %get-tuple-element.47), channel_id=1, source_target_pairs={{0,3},{1,2},{2,1},{3,0},{4,7},{5,6},{6,5},{7,4},{8,11},{9,10},{10,... | collective-permute-start | bytes 393224 | tf_op jit(solution)/shard_map/ppermute | solution.py:37
  42.5 2.4 %collective-permute-start.15 = (bf16[2,256,128]{2,1,0:T(8,128)(2,1)S(1)}, bf16[2,256,128]{2,1,0:T(8,128)(2,1)S(1)}, u32[]{:S(2)}, u32[]{:S(2)}) collective-permute-start(bf16[2,256,128]{2,1,0:T(8,128)(2,1)S(1)} %get-tuple-element.50), channel_id=1, source_target_pairs={{0,8},{4,12},{8,16},{12,20},{16,24},{20,28},{1,9},{5,13},{9,17},{1... | collective-permute-start | bytes 393224 | tf_op jit(solution)/shard_map/ppermute | solution.py:31
  45.0 1.5 %collective-permute-done.12 = bf16[512,128]{1,0:T(8,128)(2,1)S(1)} collective-permute-done((bf16[512,128]{1,0:T(8,128)(2,1)S(1)}, bf16[512,128]{1,0:T(8,128)(2,1)S(1)}, u32[]{:S(2)}, u32[]{:S(2)}) %collective-permute-start.12) | collective-permute-done | bytes 131104 | tf_op jit(solution)/shard_map/ppermute | solution.py:37
  46.7 0.7 %collective-permute-done.15 = bf16[2,256,128]{2,1,0:T(8,128)(2,1)S(1)} collective-permute-done((bf16[2,256,128]{2,1,0:T(8,128)(2,1)S(1)}, bf16[2,256,128]{2,1,0:T(8,128)(2,1)S(1)}, u32[]{:S(2)}, u32[]{:S(2)}) %collective-permute-start.15) | collective-permute-done | bytes 131104 | tf_op jit(solution)/shard_map/ppermute | solution.py:31
  47.6 0.6 %collective-permute-done.14 = f32[2,256,128]{2,1,0:T(8,128)S(1)} collective-permute-done((f32[2,256,128]{2,1,0:T(8,128)S(1)}, f32[2,256,128]{2,1,0:T(8,128)S(1)}, u32[]{:S(2)}, u32[]{:S(2)}) %collective-permute-start.14) | collective-permute-done | bytes 262176 | tf_op jit(solution)/shard_map/ppermute | solution.py:20
  48.2 0.8 %pad_maximum_fusion.2 = f32[2,512,128]{2,1,0:T(8,128)} fusion(f32[2,256,128]{2,1,0:T(8,128)S(1)} %get-tuple-element.57, f32[2,256,128]{2,1,0:T(8,128)S(1)} %get-tuple-element.56), kind=kLoop, calls=%fused_computation.11 | loop fusion | flops 131072 | bytes 1048576 | tf_op jit(solution)/shard_map/concatenate | solution.py:326
  49.1 0.6 %fusion.8 = f32[2,128]{1,0:T(2,128)} fusion(f32[2,128]{1,0:T(2,128)S(1)} %collective-permute-done.16, f32[4,128]{1,0:T(4,128)S(1)} %fusion.6, s32[]{:T(128)S(6)} %select_n.63), kind=kLoop, calls=%fused_computation.28 | loop fusion | flops 512 | bytes 3076 | tf_op jit(solution)/shard_map/div | solution.py:330
  (38 shorter events, 4.5 us)
Async XLA Ops:
  0.6 1.2 %copy-start = (bf16[2,512,512]{2,1,0:T(8,128)(2,1)S(1)}, bf16[2,512,512]{2,1,0:T(8,128)(2,1)}, u32[]{:S(2)}) copy-start(bf16[2,512,512]{2,1,0:T(8,128)(2,1)} %param.9) | copy-start | bytes 3145732
  1.9 2.1 %collective-permute-start = (bf16[2,256,512]{2,1,0:T(8,128)(2,1)S(1)}, bf16[2,256,512]{2,1,0:T(8,128)(2,1)S(1)}, u32[]{:S(2)}, u32[]{:S(2)}) collective-permute-start(bf16[2,256,512]{2,1,0:T(8,128)(2,1)S(1)} %constant_dynamic-slice_fusion.4), channel_id=1, source_target_pairs={{0,4},{4,0},{8,12},{12,8},{16,20},{20,16},{24,28},{28,24},{1,5},{5... | collective-permute-start | bytes 1572872 | tf_op jit(solution)/shard_map/ppermute | solution.py:20
  4.9 10.4 %collective-permute-start.1 = (s16[256,512]{1,0:T(8,128)(2,1)S(1)}, s16[256,512]{1,0:T(8,128)(2,1)S(1)}, u32[]{:S(2)}, u32[]{:S(2)}) collective-permute-start(s16[256,512]{1,0:T(8,128)(2,1)S(1)} %get-tuple-element.30), channel_id=1, source_target_pairs={{0,8},{4,12},{8,0},{12,4},{16,24},{20,28},{24,16},{28,20},{1,9},{5... | collective-permute-start | bytes 786440 | tf_op jit(solution)/shard_map/ppermute | solution.py:26
  11.7 9.2 %collective-permute-start.3 = (bf16[256,512]{1,0:T(8,128)(2,1)S(1)}, bf16[256,512]{1,0:T(8,128)(2,1)S(1)}, u32[]{:S(2)}, u32[]{:S(2)}) collective-permute-start(bf16[256,512]{1,0:T(8,128)(2,1)S(1)} %get-tuple-element.36), channel_id=1, source_target_pairs={{0,1},{1,0},{2,3},{3,2},{4,5},{5,4},{6,7},{7,6},{8,9},{9,8},{10,11... | collective-permute-start | bytes 786440 | tf_op jit(solution)/shard_map/ppermute | solution.py:37
  13.3 13.5 %collective-permute-start.4 = (bf16[256,512]{1,0:T(8,128)(2,1)S(1)}, bf16[256,512]{1,0:T(8,128)(2,1)S(1)}, u32[]{:S(2)}, u32[]{:S(2)}) collective-permute-start(bf16[256,512]{1,0:T(8,128)(2,1)S(1)} %get-tuple-element.37), channel_id=1, source_target_pairs={{0,2},{1,3},{2,0},{3,1},{4,6},{5,7},{6,4},{7,5},{8,10},{9,11},{10,... | collective-permute-start | bytes 786440 | tf_op jit(solution)/shard_map/ppermute | solution.py:37
  14.8 11.9 %collective-permute-start.5 = (bf16[256,512]{1,0:T(8,128)(2,1)S(1)}, bf16[256,512]{1,0:T(8,128)(2,1)S(1)}, u32[]{:S(2)}, u32[]{:S(2)}) collective-permute-start(bf16[256,512]{1,0:T(8,128)(2,1)S(1)} %get-tuple-element.38), channel_id=1, source_target_pairs={{0,3},{1,2},{2,1},{3,0},{4,7},{5,6},{6,5},{7,4},{8,11},{9,10},{10,... | collective-permute-start | bytes 786440 | tf_op jit(solution)/shard_map/ppermute | solution.py:37
  15.5 20.2 %copy-start.2 = (s32[128]{0:T(128)S(1)}, s32[128]{0:T(128)}, u32[]{:S(2)}) copy-start(s32[128]{0:T(128)} %param.17) | copy-start | bytes 1540
  15.5 13.9 %collective-permute-start.2 = (s16[256,512]{1,0:T(8,128)(2,1)S(1)}, s16[256,512]{1,0:T(8,128)(2,1)S(1)}, u32[]{:S(2)}, u32[]{:S(2)}) collective-permute-start(s16[256,512]{1,0:T(8,128)(2,1)S(1)} %round-nearest-even_convert_fusion), channel_id=1, source_target_pairs={{0,16},{4,20},{8,24},{12,28},{16,0},{20,4},{24,8},{28,12},{1,17},{... | collective-permute-start | bytes 786440 | tf_op jit(solution)/shard_map/ppermute | solution.py:26
  26.9 2.6 %collective-permute-start.6 = (bf16[256,512]{1,0:T(8,128)(2,1)S(1)}, bf16[256,512]{1,0:T(8,128)(2,1)S(1)}, u32[]{:S(2)}, u32[]{:S(2)}) collective-permute-start(bf16[256,512]{1,0:T(8,128)(2,1)S(1)} %get-tuple-element.55.refs_0_), channel_id=1, source_target_pairs={{0,4},{4,0},{8,12},{12,8},{16,20},{20,16},{24,28},{28,24},{1,5},{5... | collective-permute-start | bytes 786440 | tf_op jit(solution)/shard_map/ppermute | solution.py:20
  27.0 2.6 %collective-permute-start.7 = (bf16[256,512]{1,0:T(8,128)(2,1)S(1)}, bf16[256,512]{1,0:T(8,128)(2,1)S(1)}, u32[]{:S(2)}, u32[]{:S(2)}) collective-permute-start(bf16[256,512]{1,0:T(8,128)(2,1)S(1)} %get-tuple-element.54.refs_1_), channel_id=1, source_target_pairs={{0,4},{4,0},{8,12},{12,8},{16,20},{20,16},{24,28},{28,24},{1,5},{5... | collective-permute-start | bytes 786440 | tf_op jit(solution)/shard_map/ppermute | solution.py:20
  27.5 19.8 %copy-start.1 = (f32[128]{0:T(128)S(1)}, f32[128]{0:T(128)}, u32[]{:S(2)}) copy-start(f32[128]{0:T(128)} %param.16) | copy-start | bytes 1540
  32.1 7.4 %collective-permute-start.10 = (bf16[512,128]{1,0:T(8,128)(2,1)S(1)}, bf16[512,128]{1,0:T(8,128)(2,1)S(1)}, u32[]{:S(2)}, u32[]{:S(2)}) collective-permute-start(bf16[512,128]{1,0:T(8,128)(2,1)S(1)} %get-tuple-element.43), channel_id=1, source_target_pairs={{0,3},{1,2},{2,1},{3,0},{4,7},{5,6},{6,5},{7,4},{8,11},{9,10},{10,... | collective-permute-start | bytes 393224 | tf_op jit(solution)/shard_map/ppermute | solution.py:37
  34.7 7.7 %collective-permute-start.8 = (bf16[512,128]{1,0:T(8,128)(2,1)S(1)}, bf16[512,128]{1,0:T(8,128)(2,1)S(1)}, u32[]{:S(2)}, u32[]{:S(2)}) collective-permute-start(bf16[512,128]{1,0:T(8,128)(2,1)S(1)} %get-tuple-element.41), channel_id=1, source_target_pairs={{0,1},{1,0},{2,3},{3,2},{4,5},{5,4},{6,7},{7,6},{8,9},{9,8},{10,11... | collective-permute-start | bytes 393224 | tf_op jit(solution)/shard_map/ppermute | solution.py:37
  35.2 7.2 %collective-permute-start.9 = (bf16[512,128]{1,0:T(8,128)(2,1)S(1)}, bf16[512,128]{1,0:T(8,128)(2,1)S(1)}, u32[]{:S(2)}, u32[]{:S(2)}) collective-permute-start(bf16[512,128]{1,0:T(8,128)(2,1)S(1)} %get-tuple-element.42), channel_id=1, source_target_pairs={{0,2},{1,3},{2,0},{3,1},{4,6},{5,7},{6,4},{7,5},{8,10},{9,11},{10,... | collective-permute-start | bytes 393224 | tf_op jit(solution)/shard_map/ppermute | solution.py:37
  35.7 9.3 %collective-permute-start.11 = (bf16[512,128]{1,0:T(8,128)(2,1)S(1)}, bf16[512,128]{1,0:T(8,128)(2,1)S(1)}, u32[]{:S(2)}, u32[]{:S(2)}) collective-permute-start(bf16[512,128]{1,0:T(8,128)(2,1)S(1)} %get-tuple-element.45), channel_id=1, source_target_pairs={{0,1},{1,0},{2,3},{3,2},{4,5},{5,4},{6,7},{7,6},{8,9},{9,8},{10,11... | collective-permute-start | bytes 393224 | tf_op jit(solution)/shard_map/ppermute | solution.py:37
  37.2 9.3 %collective-permute-start.12 = (bf16[512,128]{1,0:T(8,128)(2,1)S(1)}, bf16[512,128]{1,0:T(8,128)(2,1)S(1)}, u32[]{:S(2)}, u32[]{:S(2)}) collective-permute-start(bf16[512,128]{1,0:T(8,128)(2,1)S(1)} %get-tuple-element.46), channel_id=1, source_target_pairs={{0,2},{1,3},{2,0},{3,1},{4,6},{5,7},{6,4},{7,5},{8,10},{9,11},{10,... | collective-permute-start | bytes 393224 | tf_op jit(solution)/shard_map/ppermute | solution.py:37
  39.6 7.0 %collective-permute-start.13 = (bf16[512,128]{1,0:T(8,128)(2,1)S(1)}, bf16[512,128]{1,0:T(8,128)(2,1)S(1)}, u32[]{:S(2)}, u32[]{:S(2)}) collective-permute-start(bf16[512,128]{1,0:T(8,128)(2,1)S(1)} %get-tuple-element.47), channel_id=1, source_target_pairs={{0,3},{1,2},{2,1},{3,0},{4,7},{5,6},{6,5},{7,4},{8,11},{9,10},{10,... | collective-permute-start | bytes 393224 | tf_op jit(solution)/shard_map/ppermute | solution.py:37
  42.5 4.9 %collective-permute-start.15 = (bf16[2,256,128]{2,1,0:T(8,128)(2,1)S(1)}, bf16[2,256,128]{2,1,0:T(8,128)(2,1)S(1)}, u32[]{:S(2)}, u32[]{:S(2)}) collective-permute-start(bf16[2,256,128]{2,1,0:T(8,128)(2,1)S(1)} %get-tuple-element.50), channel_id=1, source_target_pairs={{0,8},{4,12},{8,16},{12,20},{16,24},{20,28},{1,9},{5,13},{9,17},{1... | collective-permute-start | bytes 393224 | tf_op jit(solution)/shard_map/ppermute | solution.py:31
  46.6 1.6 %collective-permute-start.14 = (f32[2,256,128]{2,1,0:T(8,128)S(1)}, f32[2,256,128]{2,1,0:T(8,128)S(1)}, u32[]{:S(2)}, u32[]{:S(2)}) collective-permute-start(f32[2,256,128]{2,1,0:T(8,128)S(1)} %get-tuple-element.52), channel_id=1, source_target_pairs={{0,4},{4,0},{8,12},{12,8},{16,20},{20,16},{24,28},{28,24},{1,5},{5... | collective-permute-start | bytes 786440 | tf_op jit(solution)/shard_map/ppermute | solution.py:20
  47.5 1.6 %collective-permute-start.16 = (f32[2,128]{1,0:T(2,128)S(1)}, f32[2,128]{1,0:T(2,128)S(1)}, u32[]{:S(2)}, u32[]{:S(2)}) collective-permute-start(f32[2,128]{1,0:T(2,128)S(1)} %constant_dynamic-slice_fusion.1), channel_id=1, source_target_pairs={{0,4},{4,0},{8,12},{12,8},{16,20},{20,16},{24,28},{28,24},{1,5},{5... | collective-permute-start | bytes 3080 | tf_op jit(solution)/shard_map/ppermute | solution.py:20

commit v8 on v6

--- a/solution.py
+++ b/solution.py
@@ -102,29 +102,29 @@
     )
 
 
-def price_rows(books, disc, high_ref, low_ref, outs):
+def price_rows(books, core, disc, sources, outs):
     sets_here = SETS // books
+    half = sources[0].shape[0]
     rows = 256
+
+    def product(price, high, low):
+        part = lax.dot_general(price, high[...], TURNED, preferred_element_type=jnp.float32)
+        return part + lax.dot_general(price, low[...], TURNED, preferred_element_type=jnp.float32)
+
     for r in range(disc.shape[0] // rows):
         price = disc[r * rows : (r + 1) * rows, :]
-        part = lax.dot_general(price, high_ref[...], TURNED, preferred_element_type=jnp.float32)
-        part = part + lax.dot_general(price, low_ref[...], TURNED, preferred_element_type=jnp.float32)
+        mine, other = product(price, *sources[:2]), product(price, *sources[2:])
+        sides = jnp.where(core == 0, mine, other), jnp.where(core == 0, other, mine)
         for i in range(books):
-            outs[i][r * rows : (r + 1) * rows, :] = part[:, i * sets_here : (i + 1) * sets_here].astype(
-                outs[i].dtype
-            )
+            which, at = divmod(i * sets_here, half)
+            outs[i][r * rows : (r + 1) * rows, :] = sides[which][:, at : at + sets_here].astype(outs[i].dtype)
 
 
 def values_kernel(books, here_ref, par_ref, kept_ref, got_ref, start_ref, *refs):
-    sources, outs, (disc, high, low) = refs[:4], refs[4:-3], refs[-3:]
+    sources, outs, disc = refs[:4], refs[4:-1], refs[-1]
     core = here_ref[0]
     dates, paths, _ = kept_ref.shape
-    half = sources[0].shape[0]
     tile = 32
-    for i, source in enumerate(sources):
-        place = core if i < 2 else 1 - core
-        target = low if i % 2 else high
-        target[pl.ds(pl.multiple_of(place * half, half), half), :] = source[...]
 
     def walk(first, second, i, _):
         at = pl.ds(i * tile, tile)
@@ -145,8 +145,8 @@
         lax.fori_loop(0, paths // tile, functools.partial(walk, got_ref, kept_ref), 0)
 
     rows = dates * paths
-    price_rows(books, disc.at[rows:], high, low, outs[:books])
-    price_rows(books, disc.at[:rows], high, low, outs[books:])
+    price_rows(books, core, disc.at[rows:], sources, outs[:books])
+    price_rows(books, core, disc.at[:rows], sources, outs[books:])
 
 
 def values(here, par, kept, got, start, mats, books):
@@ -162,8 +162,7 @@
             for i in range(books)
         ]
         * 2,
-        scratch_shapes=[pltpu.VMEM((2 * rows, width), jnp.bfloat16)]
-        + [pltpu.VMEM((SETS, width), jnp.bfloat16)] * 2,
+        scratch_shapes=[pltpu.VMEM((2 * rows, width), jnp.bfloat16)],
         compiler_params=pltpu.CompilerParams(vmem_limit_bytes=16 * MIB),
         cost_estimate=pl.CostEstimate(
             flops=8 * rows * SETS * width, bytes_accessed=2 * MIB, transcendentals=2 * rows * width

time: 50.2 us -> 50.1 us (level)
  no operation moved by 1% of the time
where the time goes in v8:
time: 50.1 us; the launch traced here: 49.6 us
  starting transfers between devices  21.8 us (44%)
  waiting for transfers between devices  15.3 us (31%)
  Pallas kernels  7.25 us (14%)
  other arithmetic  3.23 us (6%)
  local copies, waits for them, and re-layouts  1.29 us (3%)
  between operations  0.83 us (2%)
    ppermute x9, starting transfers between devices, exchange(): lax.ppermute(slots[i], 'book', [(j, j ^ i) for j in range(n)])  12.6 us
    ppermute x9, waiting for transfers between devices, exchange(): lax.ppermute(slots[i], 'book', [(j, j ^ i) for j in range(n)])  11.5 us
    ppermute x2, starting transfers between devices, across(): return lax.ppermute(block, 'date', [(i, i ^ hop) for i in range(n)])  5.66 us
    pallas_call x1, Pallas kernels, weights(): pl.pallas_call(functools.partial(weights_kernel, books, per), in_specs=[s...  3.82 us
    pallas_call x1, Pallas kernels, values(): pl.pallas_call(functools.partial(values_kernel, books), in_specs=[pl.Bloc...  2.53 us
    ppermute x1, starting transfers between devices, later(): lax.ppermute(block, 'date', [(i, i + CORES) for i in range(n - CORES)])  2.31 us
    ppermute x2, waiting for transfers between devices, across(): return lax.ppermute(block, 'date', [(i, i ^ hop) for i in range(n)])  1.83 us
    ppermute x5, waiting for transfers between devices, swap(): return lax.ppermute(block, 'date', [(i, i ^ 1) for i in range(n)])  1.34 us
  transfers between devices with their start and end apart: 17, of which 10 were waited for; matrix products, arithmetic and copies ran while one was open for 5% of the time, Pallas kernels for 8%

profile of v8, /device:TPU:0, one launch (start us, length us, event | category | flops | bytes accessed | tf_op | source)
XLA Modules:
  0.0 49.6 jit_solution(6460369427772388052)
XLA Ops:
  0.7 0.8 %pad_maximum_fusion.3.par_ref = f32[3,512]{1,0:T(4,128)S(1)} fusion(f32[1,512]{1,0:T(1,128)} %bitcast.28, f32[1,512]{1,0:T(1,128)} %bitcast.29, f32[1,512]{1,0:T(1,128)} %bitcast.30), kind=kLoop, calls=%fused_computation.21 | loop fusion | flops 3072 | bytes 12288 | tf_op jit(solution)/shard_map/stack | solution.py:271
  2.5 0.7 %reshape.18.sets_ref = s32[16,256]{1,0:T(8,128)S(1)} reshape(s32[4096]{0:T(1024)} %param.15) | data formatting | bytes 32768 | tf_op jit(solution)/shard_map/reshape | solution.py:100
  3.3 0.7 %collective-permute-done.got_ref = bf16[2,256,512]{2,1,0:T(8,128)(2,1)S(1)} collective-permute-done((bf16[2,256,512]{2,1,0:T(8,128)(2,1)S(1)}, bf16[2,256,512]{2,1,0:T(8,128)(2,1)S(1)}, u32[]{:S(2)}, u32[]{:S(2)}) %collective-permute-start) | collective-permute-done | bytes 524320 | tf_op jit(solution)/shard_map/ppermute | solution.py:20
  4.0 0.9 %first_code.1 = (s16[256,512]{1,0:T(8,128)(2,1)S(1)}, f32[256,512]{1,0:T(8,128)S(1)}, f32[8,512]{1,0:T(8,128)S(1)}) custom-call(s32[3]{0:T(128)S(1)} %pad_add_fusion.here_ref, f32[3,512]{1,0:T(4,128)S(1)} %pad_maximum_fusion.3.par_ref, bf16[2,256,512]{2,1,0:T(8,128)(2,1)S(1)} %constant_dynamic-slice_fusion.3.kept_ref, ...), custom_call_target="tpu_custom_call" | custom-call | flops 2097152 | bytes 2097152 | tf_op jit(solution)/shard_map/first_code/pallas_call | solution.py:224
  4.9 3.0 %collective-permute-start.1 = (s16[256,512]{1,0:T(8,128)(2,1)S(1)}, s16[256,512]{1,0:T(8,128)(2,1)S(1)}, u32[]{:S(2)}, u32[]{:S(2)}) collective-permute-start(s16[256,512]{1,0:T(8,128)(2,1)S(1)} %get-tuple-element.30), channel_id=1, source_target_pairs={{0,8},{4,12},{8,0},{12,4},{16,24},{20,28},{24,16},{28,20},{1,9},{5... | collective-permute-start | bytes 786440 | tf_op jit(solution)/shard_map/ppermute | solution.py:26
  7.9 3.8 %weights.1 = (f32[256,512]{1,0:T(8,128)S(1)}, bf16[256,512]{1,0:T(8,128)(2,1)S(1)}, bf16[256,512]{1,0:T(8,128)(2,1)S(1)}, bf16[256,512]{1,0:T(8,128)(2,1)S(1)}) custom-call(s32[3]{0:T(128)S(1)} %pad_add_fusion.here_ref, s32[16]{0:T(128)} %bitcast.31, s32[16,256]{1,0:T(8,128)S(1)} %reshape.18.sets_ref, bf16[4096,512]{1,0:T(8,128)(2,1)} %flows_hbm.1), custom_call_target="tpu_custom_call" | custom-call | flops 1073741824 | bytes 4194304 | tf_op jit(solution)/shard_map/weights/pallas_call | solution.py:79
  11.8 1.6 %collective-permute-start.3 = (bf16[256,512]{1,0:T(8,128)(2,1)S(1)}, bf16[256,512]{1,0:T(8,128)(2,1)S(1)}, u32[]{:S(2)}, u32[]{:S(2)}) collective-permute-start(bf16[256,512]{1,0:T(8,128)(2,1)S(1)} %get-tuple-element.36), channel_id=1, source_target_pairs={{0,1},{1,0},{2,3},{3,2},{4,5},{5,4},{6,7},{7,6},{8,9},{9,8},{10,11... | collective-permute-start | bytes 786440 | tf_op jit(solution)/shard_map/ppermute | solution.py:37
  13.3 1.5 %collective-permute-start.4 = (bf16[256,512]{1,0:T(8,128)(2,1)S(1)}, bf16[256,512]{1,0:T(8,128)(2,1)S(1)}, u32[]{:S(2)}, u32[]{:S(2)}) collective-permute-start(bf16[256,512]{1,0:T(8,128)(2,1)S(1)} %get-tuple-element.37), channel_id=1, source_target_pairs={{0,2},{1,3},{2,0},{3,1},{4,6},{5,7},{6,4},{7,5},{8,10},{9,11},{10,... | collective-permute-start | bytes 786440 | tf_op jit(solution)/shard_map/ppermute | solution.py:37
  15.6 2.7 %collective-permute-start.2 = (s16[256,512]{1,0:T(8,128)(2,1)S(1)}, s16[256,512]{1,0:T(8,128)(2,1)S(1)}, u32[]{:S(2)}, u32[]{:S(2)}) collective-permute-start(s16[256,512]{1,0:T(8,128)(2,1)S(1)} %round-nearest-even_convert_fusion), channel_id=1, source_target_pairs={{0,16},{4,20},{8,24},{12,28},{16,0},{20,4},{24,8},{28,12},{1,17},{... | collective-permute-start | bytes 786440 | tf_op jit(solution)/shard_map/ppermute | solution.py:26
  18.2 2.8 %collective-permute-done.3 = bf16[256,512]{1,0:T(8,128)(2,1)S(1)} collective-permute-done((bf16[256,512]{1,0:T(8,128)(2,1)S(1)}, bf16[256,512]{1,0:T(8,128)(2,1)S(1)}, u32[]{:S(2)}, u32[]{:S(2)}) %collective-permute-start.3) | collective-permute-done | bytes 262176 | tf_op jit(solution)/shard_map/ppermute | solution.py:37
  21.0 5.7 %collective-permute-done.4 = bf16[256,512]{1,0:T(8,128)(2,1)S(1)} collective-permute-done((bf16[256,512]{1,0:T(8,128)(2,1)S(1)}, bf16[256,512]{1,0:T(8,128)(2,1)S(1)}, u32[]{:S(2)}, u32[]{:S(2)}) %collective-permute-start.4) | collective-permute-done | bytes 262176 | tf_op jit(solution)/shard_map/ppermute | solution.py:37
  27.5 1.8 %collective-permute-done.2 = s16[256,512]{1,0:T(8,128)(2,1)S(1)} collective-permute-done((s16[256,512]{1,0:T(8,128)(2,1)S(1)}, s16[256,512]{1,0:T(8,128)(2,1)S(1)}, u32[]{:S(2)}, u32[]{:S(2)}) %collective-permute-start.2) | collective-permute-done | bytes 262176 | tf_op jit(solution)/shard_map/ppermute | solution.py:26
  29.6 2.5 %values.1 = (f32[512,128]{1,0:T(8,128)S(1)}, bf16[512,128]{1,0:T(8,128)(2,1)S(1)}, bf16[512,128]{1,0:T(8,128)(2,1)S(1)}, bf16[512,128]{1,0:T(8,128)(2,1)S(1)}, f...) custom-call(s32[3]{0:T(128)S(1)} %pad_add_fusion.here_ref, ...), custom_call_target="tpu_custom_call" | custom-call | flops 1073741824 | bytes 2097152 | tf_op jit(solution)/shard_map/values/pallas_call | solution.py:156
  32.1 2.5 %collective-permute-start.10 = (bf16[512,128]{1,0:T(8,128)(2,1)S(1)}, bf16[512,128]{1,0:T(8,128)(2,1)S(1)}, u32[]{:S(2)}, u32[]{:S(2)}) collective-permute-start(bf16[512,128]{1,0:T(8,128)(2,1)S(1)} %get-tuple-element.43), channel_id=1, source_target_pairs={{0,3},{1,2},{2,1},{3,0},{4,7},{5,6},{6,5},{7,4},{8,11},{9,10},{10,... | collective-permute-start | bytes 393224 | tf_op jit(solution)/shard_map/ppermute | solution.py:37
  35.7 1.5 %collective-permute-start.11 = (bf16[512,128]{1,0:T(8,128)(2,1)S(1)}, bf16[512,128]{1,0:T(8,128)(2,1)S(1)}, u32[]{:S(2)}, u32[]{:S(2)}) collective-permute-start(bf16[512,128]{1,0:T(8,128)(2,1)S(1)} %get-tuple-element.45), channel_id=1, source_target_pairs={{0,1},{1,0},{2,3},{3,2},{4,5},{5,4},{6,7},{7,6},{8,9},{9,8},{10,11... | collective-permute-start | bytes 393224 | tf_op jit(solution)/shard_map/ppermute | solution.py:37
  37.2 1.5 %collective-permute-start.12 = (bf16[512,128]{1,0:T(8,128)(2,1)S(1)}, bf16[512,128]{1,0:T(8,128)(2,1)S(1)}, u32[]{:S(2)}, u32[]{:S(2)}) collective-permute-start(bf16[512,128]{1,0:T(8,128)(2,1)S(1)} %get-tuple-element.46), channel_id=1, source_target_pairs={{0,2},{1,3},{2,0},{3,1},{4,6},{5,7},{6,4},{7,5},{8,10},{9,11},{10,... | collective-permute-start | bytes 393224 | tf_op jit(solution)/shard_map/ppermute | solution.py:37
  38.7 0.8 %collective-permute-done.10 = bf16[512,128]{1,0:T(8,128)(2,1)S(1)} collective-permute-done((bf16[512,128]{1,0:T(8,128)(2,1)S(1)}, bf16[512,128]{1,0:T(8,128)(2,1)S(1)}, u32[]{:S(2)}, u32[]{:S(2)}) %collective-permute-start.10) | collective-permute-done | bytes 131104 | tf_op jit(solution)/shard_map/ppermute | solution.py:37
  39.5 2.4 %collective-permute-start.13 = (bf16[512,128]{1,0:T(8,128)(2,1)S(1)}, bf16[512,128]{1,0:T(8,128)(2,1)S(1)}, u32[]{:S(2)}, u32[]{:S(2)}) collective-permute-start(bf16[512,128]{1,0:T(8,128)(2,1)S(1)} %get-tuple-element.47), channel_id=1, source_target_pairs={{0,3},{1,2},{2,1},{3,0},{4,7},{5,6},{6,5},{7,4},{8,11},{9,10},{10,... | collective-permute-start | bytes 393224 | tf_op jit(solution)/shard_map/ppermute | solution.py:37
  42.5 2.3 %collective-permute-start.15 = (bf16[2,256,128]{2,1,0:T(8,128)(2,1)S(1)}, bf16[2,256,128]{2,1,0:T(8,128)(2,1)S(1)}, u32[]{:S(2)}, u32[]{:S(2)}) collective-permute-start(bf16[2,256,128]{2,1,0:T(8,128)(2,1)S(1)} %get-tuple-element.50), channel_id=1, source_target_pairs={{0,8},{4,12},{8,16},{12,20},{16,24},{20,28},{1,9},{5,13},{9,17},{1... | collective-permute-start | bytes 393224 | tf_op jit(solution)/shard_map/ppermute | solution.py:31
  45.0 1.5 %collective-permute-done.12 = bf16[512,128]{1,0:T(8,128)(2,1)S(1)} collective-permute-done((bf16[512,128]{1,0:T(8,128)(2,1)S(1)}, bf16[512,128]{1,0:T(8,128)(2,1)S(1)}, u32[]{:S(2)}, u32[]{:S(2)}) %collective-permute-start.12) | collective-permute-done | bytes 131104 | tf_op jit(solution)/shard_map/ppermute | solution.py:37
  46.6 0.6 %collective-permute-done.15 = bf16[2,256,128]{2,1,0:T(8,128)(2,1)S(1)} collective-permute-done((bf16[2,256,128]{2,1,0:T(8,128)(2,1)S(1)}, bf16[2,256,128]{2,1,0:T(8,128)(2,1)S(1)}, u32[]{:S(2)}, u32[]{:S(2)}) %collective-permute-start.15) | collective-permute-done | bytes 131104 | tf_op jit(solution)/shard_map/ppermute | solution.py:31
  47.5 0.6 %collective-permute-done.14 = f32[2,256,128]{2,1,0:T(8,128)S(1)} collective-permute-done((f32[2,256,128]{2,1,0:T(8,128)S(1)}, f32[2,256,128]{2,1,0:T(8,128)S(1)}, u32[]{:S(2)}, u32[]{:S(2)}) %collective-permute-start.14) | collective-permute-done | bytes 262176 | tf_op jit(solution)/shard_map/ppermute | solution.py:20
  48.2 0.8 %pad_maximum_fusion.2 = f32[2,512,128]{2,1,0:T(8,128)} fusion(f32[2,256,128]{2,1,0:T(8,128)S(1)} %get-tuple-element.57, f32[2,256,128]{2,1,0:T(8,128)S(1)} %get-tuple-element.56), kind=kLoop, calls=%fused_computation.11 | loop fusion | flops 131072 | bytes 1048576 | tf_op jit(solution)/shard_map/concatenate | solution.py:325
  49.0 0.6 %fusion.8 = f32[2,128]{1,0:T(2,128)} fusion(f32[2,128]{1,0:T(2,128)S(1)} %collective-permute-done.16, f32[4,128]{1,0:T(4,128)S(1)} %fusion.6, s32[]{:T(128)S(6)} %select_n.63), kind=kLoop, calls=%fused_computation.28 | loop fusion | flops 512 | bytes 3076 | tf_op jit(solution)/shard_map/div | solution.py:329
  (38 shorter events, 5.0 us)
Async XLA Ops:
  0.6 1.3 %copy-start = (bf16[2,512,512]{2,1,0:T(8,128)(2,1)S(1)}, bf16[2,512,512]{2,1,0:T(8,128)(2,1)}, u32[]{:S(2)}) copy-start(bf16[2,512,512]{2,1,0:T(8,128)(2,1)} %param.9) | copy-start | bytes 3145732
  1.9 2.1 %collective-permute-start = (bf16[2,256,512]{2,1,0:T(8,128)(2,1)S(1)}, bf16[2,256,512]{2,1,0:T(8,128)(2,1)S(1)}, u32[]{:S(2)}, u32[]{:S(2)}) collective-permute-start(bf16[2,256,512]{2,1,0:T(8,128)(2,1)S(1)} %constant_dynamic-slice_fusion.4), channel_id=1, source_target_pairs={{0,4},{4,0},{8,12},{12,8},{16,20},{20,16},{24,28},{28,24},{1,5},{5... | collective-permute-start | bytes 1572872 | tf_op jit(solution)/shard_map/ppermute | solution.py:20
  4.9 10.4 %collective-permute-start.1 = (s16[256,512]{1,0:T(8,128)(2,1)S(1)}, s16[256,512]{1,0:T(8,128)(2,1)S(1)}, u32[]{:S(2)}, u32[]{:S(2)}) collective-permute-start(s16[256,512]{1,0:T(8,128)(2,1)S(1)} %get-tuple-element.30), channel_id=1, source_target_pairs={{0,8},{4,12},{8,0},{12,4},{16,24},{20,28},{24,16},{28,20},{1,9},{5... | collective-permute-start | bytes 786440 | tf_op jit(solution)/shard_map/ppermute | solution.py:26
  11.8 9.3 %collective-permute-start.3 = (bf16[256,512]{1,0:T(8,128)(2,1)S(1)}, bf16[256,512]{1,0:T(8,128)(2,1)S(1)}, u32[]{:S(2)}, u32[]{:S(2)}) collective-permute-start(bf16[256,512]{1,0:T(8,128)(2,1)S(1)} %get-tuple-element.36), channel_id=1, source_target_pairs={{0,1},{1,0},{2,3},{3,2},{4,5},{5,4},{6,7},{7,6},{8,9},{9,8},{10,11... | collective-permute-start | bytes 786440 | tf_op jit(solution)/shard_map/ppermute | solution.py:37
  13.3 13.4 %collective-permute-start.4 = (bf16[256,512]{1,0:T(8,128)(2,1)S(1)}, bf16[256,512]{1,0:T(8,128)(2,1)S(1)}, u32[]{:S(2)}, u32[]{:S(2)}) collective-permute-start(bf16[256,512]{1,0:T(8,128)(2,1)S(1)} %get-tuple-element.37), channel_id=1, source_target_pairs={{0,2},{1,3},{2,0},{3,1},{4,6},{5,7},{6,4},{7,5},{8,10},{9,11},{10,... | collective-permute-start | bytes 786440 | tf_op jit(solution)/shard_map/ppermute | solution.py:37
  14.8 11.9 %collective-permute-start.5 = (bf16[256,512]{1,0:T(8,128)(2,1)S(1)}, bf16[256,512]{1,0:T(8,128)(2,1)S(1)}, u32[]{:S(2)}, u32[]{:S(2)}) collective-permute-start(bf16[256,512]{1,0:T(8,128)(2,1)S(1)} %get-tuple-element.38), channel_id=1, source_target_pairs={{0,3},{1,2},{2,1},{3,0},{4,7},{5,6},{6,5},{7,4},{8,11},{9,10},{10,... | collective-permute-start | bytes 786440 | tf_op jit(solution)/shard_map/ppermute | solution.py:37
  15.5 20.1 %copy-start.2 = (s32[128]{0:T(128)S(1)}, s32[128]{0:T(128)}, u32[]{:S(2)}) copy-start(s32[128]{0:T(128)} %param.17) | copy-start | bytes 1540
  15.6 13.8 %collective-permute-start.2 = (s16[256,512]{1,0:T(8,128)(2,1)S(1)}, s16[256,512]{1,0:T(8,128)(2,1)S(1)}, u32[]{:S(2)}, u32[]{:S(2)}) collective-permute-start(s16[256,512]{1,0:T(8,128)(2,1)S(1)} %round-nearest-even_convert_fusion), channel_id=1, source_target_pairs={{0,16},{4,20},{8,24},{12,28},{16,0},{20,4},{24,8},{28,12},{1,17},{... | collective-permute-start | bytes 786440 | tf_op jit(solution)/shard_map/ppermute | solution.py:26
  26.9 2.6 %collective-permute-start.6 = (bf16[256,512]{1,0:T(8,128)(2,1)S(1)}, bf16[256,512]{1,0:T(8,128)(2,1)S(1)}, u32[]{:S(2)}, u32[]{:S(2)}) collective-permute-start(bf16[256,512]{1,0:T(8,128)(2,1)S(1)} %get-tuple-element.55.refs_0_), channel_id=1, source_target_pairs={{0,4},{4,0},{8,12},{12,8},{16,20},{20,16},{24,28},{28,24},{1,5},{5... | collective-permute-start | bytes 786440 | tf_op jit(solution)/shard_map/ppermute | solution.py:20
  27.0 2.6 %collective-permute-start.7 = (bf16[256,512]{1,0:T(8,128)(2,1)S(1)}, bf16[256,512]{1,0:T(8,128)(2,1)S(1)}, u32[]{:S(2)}, u32[]{:S(2)}) collective-permute-start(bf16[256,512]{1,0:T(8,128)(2,1)S(1)} %get-tuple-element.54.refs_1_), channel_id=1, source_target_pairs={{0,4},{4,0},{8,12},{12,8},{16,20},{20,16},{24,28},{28,24},{1,5},{5... | collective-permute-start | bytes 786440 | tf_op jit(solution)/shard_map/ppermute | solution.py:20
  27.5 19.8 %copy-start.1 = (f32[128]{0:T(128)S(1)}, f32[128]{0:T(128)}, u32[]{:S(2)}) copy-start(f32[128]{0:T(128)} %param.16) | copy-start | bytes 1540
  32.1 7.4 %collective-permute-start.10 = (bf16[512,128]{1,0:T(8,128)(2,1)S(1)}, bf16[512,128]{1,0:T(8,128)(2,1)S(1)}, u32[]{:S(2)}, u32[]{:S(2)}) collective-permute-start(bf16[512,128]{1,0:T(8,128)(2,1)S(1)} %get-tuple-element.43), channel_id=1, source_target_pairs={{0,3},{1,2},{2,1},{3,0},{4,7},{5,6},{6,5},{7,4},{8,11},{9,10},{10,... | collective-permute-start | bytes 393224 | tf_op jit(solution)/shard_map/ppermute | solution.py:37
  34.6 7.8 %collective-permute-start.8 = (bf16[512,128]{1,0:T(8,128)(2,1)S(1)}, bf16[512,128]{1,0:T(8,128)(2,1)S(1)}, u32[]{:S(2)}, u32[]{:S(2)}) collective-permute-start(bf16[512,128]{1,0:T(8,128)(2,1)S(1)} %get-tuple-element.41), channel_id=1, source_target_pairs={{0,1},{1,0},{2,3},{3,2},{4,5},{5,4},{6,7},{7,6},{8,9},{9,8},{10,11... | collective-permute-start | bytes 393224 | tf_op jit(solution)/shard_map/ppermute | solution.py:37
  35.2 7.2 %collective-permute-start.9 = (bf16[512,128]{1,0:T(8,128)(2,1)S(1)}, bf16[512,128]{1,0:T(8,128)(2,1)S(1)}, u32[]{:S(2)}, u32[]{:S(2)}) collective-permute-start(bf16[512,128]{1,0:T(8,128)(2,1)S(1)} %get-tuple-element.42), channel_id=1, source_target_pairs={{0,2},{1,3},{2,0},{3,1},{4,6},{5,7},{6,4},{7,5},{8,10},{9,11},{10,... | collective-permute-start | bytes 393224 | tf_op jit(solution)/shard_map/ppermute | solution.py:37
  35.7 9.3 %collective-permute-start.11 = (bf16[512,128]{1,0:T(8,128)(2,1)S(1)}, bf16[512,128]{1,0:T(8,128)(2,1)S(1)}, u32[]{:S(2)}, u32[]{:S(2)}) collective-permute-start(bf16[512,128]{1,0:T(8,128)(2,1)S(1)} %get-tuple-element.45), channel_id=1, source_target_pairs={{0,1},{1,0},{2,3},{3,2},{4,5},{5,4},{6,7},{7,6},{8,9},{9,8},{10,11... | collective-permute-start | bytes 393224 | tf_op jit(solution)/shard_map/ppermute | solution.py:37
  37.2 9.3 %collective-permute-start.12 = (bf16[512,128]{1,0:T(8,128)(2,1)S(1)}, bf16[512,128]{1,0:T(8,128)(2,1)S(1)}, u32[]{:S(2)}, u32[]{:S(2)}) collective-permute-start(bf16[512,128]{1,0:T(8,128)(2,1)S(1)} %get-tuple-element.46), channel_id=1, source_target_pairs={{0,2},{1,3},{2,0},{3,1},{4,6},{5,7},{6,4},{7,5},{8,10},{9,11},{10,... | collective-permute-start | bytes 393224 | tf_op jit(solution)/shard_map/ppermute | solution.py:37
  39.5 6.9 %collective-permute-start.13 = (bf16[512,128]{1,0:T(8,128)(2,1)S(1)}, bf16[512,128]{1,0:T(8,128)(2,1)S(1)}, u32[]{:S(2)}, u32[]{:S(2)}) collective-permute-start(bf16[512,128]{1,0:T(8,128)(2,1)S(1)} %get-tuple-element.47), channel_id=1, source_target_pairs={{0,3},{1,2},{2,1},{3,0},{4,7},{5,6},{6,5},{7,4},{8,11},{9,10},{10,... | collective-permute-start | bytes 393224 | tf_op jit(solution)/shard_map/ppermute | solution.py:37
  42.5 4.8 %collective-permute-start.15 = (bf16[2,256,128]{2,1,0:T(8,128)(2,1)S(1)}, bf16[2,256,128]{2,1,0:T(8,128)(2,1)S(1)}, u32[]{:S(2)}, u32[]{:S(2)}) collective-permute-start(bf16[2,256,128]{2,1,0:T(8,128)(2,1)S(1)} %get-tuple-element.50), channel_id=1, source_target_pairs={{0,8},{4,12},{8,16},{12,20},{16,24},{20,28},{1,9},{5,13},{9,17},{1... | collective-permute-start | bytes 393224 | tf_op jit(solution)/shard_map/ppermute | solution.py:31
  46.5 1.6 %collective-permute-start.14 = (f32[2,256,128]{2,1,0:T(8,128)S(1)}, f32[2,256,128]{2,1,0:T(8,128)S(1)}, u32[]{:S(2)}, u32[]{:S(2)}) collective-permute-start(f32[2,256,128]{2,1,0:T(8,128)S(1)} %get-tuple-element.52), channel_id=1, source_target_pairs={{0,4},{4,0},{8,12},{12,8},{16,20},{20,16},{24,28},{28,24},{1,5},{5... | collective-permute-start | bytes 786440 | tf_op jit(solution)/shard_map/ppermute | solution.py:20
  47.4 1.6 %collective-permute-start.16 = (f32[2,128]{1,0:T(2,128)S(1)}, f32[2,128]{1,0:T(2,128)S(1)}, u32[]{:S(2)}, u32[]{:S(2)}) collective-permute-start(f32[2,128]{1,0:T(2,128)S(1)} %constant_dynamic-slice_fusion.1), channel_id=1, source_target_pairs={{0,4},{4,0},{8,12},{12,8},{16,20},{20,16},{24,28},{28,24},{1,5},{5... | collective-permute-start | bytes 3080 | tf_op jit(solution)/shard_map/ppermute | solution.py:20
